TPU v7x, 32 devices: a whole 2x2x4 slice. The times are simulated.
32 devices in a mesh: gx: 4 (over y, x), gy: 8 (over z, core).
Axes of the slice: x: 2, y: 2, z: 4, core: 2. Of those that a mesh axis runs over, the one named last changes fastest.
Arguments:
- positions: float32 [4, 8, 3, 256], P('gx', 'gy'), may hold values from 0 to 1
- species: int32 [4, 8, 256], P('gx', 'gy'), may hold values from 0 to 88
- dest_key: int32 [4, 8, 256], P('gx', 'gy'), may hold values from 0 to 4, as said below
- send_list: int32 [4, 8, 4, 32], P('gx', 'gy'), may hold values from 0 to 255, as said below
- send_count: int32 [4, 8, 4], P('gx', 'gy'), may hold values from 8 to 32, as said below
- border: int32 [4, 8, 128], P('gx', 'gy'), may hold values from 0 to 255, as said below
- neighbours: int32 [4, 8, 384, 12], P('gx', 'gy'), may hold values from -1 to 1535, as said below
- embedding: float32 [89, 128], replicated, may hold values from -4 to 4
- radial_in: float32 [2, 8, 64], replicated, may hold values from -2 to 2
- radial_mid: float32 [2, 64, 64], replicated, may hold values from -0.75 to 0.75
- radial_out_one: float32 [64, 384], replicated, may hold values from -4 to 4
- radial_out_two: float32 [64, 896], replicated, may hold values from -4 to 4
- mix: float32 [2, 3, 128, 128], replicated, may hold values from -0.5 to 0.5
- mix_out_one: float32 [3, 128, 128], replicated, may hold values from -0.5 to 0.5
- mix_out_two: float32 [128, 128], replicated, may hold values from -0.5 to 0.5
- product_one: float32 [5, 128], replicated, may hold values from -4 to 4
- product_two: float32 [3, 128], replicated, may hold values from -4 to 4
- read_lin: float32 [128], replicated, may hold values from -0.5 to 0.5
- read_hidden: float32 [128, 16], replicated, may hold values from -0.5 to 0.5
- read_out: float32 [16], replicated, may hold values from -1.5 to 1.5
Outputs:
- atom_energy: float32 [4, 8, 384], P('gx', 'gy')
- forces: float32 [4, 8, 3, 384], P('gx', 'gy')
Inputs may be any that keep to these rules, and one draw needn't show every extreme that they name: `dest_key`: 0 keeps the atom; 1, 2, 3, 4 send it to the next device along gx, the previous along gx, the next along gy, the previous along gy (periodic); each device has at most 32 atoms of each nonzero key. `send_list`: row d holds in increasing order the slots whose dest_key is d + 1, then other slots as padding. `send_count`: the number of slots whose dest_key is d + 1; some device has exactly 32 in some direction in every draw. `border`: distinct slots whose dest_key is 0. `neighbours`: -1 marks an empty slot; a value below 384 is a local row after migration; 384 + (3 * a + b) * 128 + k is the k-th border row of the device at offset (a - 1, b - 1) along (gx, gy), with (a, b) never (1, 1); devices differ in how many slots are empty.
All inputs are finite; a program needn't handle non-finite values.
Results may differ from a plain program's by a relative error of at most 0.003.
Values may be sent and summed in bfloat16 or wider, within the bound.
A program may use at most 192 MiB of HBM per device.

v0:
```python
import math

import jax
import jax.numpy as jnp
from jax import lax
from jax.sharding import PartitionSpec as P

cutoff_radius = 5.0
cell_side = 1.0
highest = lax.Precision.HIGHEST


def from_behind(block, axis, distance):
    devices = range(lax.axis_size(axis))
    route = [((i - distance) % len(devices), i) for i in devices]
    return lax.ppermute(block, axis, route)


def as_sent(array):

    def short(part):
        return part.astype(jnp.bfloat16) if part.dtype == jnp.float32 else part

    return jax.tree.map(short, array)


def extended(array, sides, width):
    for axis, dim in sides:
        count, length = (lax.axis_size(axis), array.shape[dim])
        up = [(i, (i + 1) % count) for i in range(count)]
        down = [(j, i) for i, j in up]
        last = lax.slice_in_dim(array, length - width, length, axis=dim)
        first = lax.slice_in_dim(array, 0, width, axis=dim)
        before = lax.ppermute(last, axis, up)
        after = lax.ppermute(first, axis, down)
        array = jnp.concatenate([before, array, after], axis=dim)
    return array


def geometry(offsets, basis_count):
    squared = jnp.sum(offsets * offsets, axis=0) + 1.0
    distance = jnp.sqrt(squared)
    pointer = offsets / distance[None, :]
    scaled = distance / cutoff_radius
    sixth = scaled * scaled * scaled * scaled * scaled * scaled
    envelope = 1.0 - 28.0 * sixth + 48.0 * sixth * scaled - 21.0 * sixth * scaled * scaled
    orders = jnp.arange(1, basis_count + 1).astype(jnp.float32)[:, None]
    basis = (
        math.sqrt(2.0 / cutoff_radius)
        * jnp.sin(orders * (math.pi / cutoff_radius) * distance[None, :])
        * (envelope / distance)[None, :]
    )
    along_x = pointer[0]
    along_y = pointer[1]
    along_z = pointer[2]
    root_five = math.sqrt(5.0)
    root_fifteen = math.sqrt(15.0)
    vector_part = math.sqrt(3.0) * pointer
    tensor_part = jnp.stack(
        [
            root_fifteen * along_x * along_y,
            root_fifteen * along_y * along_z,
            0.5 * root_five * (2.0 * along_z * along_z - along_x * along_x - along_y * along_y),
            root_fifteen * along_x * along_z,
            0.5 * root_fifteen * (along_x * along_x - along_y * along_y),
        ]
    )
    return (basis, vector_part, tensor_part)


def radial(basis, w_in, w_mid, w_out):
    hidden = jax.nn.silu(jnp.dot(w_in.T, basis, precision=highest))
    hidden = jax.nn.silu(jnp.dot(w_mid.T, hidden, precision=highest))
    return jnp.dot(w_out.T, hidden, precision=highest)


def contract(matrix, values):
    return jnp.einsum("cd,...cn->...dn", matrix, values, precision=highest)


def interaction(
    first, pos_all, feats_all, occ_all, neighbour_block, pos_block, occ_block, residual, weights
):
    w_in, w_mid, w_out, mixing, mixing_out, coefs = weights
    atoms, slots = neighbour_block.shape
    channels = mixing.shape[-1]
    flat_index = jnp.maximum(neighbour_block, 0).reshape(-1)
    edge_mask = (
        (neighbour_block >= 0).astype(jnp.float32).reshape(-1)
        * occ_all[flat_index]
        * jnp.repeat(occ_block, slots)
    )
    offsets = pos_all[:, flat_index] - jnp.repeat(pos_block, slots, axis=1)
    basis, vector_part, tensor_part = geometry(offsets, w_in.shape[0])
    source = feats_all[:, flat_index] * edge_mask[None, :]
    paths = 3 if first else 7
    edge_weights = radial(basis, w_in, w_mid, w_out).reshape(paths, channels, -1)
    scalar = source[:channels]
    if first:
        msg_scalar = edge_weights[0] * scalar
        msg_vector = edge_weights[1][None] * scalar[None] * vector_part[:, None]
        msg_tensor = edge_weights[2][None] * scalar[None] * tensor_part[:, None]
    else:
        vectors = source[channels : 4 * channels].reshape(3, channels, -1)
        tensors = source[4 * channels :].reshape(5, channels, -1)
        msg_scalar = (
            edge_weights[0] * scalar
            + edge_weights[1] * jnp.sum(vector_part[:, None] * vectors, axis=0)
            + edge_weights[2] * jnp.sum(tensor_part[:, None] * tensors, axis=0)
        )
        msg_vector = (
            edge_weights[3][None] * scalar[None] * vector_part[:, None]
            + edge_weights[4][None] * vectors
        )
        msg_tensor = (
            edge_weights[5][None] * scalar[None] * tensor_part[:, None]
            + edge_weights[6][None] * tensors
        )

    def pooling(message):
        return jnp.sum(message.reshape(message.shape[:-1] + (atoms, slots)), axis=-1) / slots

    mixed_scalar = contract(mixing[0], pooling(msg_scalar))
    mixed_vector = contract(mixing[1], pooling(msg_vector))
    mixed_tensor = contract(mixing[2], pooling(msg_tensor))
    product_scalar = (
        mixed_scalar
        + coefs[0][:, None] * mixed_scalar * mixed_scalar
        + coefs[1][:, None] * jnp.sum(mixed_vector * mixed_vector, axis=0)
        + coefs[2][:, None] * jnp.sum(mixed_tensor * mixed_tensor, axis=0)
    )
    if first:
        product_vector = mixed_vector * (1.0 + coefs[3][:, None] * mixed_scalar)[None]
        product_tensor = mixed_tensor * (1.0 + coefs[4][:, None] * mixed_scalar)[None]
        new_scalar = contract(mixing_out[0], product_scalar) + residual
        new_vector = contract(mixing_out[1], product_vector).reshape(3 * channels, atoms)
        new_tensor = contract(mixing_out[2], product_tensor).reshape(5 * channels, atoms)
        return jnp.concatenate([new_scalar, new_vector, new_tensor], axis=0)
    return contract(mixing_out, product_scalar) + residual[:channels]


def run_layer(first, pos_all, feats_all, occ_all, occupied, neighbour_rows, weights):
    total_rows = neighbour_rows.shape[0]
    block_rows = math.gcd(total_rows, 128)
    block_count = total_rows // block_rows

    def one_block(block_index):
        start = block_index * block_rows
        neighbour_block = lax.dynamic_slice_in_dim(neighbour_rows, start, block_rows, 0)
        pos_block = lax.dynamic_slice_in_dim(pos_all, start, block_rows, 1)
        occ_block = lax.dynamic_slice_in_dim(occupied, start, block_rows, 0)
        residual = lax.dynamic_slice_in_dim(feats_all, start, block_rows, 1)
        return interaction(
            first,
            pos_all,
            feats_all,
            occ_all,
            neighbour_block,
            pos_block,
            occ_block,
            residual,
            weights,
        )

    outputs = lax.map(jax.checkpoint(one_block), jnp.arange(block_count, dtype=jnp.int32))
    return jnp.moveaxis(outputs, 0, 1).reshape(outputs.shape[1], total_rows)


def shift_table():
    grid_shift = cell_side * (jnp.arange(3).astype(jnp.float32) - 1.0)
    first_axis = jnp.broadcast_to(grid_shift[:, None], (3, 3))
    second_axis = jnp.broadcast_to(grid_shift[None, :], (3, 3))
    return jnp.stack([first_axis, second_axis, jnp.zeros((3, 3), jnp.float32)], axis=-1)


def give_back_features(pieces):
    column = pieces[:, 1]
    for alongside, stride in ((0, -1), (2, 1)):
        column = column + from_behind(
            pieces[:, alongside].astype(jnp.bfloat16), "gy", stride
        ).astype(jnp.float32)
    total = column[1]
    for across, stride in ((0, -1), (2, 1)):
        total = total + from_behind(as_sent(column[across]), "gx", stride)
    return total


def give_back_coords(pieces):
    column = pieces[:, 1]
    for alongside, stride in ((0, -1), (2, 1)):
        column = column + from_behind(pieces[:, alongside], "gy", stride)
    total = column[1]
    for across, stride in ((0, -1), (2, 1)):
        total = total + from_behind(column[across], "gx", stride)
    return total


def on_device(
    positions,
    species,
    dest_key,
    send_list,
    send_count,
    border,
    neighbours,
    embedding,
    radial_in,
    radial_mid,
    radial_out_one,
    radial_out_two,
    mix,
    mix_out_one,
    mix_out_two,
    product_one,
    product_two,
    read_lin,
    read_hidden,
    read_out,
):
    own_coords = positions[0, 0]
    own_kinds = species[0, 0]
    staying = (dest_key[0, 0] == 0).astype(jnp.float32)
    listed = send_list[0, 0]
    counted = send_count[0, 0]
    edge_lists = neighbours[0, 0]
    border_rows = border[0, 0]
    slot_count = listed.shape[1]
    border_count = border_rows.shape[0]
    channels = embedding.shape[1]
    slot_used = jnp.arange(slot_count)[None, :] < counted[:, None]
    leaving_kinds = jnp.where(slot_used, own_kinds[listed], -1).astype(jnp.float32)
    leaving = jnp.concatenate(
        [jnp.moveaxis(jnp.take(own_coords, listed, axis=1), 1, 0), leaving_kinds[:, None, :]],
        axis=1,
    )
    border_packet = jnp.concatenate(
        [own_coords[:, border_rows], own_kinds[border_rows].astype(jnp.float32)[None, :]], axis=0
    )
    arrived = [leaving[0], leaving[1], leaving[2], leaving[3]]
    for target, stride in ((0, 1), (1, -1)):
        arrived[target] = from_behind(leaving[target], "gx", stride)
    for target, stride in ((2, 1), (3, -1)):
        arrived[target] = from_behind(leaving[target], "gy", stride)
    beside_all = extended(border_packet[None, None], (("gx", 0), ("gy", 1)), 1)
    arrival_moves = ((0, -1.0), (0, 1.0), (1, -1.0), (1, 1.0))
    adjusted = []
    for target in range(4):
        coordinate, amount = arrival_moves[target]
        adjusted.append(arrived[target].at[coordinate].add(amount * cell_side))
    incoming = jnp.concatenate(adjusted, axis=1)
    local_coords = jnp.concatenate([own_coords, incoming[:3]], axis=1)
    local_kinds = jnp.concatenate([own_kinds, incoming[3].astype(jnp.int32)])
    occupied = jnp.concatenate([staying, (incoming[3] >= 0).astype(jnp.float32)])
    ghost_block = beside_all[:, :, :3, :] + shift_table()[:, :, :, None]
    ghost_coords = jnp.moveaxis(ghost_block, 2, 0).reshape(3, 9 * border_count)
    ghost_kinds = beside_all[:, :, 3, :].reshape(9 * border_count).astype(jnp.int32)
    coords_all = jnp.concatenate([local_coords, ghost_coords], axis=1)
    kinds_all = jnp.maximum(jnp.concatenate([local_kinds, ghost_kinds]), 0)
    occupied_all = jnp.concatenate([occupied, jnp.ones((9 * border_count,), jnp.float32)])
    one_hot = (kinds_all[None, :] == jnp.arange(embedding.shape[0])[:, None]).astype(jnp.float32)
    initial = jnp.dot(embedding.T, one_hot, precision=highest)
    first_weights = (radial_in[0], radial_mid[0], radial_out_one, mix[0], mix_out_one, product_one)
    second_weights = (radial_in[1], radial_mid[1], radial_out_two, mix[1], mix_out_two, product_two)

    def first_layer(coords_in):
        return run_layer(
            True, coords_in, initial, occupied_all, occupied, edge_lists, first_weights
        )

    hidden_one, pull_one = jax.vjp(first_layer, coords_all)
    rounded = hidden_one.astype(jnp.bfloat16)
    border_feats = rounded[:, border_rows]
    partial_feats = extended(border_feats[None, None], (("gx", 0),), 1)
    around_feats = extended(partial_feats, (("gy", 1),), 1)
    ghost_feats = jnp.moveaxis(around_feats, 2, 0).reshape(rounded.shape[0], 9 * border_count)
    table = jnp.concatenate([rounded, ghost_feats], axis=1).astype(jnp.float32)

    def second_layer(coords_in, table_in):
        scalars = run_layer(
            False, coords_in, table_in, occupied_all, occupied, edge_lists, second_weights
        )
        readout = jax.nn.silu(jnp.dot(read_hidden.T, scalars, precision=highest))
        return occupied * jnp.dot(read_out, readout, precision=highest)

    energy_two, pull_two = jax.vjp(second_layer, coords_all, table)
    energy_one = occupied * jnp.dot(
        read_lin, rounded[:channels].astype(jnp.float32), precision=highest
    )
    atom_energy = energy_one + energy_two
    coords_grad_two, table_grad = pull_two(jnp.ones_like(energy_two))
    local_rows = occupied.shape[0]
    feats_grad = table_grad[:, :local_rows].at[:channels].add(read_lin[:, None] * occupied[None, :])
    ghost_grad = jnp.moveaxis(
        table_grad[:, local_rows:].reshape(table_grad.shape[0], 3, 3, border_count), 0, 2
    )
    feats_grad = feats_grad.at[:, border_rows].add(give_back_features(ghost_grad))
    (coords_grad_one,) = pull_one(feats_grad)
    coords_grad = coords_grad_one + coords_grad_two
    ghost_coords_grad = jnp.moveaxis(
        coords_grad[:, local_rows:].reshape(3, 3, 3, border_count), 0, 2
    )
    forces = (
        -coords_grad[:, :local_rows].at[:, border_rows].add(give_back_coords(ghost_coords_grad))
    )
    return (atom_energy[None, None], forces[None, None])


def solution(mesh):
    in_specs = (
        P("gx", "gy", None, None),
        P("gx", "gy", None),
        P("gx", "gy", None),
        P("gx", "gy", None, None),
        P("gx", "gy", None),
        P("gx", "gy", None),
        P("gx", "gy", None, None),
        P(),
        P(),
        P(),
        P(),
        P(),
        P(),
        P(),
        P(),
        P(),
        P(),
        P(),
        P(),
        P(),
    )
    out_specs = (P("gx", "gy", None), P("gx", "gy", None, None))
    return jax.shard_map(
        on_device, mesh=mesh, in_specs=in_specs, out_specs=out_specs, check_vma=False
    )
```

profile of v0, /device:TPU:0, one launch (start us, length us, event | category | flops | bytes accessed | tf_op | source)
XLA Modules:
  0.0 1764.6 jit_solution(12887357136733103098)
XLA Ops:
  46.5 132.6 %while.59 = (s32[]{:T(128)}, bf16[3,1152,128]{1,2,0:T(8,128)(2,1)}, s32[3]{0:T(128)S(1)}, s32[384,12]{1,0:T(8,128)S(1)}, f32[3,1536]{0,1:T(8,128)}, /*index=5*/f...) while((s32[]{:T(128)}, bf16[3,1152,128]{1,2,0:T(8,128)(2,1)}, ...), condition=%wide.region_7.8_spmd.clone, body=%wide.region_0.7_spmd.clone.sunk | while | flops 997599232 | bytes 40897072 | solution.py:165
  199.3 15.2 collective-permute-done.11
  221.1 346.2 %while.60 = (s32[]{:T(128)}, f32[3,128,128]{1,2,0:T(8,128)}, s32[3]{0:T(128)S(1)}, s32[384,12]{1,0:T(8,128)S(1)}, f32[3,1536]{0,1:T(8,128)}, /*index=5*/f32[64,8...) while((s32[]{:T(128)}, f32[3,128,128]{1,2,0:T(8,128)}, ...), condition=%wide.region_17.18_spmd.clone, body=%wide.region_8.17_spmd.clone.sunk | while | flops 1407217152 | bytes 156353264 | solution.py:165
  223.0 11.4 gather_fusion.3
  338.2 11.4 gather_fusion.3
  453.5 11.4 gather_fusion.3
  569.8 824.2 %while.61 = (s32[]{:T(128)}, f32[3,1536]{0,1:T(8,128)}, f32[1152,1536]{0,1:T(8,128)}, s32[3]{0:T(128)S(1)}, f32[3,128,128]{1,2,0:T(8,128)S(1)}, /*index=5*/s32[3...) while((s32[]{:T(128)}, f32[3,1536]{0,1:T(8,128)}, ...), condition=%wide.region_39.40_spmd.clone, body=%wide.region_18.39_spmd.clone.sunk | while | flops 2815792640 | bytes 465380640 | solution.py:165
  578.3 11.5 gather_fusion.7
  670.7 9.5 multiply_reduce_fusion.68
  726.0 9.3 multiply_reduce_fusion.69
  772.0 9.1 scatter_custom_fusion.21
  814.6 18.8 %scatter_custom_fusion.22 = f32[1152,1536]{0,1:T(8,128)} fusion(s32[1536]{0:T(1024)} %copy-done.105, f32[1536,1152]{1,0:T(8,128)} %copy.863, f32[]{:T(128)} %constant.686.clone.1..sunk.1), kind=kCustom, calls=%fused_computation.223.clone.1 | custom fusion | flops 1769472 | bytes 7078400 | tf_op jit(solution)/shard_map/transpose(jvp())/while/body/eval_jaxpr/checkpoint/scatter-add | solution.py:95
  850.6 11.5 gather_fusion.7
  943.1 9.5 multiply_reduce_fusion.68
  1044.2 9.1 scatter_custom_fusion.21
  1086.8 18.8 %scatter_custom_fusion.22 = f32[1152,1536]{0,1:T(8,128)} fusion(s32[1536]{0:T(1024)} %copy-done.105, f32[1536,1152]{1,0:T(8,128)} %copy.863, f32[]{:T(128)} %constant.686.clone.1..sunk.1), kind=kCustom, calls=%fused_computation.223.clone.1 | custom fusion | flops 1769472 | bytes 7078400 | tf_op jit(solution)/shard_map/transpose(jvp())/while/body/eval_jaxpr/checkpoint/scatter-add | solution.py:95
  1125.0 11.5 gather_fusion.7
  1217.2 9.5 multiply_reduce_fusion.68
  1272.6 9.1 multiply_reduce_fusion.69
  1318.4 9.1 scatter_custom_fusion.21
  1361.2 18.8 %scatter_custom_fusion.22 = f32[1152,1536]{0,1:T(8,128)} fusion(s32[1536]{0:T(1024)} %copy-done.105, f32[1536,1152]{1,0:T(8,128)} %copy.863, f32[]{:T(128)} %constant.686.clone.1..sunk.1), kind=kCustom, calls=%fused_computation.223.clone.1 | custom fusion | flops 1769472 | bytes 7078400 | tf_op jit(solution)/shard_map/transpose(jvp())/while/body/eval_jaxpr/checkpoint/scatter-add | solution.py:95
  1406.8 15.6 collective-permute-done.13
  1442.8 304.8 %while.62 = (s32[]{:T(128)}, f32[3,1536]{0,1:T(8,128)}, s32[3]{0:T(128)}, f32[3,1152,128]{2,1,0:T(8,128)}, s32[384,12]{1,0:T(8,128)S(1)}, /*index=5*/f32[3,1536]...) while((s32[]{:T(128)}, f32[3,1536]{0,1:T(8,128)}, ...), condition=%wide.region_57.58_spmd.clone, body=%wide.region_41.57_spmd.clone.sunk | while | flops 1771674112 | bytes 99862632 | solution.py:165
  1543.3 9.1 scatter_custom_fusion.24
  (2040 shorter events, 1487.4 us)
Async XLA Ops:
  5.7 30.3 %collective-permute-start.5 = (f32[1,1,4,128]{3,2,1,0:T(4,128)S(1)}, f32[1,1,4,128]{3,2,1,0:T(4,128)S(1)}, u32[]{:S(2)}, u32[]{:S(2)}) collective-permute-start(f32[1,1,4,128]{3,2,1,0:T(4,128)S(1)} %maximum_bitcast_fusion.1), channel_id=1, source_target_pairs={{8,0},{16,8},{24,16},{0,24},{9,1},{17,9},{25,17},{1,25},{10,2},{18... | collective-permute-start | bytes 6152 | tf_op jit(solution)/shard_map/ppermute | solution.py:35
  9.7 26.4 %collective-permute-start.4 = (f32[1,1,4,128]{3,2,1,0:T(4,128)S(1)}, f32[1,1,4,128]{3,2,1,0:T(4,128)S(1)}, u32[]{:S(2)}, u32[]{:S(2)}) collective-permute-start(f32[1,1,4,128]{3,2,1,0:T(4,128)S(1)} %maximum_bitcast_fusion.1), channel_id=1, source_target_pairs={{0,8},{8,16},{16,24},{24,0},{1,9},{9,17},{17,25},{25,1},{2,10},{10... | collective-permute-start | bytes 6152 | tf_op jit(solution)/shard_map/ppermute | solution.py:34
  14.3 17.1 collective-permute-start.3
  17.1 14.3 collective-permute-start.2
  17.1 14.3 collective-permute-start.1
  31.4 4.5 collective-permute-start
  36.1 3.5 collective-permute-start.7
  38.2 4.9 collective-permute-start.6
  181.7 8.4 collective-permute-start.9
  181.8 11.5 collective-permute-start.8
  194.3 20.2 %collective-permute-start.11 = (bf16[3,1,1152,128]{2,3,1,0:T(8,128)(2,1)}, bf16[3,1,1152,128]{2,3,1,0:T(8,128)(2,1)}, u32[]{:S(2)}, u32[]{:S(2)}) collective-permute-start(bf16[3,1,1152,128]{2,3,1,0:T(8,128)(2,1)} %pad_maximum_fusion.1), channel_id=1, source_target_pairs={{1,0},{2,1},{3,2},{4,3},{5,4},{6,5},{7,6},{0,7},{9,8},{10,9},{11,1... | collective-permute-start | bytes 2654216 | tf_op jit(solution)/shard_map/ppermute | solution.py:35
  196.3 19.9 %collective-permute-start.10 = (bf16[3,1,1152,128]{2,3,1,0:T(8,128)(2,1)}, bf16[3,1,1152,128]{2,3,1,0:T(8,128)(2,1)}, u32[]{:S(2)}, u32[]{:S(2)}) collective-permute-start(bf16[3,1,1152,128]{2,3,1,0:T(8,128)(2,1)} %pad_maximum_fusion.1), channel_id=1, source_target_pairs={{0,1},{1,2},{2,3},{3,4},{4,5},{5,6},{6,7},{7,0},{8,9},{9,10},{10,1... | collective-permute-start | bytes 2654216 | tf_op jit(solution)/shard_map/ppermute | solution.py:34
  221.1 346.2 %copy-start.124 = (f32[128,16]{0,1:T(8,128)S(1)}, f32[128,16]{0,1:T(8,128)}, u32[]{:S(2)}) copy-start(f32[128,16]{0,1:T(8,128)} %param.56) | copy-start | bytes 24580
  578.3 57.8 %copy-start.76 = (f32[1536]{0:T(1024)}, f32[1536]{0:T(1024)S(1)}, u32[]{:S(2)}) copy-start(f32[1536]{0:T(1024)S(1)} %get-tuple-element.2376) | copy-start | bytes 18436 | tf_op jit(solution)/shard_map/transpose(jvp())/while
  850.6 57.8 %copy-start.76 = (f32[1536]{0:T(1024)}, f32[1536]{0:T(1024)S(1)}, u32[]{:S(2)}) copy-start(f32[1536]{0:T(1024)S(1)} %get-tuple-element.2376) | copy-start | bytes 18436 | tf_op jit(solution)/shard_map/transpose(jvp())/while
  1125.0 57.8 %copy-start.76 = (f32[1536]{0:T(1024)}, f32[1536]{0:T(1024)S(1)}, u32[]{:S(2)}) copy-start(f32[1536]{0:T(1024)S(1)} %get-tuple-element.2376) | copy-start | bytes 18436 | tf_op jit(solution)/shard_map/transpose(jvp())/while
  1399.5 23.0 %collective-permute-start.13 = (bf16[3,1152,128]{1,2,0:T(8,128)(2,1)S(1)}, bf16[3,1152,128]{1,2,0:T(8,128)(2,1)S(1)}, u32[]{:S(2)}, u32[]{:S(2)}) collective-permute-start(bf16[3,1152,128]{1,2,0:T(8,128)(2,1)S(1)} %get-tuple-element.1719), channel_id=1, source_target_pairs={{7,0},{0,1},{1,2},{2,3},{3,4},{4,5},{5,6},{6,7},{15,8},{8,9},{9,10... | collective-permute-start | bytes 2654216 | tf_op jit(solution)/shard_map/ppermute | solution.py:16
  1399.5 22.9 %collective-permute-start.12 = (bf16[3,1152,128]{1,2,0:T(8,128)(2,1)S(1)}, bf16[3,1152,128]{1,2,0:T(8,128)(2,1)}, u32[]{:S(2)}, u32[]{:S(2)}) collective-permute-start(bf16[3,1152,128]{1,2,0:T(8,128)(2,1)S(1)} %get-tuple-element.1718), channel_id=1, source_target_pairs={{1,0},{2,1},{3,2},{4,3},{5,4},{6,5},{7,6},{0,7},{9,8},{10,9},{11,1... | collective-permute-start | bytes 2654216 | tf_op jit(solution)/shard_map/ppermute | solution.py:16
  1425.3 8.2 collective-permute-start.15
  1425.7 10.9 collective-permute-start.14
  1749.3 7.7 collective-permute-start.17
  1749.3 7.6 collective-permute-start.16
  1757.0 5.2 collective-permute-start.19
  1757.1 5.2 collective-permute-start.18
  (412 other events, 2756.3 us)
where the time goes:
time: 1790 us; the launch traced here: 1760 us
  local copies, waits for them, and re-layouts  894 us (50%)
  other arithmetic  530 us (30%)
  matrix products  213 us (12%)
  waiting for transfers between devices  60.2 us (3%)
  loops' own time  36.7 us (2%)
  starting transfers between devices  29.5 us (2%)
    gather x24, local copies, waits for them, and re-layouts, interaction(): source = feats_all[:, flat_index] * edge_mask[None, :]  125 us
    gather x18, local copies, waits for them, and re-layouts, interaction(): occ_all[flat_index]  101 us
    dot_general x78, matrix products, contract(): return jnp.einsum('cd,...cn->...dn', matrix, values, precision=highest)  98.3 us
    reduce_sum x36, other arithmetic, pooling(): jnp.sum(message.reshape(message.shape[:-1] + (atoms, slots)), axis=-1)  86.6 us
    dot_general x18, matrix products, radial(): return jnp.dot(w_out.T, hidden, precision=highest)  75 us
    gather x39, local copies, waits for them, and re-layouts, interaction(): offsets = pos_all[:, flat_index] - jnp.repeat(pos_block, slots, axis=1)  56.9 us
    scatter-add x3, other arithmetic, interaction(): source = feats_all[:, flat_index] * edge_mask[None, :]  56.5 us
    scatter-add x6, other arithmetic, interaction(): offsets = pos_all[:, flat_index] - jnp.repeat(pos_block, slots, axis=1)  54.4 us
  transfers between devices with their start and end apart: 20, of which 12 were waited for; matrix products, arithmetic and copies ran while one was open for 2% of the time, Pallas kernels for 0%

commit v1 on v0

v1 whole, which is shorter than its diff:
```python
import math

import jax
import jax.numpy as jnp
from jax import lax
from jax.experimental import pallas as pl
from jax.experimental.pallas import tpu as pltpu
from jax.sharding import PartitionSpec as P

f32 = jnp.float32
bf16 = jnp.bfloat16
highest = lax.Precision.HIGHEST
CUT = 5.0
L = 128
G = 256
CB = 16
VMEM_LIMIT = 56 * 1024 * 1024


def params():
    return pltpu.CompilerParams(vmem_limit_bytes=VMEM_LIMIT)


def dot(a, b):
    return jnp.dot(a, b, preferred_element_type=f32)


def dot_high(a, b):
    return jnp.dot(a, b, preferred_element_type=f32, precision=highest)


def hi_lo(x):
    hi = x.astype(bf16)
    return hi, (x - hi.astype(f32)).astype(bf16)


def dot_split(stack, x):
    hi, lo = hi_lo(x)
    return dot(stack, jnp.concatenate([hi, hi, lo], axis=0))


def silu(x):
    return x * jax.nn.sigmoid(x)


def silu_slope(x):
    sig = jax.nn.sigmoid(x)
    return sig * (1.0 + x * (1.0 - sig))


def geometry(ox, oy, oz):
    squared = ox * ox + oy * oy + oz * oz + 1.0
    distance = jnp.sqrt(squared)
    inverse = 1.0 / distance
    ux, uy, uz = ox * inverse, oy * inverse, oz * inverse
    t = distance / CUT
    sixth = t * t * t * t * t * t
    envelope = 1.0 - 28.0 * sixth + 48.0 * sixth * t - 21.0 * sixth * t * t
    orders = (lax.broadcasted_iota(jnp.int32, (8, ox.shape[1]), 0) + 1).astype(f32)
    wave = jnp.sin(orders * (math.pi / CUT) * jnp.broadcast_to(distance, orders.shape))
    scale = math.sqrt(2.0 / CUT) * envelope * inverse
    basis = wave * jnp.broadcast_to(scale, orders.shape)
    r3, r5, r15 = math.sqrt(3.0), math.sqrt(5.0), math.sqrt(15.0)
    harmonics = (
        r3 * ux,
        r3 * uy,
        r3 * uz,
        r15 * ux * uy,
        r15 * uy * uz,
        0.5 * r5 * (2.0 * uz * uz - ux * ux - uy * uy),
        r15 * ux * uz,
        0.5 * r15 * (ux * ux - uy * uy),
    )
    return basis, harmonics


def one_hot_columns(rows, index_row):
    place = lax.broadcasted_iota(jnp.int32, (rows, index_row.shape[1]), 0)
    return jnp.where(place == index_row, 1.0, 0.0).astype(bf16)


def one_hot_rows(index_column, base, columns):
    place = lax.broadcasted_iota(jnp.int32, (index_column.shape[0], columns), 1) + base
    return jnp.where(place == index_column, 1.0, 0.0).astype(bf16)


@jax.custom_vjp
def mixed(w, wt, x):
    return dot_split(wt, x)


def mixed_fwd(w, wt, x):
    return dot_split(wt, x), (w, wt)


def mixed_bwd(saved, g):
    w, wt = saved
    return None, None, dot_split(w, g)


mixed.defvjp(mixed_fwd, mixed_bwd)


def mix_orders(mats, mats_t, parts):
    scalar = mixed(mats[0], mats_t[0], parts[0])
    vector = mixed(mats[1], mats_t[1], jnp.concatenate(parts[1:4], axis=1))
    tensor = mixed(mats[2], mats_t[2], jnp.concatenate(parts[4:9], axis=1))
    return scalar, [vector[:, i * L : (i + 1) * L] for i in range(3)], [
        tensor[:, i * L : (i + 1) * L] for i in range(5)
    ]


def product_scalar(coefs, s, v, q):
    total = s + coefs[0] * s * s
    total = total + coefs[1] * (v[0] * v[0] + v[1] * v[1] + v[2] * v[2])
    return total + coefs[2] * (
        q[0] * q[0] + q[1] * q[1] + q[2] * q[2] + q[3] * q[3] + q[4] * q[4]
    )


def node_one(parts, mats, mats_t, outs, outs_t, coefs):
    s, v, q = mix_orders(mats, mats_t, parts)
    b0 = product_scalar(coefs, s, v, q)
    gate1 = 1.0 + coefs[3] * s
    gate2 = 1.0 + coefs[4] * s
    s, v, q = mix_orders(outs, outs_t, [b0] + [x * gate1 for x in v] + [x * gate2 for x in q])
    return [s] + v + q


def node_two(parts, residual, mats, mats_t, out, out_t, coefs, hid, hid_t, read):
    s, v, q = mix_orders(mats, mats_t, parts)
    scalars = mixed(out, out_t, product_scalar(coefs, s, v, q)) + residual
    hidden = silu(mixed(hid, hid_t, scalars))
    return jnp.sum(read * hidden, axis=0, keepdims=True)


def radial_forward(w_in_t, mid_stack, basis):
    pre1 = dot_high(w_in_t, basis)
    pre2 = dot_split(mid_stack, silu(pre1))
    return pre1, pre2


def radial_backward(out_back, mid_back, w_in, dw, pre1, pre2):
    dpre2 = dot(out_back, jnp.concatenate([dw, dw], axis=0)) * silu_slope(pre2)
    dpre1 = dot_split(mid_back, dpre2) * silu_slope(pre1)
    return dot_high(w_in, dpre1)


def layer_one_kernel(
    nodes, idx, emb, w_in_t, mid_stack, out_stack, mix, mix_t, outs, outs_t, coefs, border,
    rounded, border_feats, idx_out, offs, f_out, w_out, pre1_out, pre2_out, pooled, y_s,
):
    atoms = rounded.shape[1]
    total = nodes.shape[1]
    slots = idx.shape[1] // atoms
    n = nodes[...]
    hi = n.astype(bf16).astype(f32)
    mid = (n - hi).astype(bf16).astype(f32)
    lo = n - hi - mid
    stack = jnp.concatenate([hi, mid, lo, jnp.zeros_like(lo)], axis=0).astype(bf16)

    def block(b, carry):
        own = nodes[:, pl.ds(pl.multiple_of(b * L, L), L)]
        own2 = jnp.concatenate([own, own], axis=1)

        def gather(c, carry):
            at = pl.ds(pl.multiple_of(b * (L * slots) + c * G, G), G)
            index = idx[:, at]
            got = dot(stack, one_hot_columns(total, index))
            got = got[0:8] + got[8:16] + got[16:24]
            valid = (index >= 0) & (got[4:5] * own2[4:5] > 0.5)
            idx_out[:, at] = jnp.where(valid, index, -1)
            offset = got - own2
            offs[:, at] = offset
            kind = jnp.where(valid, jnp.maximum(got[3:4], 0.0).astype(jnp.int32), -1)
            hot = one_hot_columns(L, kind)
            f_out[:, at] = dot(emb[...], jnp.concatenate([hot, hot], axis=0))
            basis, ys = geometry(offset[0:1], offset[1:2], offset[2:3])
            y_s[:, pl.ds(pl.multiple_of(c * G, G), G)] = jnp.concatenate(ys, axis=0)
            pre1, pre2 = radial_forward(w_in_t[...], mid_stack[...], basis)
            pre1_out[:, at] = pre1
            pre2_out[:, at] = pre2
            w_out[:, at] = dot_split(out_stack[...], silu(pre2))
            return carry

        lax.fori_loop(0, slots * L // G, gather, 0)

        def channels(c, carry):
            row = pl.multiple_of(c * CB, CB)
            acc = [jnp.zeros((CB, L), f32)] * 9
            for s in range(slots):
                at = pl.ds(pl.multiple_of(b * (L * slots) + s * L, L), L)
                f = f_out[pl.ds(row, CB), at]
                w = [w_out[pl.ds(row + p * L, CB), at] * f for p in range(3)]
                acc[0] = acc[0] + w[0]
                for k in range(8):
                    y = y_s[k : k + 1, s * L : (s + 1) * L]
                    acc[1 + k] = acc[1 + k] + (w[1] if k < 3 else w[2]) * y
            for k in range(9):
                pooled[pl.ds(row + k * L, CB), pl.ds(pl.multiple_of(b * L, L), L)] = acc[k] / slots
            return carry

        lax.fori_loop(0, L // CB, channels, 0)
        here = pl.ds(pl.multiple_of(b * L, L), L)
        parts = [pooled[k * L : (k + 1) * L, here] for k in range(9)]
        new = node_one(
            parts, [mix[k] for k in range(3)], [mix_t[k] for k in range(3)],
            [outs[k] for k in range(3)], [outs_t[k] for k in range(3)],
            [coefs[:, k : k + 1] for k in range(5)],
        )
        kind = jnp.maximum(own[3:4], 0.0).astype(jnp.int32)
        hot = one_hot_columns(L, kind)
        new[0] = new[0] + dot(emb[...], jnp.concatenate([hot, hot], axis=0))
        for k in range(9):
            rounded[k * L : (k + 1) * L, here] = new[k].astype(bf16)
        return carry

    lax.fori_loop(0, atoms // L, block, 0)
    border_feats[...] = dot(rounded[...], one_hot_columns(atoms, border[...])).astype(bf16)


def layer_two_kernel(
    rounded, prev, center, nxt, idx, idx_col, offs, occ, w_in, w_in_t, mid_stack, mid_back, out_stack, out_back,
    mix, mix_t, out, out_t, coefs, lin, hid, hid_t, read,
    energy, dlocal, dprev, dcenter, dnext, doffs,
    table, dtable, dres, src, w_s, dw_s, pre1_s, pre2_s, y_s, dy_s, pooled, dpooled,
):
    atoms = energy.shape[1]
    total = table.shape[1]
    slots = idx.shape[1] // atoms
    edges = slots * L
    dtable[...] = jnp.zeros_like(dtable)
    table[:, 0:atoms] = rounded[...]
    table[:, atoms : atoms + 3 * L] = prev[...]
    table[:, atoms + 3 * L : atoms + 6 * L] = center[...]
    table[:, atoms + 6 * L : atoms + 9 * L] = nxt[...]

    def block(b, carry):
        def gather(c, carry):
            at = pl.ds(pl.multiple_of(b * edges + c * G, G), G)
            to = pl.ds(pl.multiple_of(c * G, G), G)
            src[:, to] = dot(table[...], one_hot_columns(total, idx[:, at])).astype(bf16)
            basis, ys = geometry(offs[0:1, at], offs[1:2, at], offs[2:3, at])
            y_s[:, to] = jnp.concatenate(ys, axis=0)
            pre1, pre2 = radial_forward(w_in_t[...], mid_stack[...], basis)
            pre1_s[:, to] = pre1
            pre2_s[:, to] = pre2
            w_s[:, to] = dot_split(out_stack[...], silu(pre2))
            return carry

        lax.fori_loop(0, edges // G, gather, 0)

        def load(row, s):
            at = slice(s * L, (s + 1) * L)
            f = [src[pl.ds(row + k * L, CB), at].astype(f32) for k in range(9)]
            w = [w_s[pl.ds(row + p * L, CB), at] for p in range(7)]
            y = [y_s[k : k + 1, at] for k in range(8)]
            return f, w, y

        def forward(c, carry):
            row = pl.multiple_of(c * CB, CB)
            acc = [jnp.zeros((CB, L), f32)] * 9
            for s in range(slots):
                f, w, y = load(row, s)
                along1 = f[1] * y[0] + f[2] * y[1] + f[3] * y[2]
                along2 = f[4] * y[3] + f[5] * y[4] + f[6] * y[5] + f[7] * y[6] + f[8] * y[7]
                acc[0] = acc[0] + w[0] * f[0] + w[1] * along1 + w[2] * along2
                s1, s2 = w[3] * f[0], w[5] * f[0]
                for k in range(3):
                    acc[1 + k] = acc[1 + k] + s1 * y[k] + w[4] * f[1 + k]
                for k in range(3, 8):
                    acc[1 + k] = acc[1 + k] + s2 * y[k] + w[6] * f[1 + k]
            for k in range(9):
                pooled[pl.ds(row + k * L, CB), :] = acc[k] / slots
            return carry

        lax.fori_loop(0, L // CB, forward, 0)
        here = pl.ds(pl.multiple_of(b * L, L), L)
        mats = [mix[k] for k in range(3)]
        mats_t = [mix_t[k] for k in range(3)]
        cs = [coefs[:, k : k + 1] for k in range(3)]
        occupied = occ[:, here]

        def node(parts, residual):
            return node_two(
                parts, residual, mats, mats_t, out[...], out_t[...], cs,
                hid[...], hid_t[...], read[...],
            )

        residual = table[0:L, here].astype(f32)
        value, pull = jax.vjp(
            node, [pooled[k * L : (k + 1) * L, :] for k in range(9)], residual
        )
        linear = jnp.sum(lin[...] * residual, axis=0, keepdims=True)
        energy[:, here] = (value + linear) * occupied
        dparts, dresidual = pull(occupied)
        for k in range(9):
            dpooled[k * L : (k + 1) * L, :] = dparts[k] / slots
        dy_s[...] = jnp.zeros_like(dy_s)

        def backward(c, carry):
            row = pl.multiple_of(c * CB, CB)
            g = [dpooled[pl.ds(row + k * L, CB), :] for k in range(9)]
            for s in range(slots):
                at = slice(s * L, (s + 1) * L)
                f, w, y = load(row, s)
                dw = [None] * 7
                dw[0] = g[0] * f[0]
                dw[1] = g[0] * (f[1] * y[0] + f[2] * y[1] + f[3] * y[2])
                dw[2] = g[0] * (
                    f[4] * y[3] + f[5] * y[4] + f[6] * y[5] + f[7] * y[6] + f[8] * y[7]
                )
                g1 = g[1] * y[0] + g[2] * y[1] + g[3] * y[2]
                g2 = g[4] * y[3] + g[5] * y[4] + g[6] * y[5] + g[7] * y[6] + g[8] * y[7]
                dw[3] = f[0] * g1
                dw[4] = g[1] * f[1] + g[2] * f[2] + g[3] * f[3]
                dw[5] = f[0] * g2
                dw[6] = g[4] * f[4] + g[5] * f[5] + g[6] * f[6] + g[7] * f[7] + g[8] * f[8]
                for p in range(7):
                    dw_s[pl.ds(row + p * L, CB), at] = dw[p].astype(bf16)
                v0, q0 = w[1] * g[0], w[2] * g[0]
                sv, sq = w[3] * f[0], w[5] * f[0]
                df = w[0] * g[0] + w[3] * g1 + w[5] * g2
                src[pl.ds(row, CB), at] = df.astype(bf16)
                for k in range(8):
                    base = v0 if k < 3 else q0
                    side = sv if k < 3 else sq
                    direct = w[4] if k < 3 else w[6]
                    dy = base * f[1 + k] + side * g[1 + k]
                    dy_s[k * 8 : (k + 1) * 8, at] += dy[0:8] + dy[8:16]
                    df = base * y[k] + direct * g[1 + k]
                    src[pl.ds(row + (1 + k) * L, CB), at] = df.astype(bf16)
            return carry

        lax.fori_loop(0, L // CB, backward, 0)

        def edge_back(c, carry):
            at = pl.ds(pl.multiple_of(b * edges + c * G, G), G)
            to = pl.ds(pl.multiple_of(c * G, G), G)
            dbasis = radial_backward(
                out_back[...], mid_back[...], w_in[...], dw_s[:, to], pre1_s[:, to], pre2_s[:, to]
            )
            dys = tuple(
                jnp.sum(dy_s[k * 8 : (k + 1) * 8, to], axis=0, keepdims=True) for k in range(8)
            )
            _, pull = jax.vjp(geometry, offs[0:1, at], offs[1:2, at], offs[2:3, at])
            dx, dy, dz = pull((dbasis, dys))
            doffs[:, at] = jnp.concatenate([dx, dy, dz, jnp.zeros((5, G), f32)], axis=0)
            return carry

        lax.fori_loop(0, edges // G, edge_back, 0)

        def scatter(t, carry):
            to = pl.ds(pl.multiple_of(t * G, G), G)
            column = idx_col[pl.ds(pl.multiple_of(b * edges, 8), edges), :]
            part = dot(src[...], one_hot_rows(column, t * G, G))

            dtable[:, to] += part
            return carry

        lax.fori_loop(0, total // G, scatter, 0)
        dres[:, here] = dresidual
        return carry

    lax.fori_loop(0, atoms // L, block, 0)
    dlocal[...] = dtable[:, 0:atoms]
    dlocal[0:L, :] += dres[...] + lin[...] * occ[...]
    dprev[...] = dtable[:, atoms : atoms + 3 * L].astype(bf16)
    dcenter[...] = dtable[:, atoms + 3 * L : atoms + 6 * L]
    dnext[...] = dtable[:, atoms + 6 * L : atoms + 9 * L].astype(bf16)


def layer_one_back_kernel(
    dlocal, back, border_col, idx_col, offs, doffs_two, f_in, w_in_edges, pre1_in, pre2_in, pooled,
    w_in, mid_back, out_back, mix, mix_t, outs, outs_t, coefs,
    dpos, dw_s, y_s, dy_s, dh_s, dpooled,
):
    atoms = dlocal.shape[1]
    total = dpos.shape[1]
    slots = offs.shape[1] // atoms
    edges = slots * L
    hot = one_hot_rows(border_col[...], 0, atoms)
    back_hi, back_lo = hi_lo(back[...])
    dh_s[...] = dlocal[...] + dot(back_hi, hot) + dot(back_lo, hot)
    dpos[...] = jnp.zeros_like(dpos)

    def block(b, carry):
        here = pl.ds(pl.multiple_of(b * L, L), L)
        mats = [mix[k] for k in range(3)]
        mats_t = [mix_t[k] for k in range(3)]
        out = [outs[k] for k in range(3)]
        out_t = [outs_t[k] for k in range(3)]
        cs = [coefs[:, k : k + 1] for k in range(5)]
        _, pull = jax.vjp(
            lambda parts: node_one(parts, mats, mats_t, out, out_t, cs),
            [pooled[k * L : (k + 1) * L, here] for k in range(9)],
        )
        (dparts,) = pull([dh_s[k * L : (k + 1) * L, here] for k in range(9)])
        for k in range(9):
            dpooled[k * L : (k + 1) * L, :] = dparts[k] / slots

        def harmonics(c, carry):
            at = pl.ds(pl.multiple_of(b * edges + c * G, G), G)
            _, ys = geometry(offs[0:1, at], offs[1:2, at], offs[2:3, at])
            y_s[:, pl.ds(pl.multiple_of(c * G, G), G)] = jnp.concatenate(ys, axis=0)
            return carry

        lax.fori_loop(0, edges // G, harmonics, 0)
        dy_s[...] = jnp.zeros_like(dy_s)

        def backward(c, carry):
            row = pl.multiple_of(c * CB, CB)
            g = [dpooled[pl.ds(row + k * L, CB), :] for k in range(9)]
            for s in range(slots):
                at = slice(s * L, (s + 1) * L)
                far = pl.ds(pl.multiple_of(b * edges + s * L, L), L)
                f = f_in[pl.ds(row, CB), far]
                y = [y_s[k : k + 1, at] for k in range(8)]
                dw_s[pl.ds(row, CB), at] = (g[0] * f).astype(bf16)
                g1 = g[1] * y[0] + g[2] * y[1] + g[3] * y[2]
                g2 = g[4] * y[3] + g[5] * y[4] + g[6] * y[5] + g[7] * y[6] + g[8] * y[7]
                dw_s[pl.ds(row + L, CB), at] = (f * g1).astype(bf16)
                dw_s[pl.ds(row + 2 * L, CB), at] = (f * g2).astype(bf16)
                w1 = w_in_edges[pl.ds(row + L, CB), far] * f
                w2 = w_in_edges[pl.ds(row + 2 * L, CB), far] * f
                for k in range(8):
                    dy = (w1 if k < 3 else w2) * g[1 + k]
                    dy_s[k * 8 : (k + 1) * 8, at] += dy[0:8] + dy[8:16]
            return carry

        lax.fori_loop(0, L // CB, backward, 0)

        def edge_back(c, own):
            at = pl.ds(pl.multiple_of(b * edges + c * G, G), G)
            to = pl.ds(pl.multiple_of(c * G, G), G)
            dbasis = radial_backward(
                out_back[...], mid_back[...], w_in[...], dw_s[:, to], pre1_in[:, at], pre2_in[:, at]
            )
            dys = tuple(
                jnp.sum(dy_s[k * 8 : (k + 1) * 8, to], axis=0, keepdims=True) for k in range(8)
            )
            _, pull = jax.vjp(geometry, offs[0:1, at], offs[1:2, at], offs[2:3, at])
            dx, dy, dz = pull((dbasis, dys))
            d = jnp.concatenate([dx, dy, dz, jnp.zeros((5, G), f32)], axis=0) + doffs_two[:, at]
            hi = d.astype(bf16).astype(f32)
            both = jnp.concatenate([hi, d - hi], axis=0).astype(bf16)
            column = idx_col[pl.ds(pl.multiple_of(b * edges + c * G, G), G), :]
            part = dot(both, one_hot_rows(column, 0, total))
            dpos[...] += part[0:8] + part[8:16]
            return own + d[:, 0:L] + d[:, L : 2 * L]

        own = lax.fori_loop(0, edges // G, edge_back, jnp.zeros((8, L), f32))
        dpos[:, here] -= own
        return carry

    lax.fori_loop(0, atoms // L, block, 0)


def from_behind(block, axis, distance):
    devices = range(lax.axis_size(axis))
    route = [((i - distance) % len(devices), i) for i in devices]
    return lax.ppermute(block, axis, route)


def parts_of(w):
    hi = lax.reduce_precision(w, 8, 7)
    return hi.astype(bf16), (w - hi).astype(bf16)


def k_stack(w):
    hi, lo = parts_of(w)
    return jnp.concatenate([hi, lo, hi], axis=-1)


def call(kernel, outs, scratch, *args):
    return pl.pallas_call(
        kernel,
        out_shape=[jax.ShapeDtypeStruct(s, d) for s, d in outs],
        scratch_shapes=[pltpu.VMEM(s, d) for s, d in scratch],
        compiler_params=params(),
    )(*args)


def on_device(
    positions, species, dest_key, send_list, send_count, border, neighbours, embedding, radial_in,
    radial_mid, radial_out_one, radial_out_two, mix, mix_out_one, mix_out_two, product_one,
    product_two, read_lin, read_hidden, read_out,
):
    own_coords = positions[0, 0]
    own_kinds = species[0, 0]
    listed = send_list[0, 0]
    border_rows = border[0, 0]
    slot_count = listed.shape[1]
    atoms, slots = neighbours.shape[2:]
    count = border_rows.shape[0]
    edge_total = atoms * slots
    total = atoms + 9 * count
    channels = embedding.shape[1]
    feats = 9 * channels

    packet = jnp.concatenate([own_coords, own_kinds.astype(f32)[None]], axis=0)
    wanted = jnp.concatenate([listed.reshape(-1), border_rows])
    hot = (jnp.arange(own_kinds.shape[0])[:, None] == wanted[None, :]).astype(f32)
    picked = jnp.dot(packet, hot, precision=highest)
    used = jnp.arange(slot_count)[None, :] < send_count[0, 0][:, None]
    used = jnp.concatenate([used.reshape(-1), jnp.ones((count,), bool)])
    picked = jnp.concatenate([picked[:3], jnp.where(used, picked[3], -1.0)[None]], axis=0)
    leave = [picked[:, d * slot_count : (d + 1) * slot_count] for d in range(4)]
    edge_packet = picked[:, 4 * slot_count :]
    up = from_behind(jnp.concatenate([edge_packet, leave[0]], axis=1), "gx", 1)
    down = from_behind(jnp.concatenate([edge_packet, leave[1]], axis=1), "gx", -1)

    def shift(block, axis, amount):
        return block + jnp.zeros((4, 1), f32).at[axis, 0].set(amount)

    triple = jnp.concatenate(
        [shift(up[:, :count], 0, -1.0), edge_packet, shift(down[:, :count], 0, 1.0)], axis=1
    )
    before = from_behind(jnp.concatenate([triple, leave[2]], axis=1), "gy", 1)
    after = from_behind(jnp.concatenate([triple, leave[3]], axis=1), "gy", -1)
    local = jnp.concatenate(
        [
            packet,
            shift(up[:, count:], 0, -1.0),
            shift(down[:, count:], 0, 1.0),
            shift(before[:, 3 * count :], 1, -1.0),
            shift(after[:, 3 * count :], 1, 1.0),
        ],
        axis=1,
    )
    staying = (dest_key[0, 0] == 0).astype(f32)
    occupied = jnp.concatenate([staying, (local[3, staying.shape[0] :] >= 0).astype(f32)])
    everything = jnp.concatenate(
        [local, shift(before[:, : 3 * count], 1, -1.0), triple, shift(after[:, : 3 * count], 1, 1.0)],
        axis=1,
    )
    occupied_all = jnp.concatenate([occupied, jnp.ones((9 * count,), f32)])
    nodes = jnp.concatenate([everything, occupied_all[None], jnp.zeros((3, total), f32)], axis=0)

    index = neighbours[0, 0]
    ghost = index - atoms
    which = ghost // count
    moved = atoms + ((which % 3) * 3 + which // 3) * count + ghost % count
    index = jnp.where(index >= atoms, moved, index)
    index = index.reshape(atoms // L, L, slots).transpose(0, 2, 1).reshape(1, edge_total)

    emb = jnp.pad(embedding, ((0, L - embedding.shape[0]), (0, 0))).T
    emb = jnp.concatenate(parts_of(emb), axis=1)
    w_in_t = jnp.swapaxes(radial_in, 1, 2)
    mid_t = k_stack(jnp.swapaxes(radial_mid, 1, 2))
    mid = k_stack(radial_mid)
    one_t, two_t = k_stack(radial_out_one.T), k_stack(radial_out_two.T)
    one_b = jnp.concatenate(parts_of(radial_out_one), axis=1)
    two_b = jnp.concatenate(parts_of(radial_out_two), axis=1)
    mix_t, mix_k = k_stack(jnp.swapaxes(mix, 2, 3)), k_stack(mix)
    outs_t, outs_k = k_stack(jnp.swapaxes(mix_out_one, 1, 2)), k_stack(mix_out_one)

    hidden = radial_in.shape[2]
    rounded, border_feats, idx, offs, f_e, w_e, pre1, pre2, pooled = call(
        layer_one_kernel,
        [
            ((feats, atoms), bf16), ((feats, count), bf16), ((1, edge_total), jnp.int32),
            ((8, edge_total), f32), ((channels, edge_total), f32), ((3 * channels, edge_total), f32),
            ((hidden, edge_total), f32), ((hidden, edge_total), f32), ((feats, atoms), f32),
        ],
        [((8, slots * L), f32)],
        nodes, index, emb, w_in_t[0], mid_t[0], one_t, mix_k[0], mix_t[0], outs_k, outs_t,
        product_one.T, border_rows[None],
    )
    left = from_behind(border_feats, "gx", 1)
    right = from_behind(border_feats, "gx", -1)
    middle = jnp.concatenate([left, border_feats, right], axis=1)
    prev = from_behind(middle, "gy", 1)
    nxt = from_behind(middle, "gy", -1)
    idx_col = idx.reshape(edge_total, 1)

    energy, dlocal, dprev, dcenter, dnext, doffs = call(
        layer_two_kernel,
        [
            ((1, atoms), f32), ((feats, atoms), f32), ((feats, 3 * count), bf16),
            ((feats, 3 * count), f32), ((feats, 3 * count), bf16), ((8, edge_total), f32),
        ],
        [
            ((feats, total), bf16), ((feats, total), f32), ((channels, atoms), f32),
            ((feats, slots * L), bf16), ((7 * channels, slots * L), f32),
            ((7 * channels, slots * L), bf16), ((hidden, slots * L), f32),
            ((hidden, slots * L), f32), ((8, slots * L), f32), ((64, slots * L), f32),
            ((feats, L), f32), ((feats, L), f32),
        ],
        rounded, prev, middle, nxt, idx, idx_col, offs, occupied[None], radial_in[1], w_in_t[1],
        mid_t[1], mid[1], two_t, two_b, mix_k[1], mix_t[1], k_stack(mix_out_two), k_stack(mix_out_two.T), product_two.T,
        read_lin[:, None], k_stack(read_hidden), k_stack(read_hidden.T), read_out[:, None],
    )
    column = dcenter + from_behind(dprev, "gy", -1).astype(f32)
    column = column + from_behind(dnext, "gy", 1).astype(f32)
    back = column[:, count : 2 * count]
    back = back + from_behind(column[:, :count].astype(bf16), "gx", -1).astype(f32)
    back = back + from_behind(column[:, 2 * count :].astype(bf16), "gx", 1).astype(f32)

    (dpos,) = call(
        layer_one_back_kernel,
        [((8, total), f32)],
        [
            ((3 * channels, slots * L), bf16), ((8, slots * L), f32), ((64, slots * L), f32),
            ((feats, atoms), f32), ((feats, L), f32),
        ],
        dlocal, back, border_rows[:, None], idx_col, offs, doffs, f_e, w_e, pre1, pre2, pooled,
        radial_in[0], mid[0], one_b, mix_k[0], mix_t[0], outs_k, outs_t, product_one.T,
    )
    dpos = dpos[:3]
    column = dpos[:, atoms + 3 * count : atoms + 6 * count]
    column = column + from_behind(dpos[:, atoms : atoms + 3 * count], "gy", -1)
    column = column + from_behind(dpos[:, atoms + 6 * count :], "gy", 1)
    back = column[:, count : 2 * count]
    back = back + from_behind(column[:, :count], "gx", -1)
    back = back + from_behind(column[:, 2 * count :], "gx", 1)
    hot = (border_rows[:, None] == jnp.arange(atoms)[None, :]).astype(f32)
    forces = -(dpos[:, :atoms] + jnp.dot(back, hot, precision=highest))
    return (energy[None], forces[None, None])


def solution(mesh):
    whole = P()
    in_specs = (
        P("gx", "gy", None, None),
        P("gx", "gy", None),
        P("gx", "gy", None),
        P("gx", "gy", None, None),
        P("gx", "gy", None),
        P("gx", "gy", None),
        P("gx", "gy", None, None),
    ) + (whole,) * 13
    out_specs = (P("gx", "gy", None), P("gx", "gy", None, None))
    return jax.shard_map(
        on_device, mesh=mesh, in_specs=in_specs, out_specs=out_specs, check_vma=False
    )
```

time: 1790 us -> 275 us (0.15); the launches traced: 1760 us -> 275 us
  local copies, waits for them, and re-layouts: 894 us -> 18.8 us
  other arithmetic: 530 us -> 14.9 us
  matrix products: 213 us -> 1.1 us
  Pallas kernels: 0 us -> 146 us
  loops' own time: 36.7 us -> 0 us
    gather x89 -> x0, local copies, waits for them, and re-layouts: 291 us -> none  [the longest x24 125 us: interaction(): source = feats_all[:, flat_index] * edge_mask[None, :]]
    dot_general x137 -> x2, matrix products: 213 us -> 1.1 us  [the longest x1 0.95 us: on_device(): forces = -(dpos[:, :atoms] + jnp.dot(back, hot, precision=highest))]
    reduce_sum x84 -> x0, other arithmetic: 187 us -> none  [the longest x36 86.6 us: pooling(): jnp.sum(message.reshape(message.shape[:-1] + (atoms, slots)), axis=-1)]
    mul x132 -> x0, local copies, waits for them, and re-layouts: 151 us -> none  [the longest x3 24.2 us: interaction(): source = feats_all[:, flat_index] * edge_mask[None, :]]
    pallas_call x0 -> x3, Pallas kernels: none -> 146 us  [call(): pl.pallas_call(kernel, out_shape=[jax.ShapeDtypeStruct(s, d) for s, d in...]
    reshape x106 -> x2, local copies, waits for them, and re-layouts: 122 us -> 2.76 us  [the longest x1 2.14 us: on_device(): idx_col = idx.reshape(edge_total, 1)]
    scatter-add x12 -> x0, other arithmetic: 117 us -> none  [the longest x3 56.5 us: interaction(): source = feats_all[:, flat_index] * edge_mask[None, :]]
    mul x114 -> x0, other arithmetic: 108 us -> none  [the longest x9 32 us: interaction(): source = feats_all[:, flat_index] * edge_mask[None, :]]
  transfers between devices with their start and end apart: 20 -> 16, of which waited for: 12 -> 13; matrix products, arithmetic and copies ran while one was open for 2% -> 8% of each run, Pallas kernels for 0% -> 0%
where the time goes in v1:
time: 275 us
  Pallas kernels  146 us (53%)
  waiting for transfers between devices  67.1 us (24%)
  starting transfers between devices  25.3 us (9%)
  local copies, waits for them, and re-layouts  18.8 us (7%)
  other arithmetic  14.9 us (5%)
    pallas_call x3, Pallas kernels, call(): pl.pallas_call(kernel, out_shape=[jax.ShapeDtypeStruct(s, d) for s, d in...  146 us
    ppermute x16, waiting for transfers between devices, from_behind(): return lax.ppermute(block, axis, route)  67.1 us
    ppermute x16, starting transfers between devices, from_behind(): return lax.ppermute(block, axis, route)  25.3 us
    unnamed x60, local copies, waits for them, and re-layouts  7.26 us
  transfers between devices with their start and end apart: 16, of which 13 were waited for; matrix products, arithmetic and copies ran while one was open for 8% of the time, Pallas kernels for 0%

profile of v1, /device:TPU:0, one launch (start us, length us, event | category | flops | bytes accessed | tf_op | source)
XLA Modules:
  0.0 274.9 jit_solution(7468238251302250087)
XLA Ops:
  4.7 3.9 %collective-permute-start.1 = (f32[4,160]{1,0:T(4,128)S(1)}, f32[4,160]{1,0:T(4,128)S(1)}, u32[]{:S(2)}, u32[]{:S(2)}) collective-permute-start(f32[4,160]{1,0:T(4,128)S(1)} %get-tuple-element.174), channel_id=1, source_target_pairs={{8,0},{16,8},{24,16},{0,24},{9,1},{17,9},{25,17},{1,25},{10,2},{18... | collective-permute-start | bytes 7688 | tf_op jit(solution)/shard_map/ppermute | solution.py:462
  24.2 2.8 %collective-permute-start.3 = (f32[4,416]{1,0:T(4,128)S(1)}, f32[4,416]{1,0:T(4,128)S(1)}, u32[]{:S(2)}, u32[]{:S(2)}) collective-permute-start(f32[4,416]{1,0:T(4,128)S(1)} %get-tuple-element.169), channel_id=1, source_target_pairs={{1,0},{2,1},{3,2},{4,3},{5,4},{6,5},{7,6},{0,7},{9,8},{10,9},{11,1... | collective-permute-start | bytes 19976 | tf_op jit(solution)/shard_map/ppermute | solution.py:462
  28.4 3.4 %collective-permute-done.2 = f32[4,416]{1,0:T(4,128)S(1)} collective-permute-done((f32[4,416]{1,0:T(4,128)S(1)}, f32[4,416]{1,0:T(4,128)S(1)}, u32[]{:S(2)}, u32[]{:S(2)}) %collective-permute-start.2) | collective-permute-done | bytes 6688 | tf_op jit(solution)/shard_map/ppermute | solution.py:462
  33.0 28.4 %shard_map.203 = (bf16[1152,384]{1,0:T(8,128)(2,1)}, bf16[1152,128]{1,0:T(8,128)(2,1)}, s32[1,4608]{1,0:T(1,128)}, f32[8,4608]{1,0:T(8,128)}, f32[128,4608]{1,0:...) custom-call(f32[8,1536]{1,0:T(8,128)} %maximum_maximum_fusion.nodes, ...), custom_call_target="tpu_custom_call" | custom-call | tf_op jit(solution)/shard_map/pallas_call | solution.py:476
  61.4 1.7 collective-permute-start.4
  64.5 6.4 %collective-permute-done.4 = bf16[1152,128]{1,0:T(8,128)(2,1)S(1)} collective-permute-done((bf16[1152,128]{1,0:T(8,128)(2,1)}, bf16[1152,128]{1,0:T(8,128)(2,1)S(1)}, u32[]{:S(2)}, u32[]{:S(2)}) %collective-permute-start.4) | collective-permute-done | bytes 294944 | tf_op jit(solution)/shard_map/ppermute | solution.py:462
  72.0 1.4 collective-permute-done.5
  73.6 3.7 %collective-permute-start.7 = (bf16[1152,384]{1,0:T(8,128)(2,1)S(1)}, bf16[1152,384]{1,0:T(8,128)(2,1)S(1)}, u32[]{:S(2)}, u32[]{:S(2)}) collective-permute-start(bf16[1152,384]{1,0:T(8,128)(2,1)S(1)} %constant_dynamic-update-slice_fusion.center), channel_id=1, source_target_pairs={{1,0},{2,1},{3,2},{4,3},{5,4},{6,5},{7,6},{0,7},{9,8},{10,9},{11,1... | collective-permute-start | bytes 2654216 | tf_op jit(solution)/shard_map/ppermute | solution.py:462
  79.2 2.1 copy.75.idx_col
  81.9 13.2 %collective-permute-done.6.prev = bf16[1152,384]{1,0:T(8,128)(2,1)S(1)} collective-permute-done((bf16[1152,384]{1,0:T(8,128)(2,1)S(1)}, bf16[1152,384]{1,0:T(8,128)(2,1)S(1)}, u32[]{:S(2)}, u32[]{:S(2)}) %collective-permute-start.6) | collective-permute-done | bytes 884768 | tf_op jit(solution)/shard_map/ppermute | solution.py:462
  96.4 88.9 %shard_map.204 = (f32[1,384]{1,0:T(1,128)}, f32[1152,384]{1,0:T(8,128)}, bf16[1152,384]{1,0:T(8,128)(2,1)}, f32[1152,384]{1,0:T(8,128)}, bf16[1152,384]{1,0:T(8,128)(2,1)}, /*index=5*/f32[8,4608]{1,0:T(8,128)}) custom-call(bf16[1152,384]{1,0:T(8,128)(2,1)} %get-tuple-element.97.rounded, bf16[1152,384]{1,0:T(8,128)(2,1)} %copy-done.2, ...), custom_call_target="tpu_custom_call" | custom-call | tf_op jit(solution)/shard_map/pallas_call | solution.py:476
  185.3 2.7 collective-permute-start.8
  188.8 19.4 %collective-permute-done.8 = bf16[1152,384]{1,0:T(8,128)(2,1)S(1)} collective-permute-done((bf16[1152,384]{1,0:T(8,128)(2,1)}, bf16[1152,384]{1,0:T(8,128)(2,1)S(1)}, u32[]{:S(2)}, u32[]{:S(2)}) %collective-permute-start.8) | collective-permute-done | bytes 884768 | tf_op jit(solution)/shard_map/ppermute | solution.py:462
  208.2 2.2 collective-permute-done.9
  210.4 1.8 fusion.41
  212.2 2.5 collective-permute-start.10
  215.5 7.2 %collective-permute-done.10 = bf16[1152,128]{1,0:T(8,128)(2,1)S(1)} collective-permute-done((bf16[1152,128]{1,0:T(8,128)(2,1)S(1)}, bf16[1152,128]{1,0:T(8,128)(2,1)S(1)}, u32[]{:S(2)}, u32[]{:S(2)}) %collective-permute-start.10) | collective-permute-done | bytes 294944 | tf_op jit(solution)/shard_map/ppermute | solution.py:462
  222.7 3.3 %collective-permute-done.11 = bf16[1152,128]{1,0:T(8,128)(2,1)S(1)} collective-permute-done((bf16[1152,128]{1,0:T(8,128)(2,1)S(1)}, bf16[1152,128]{1,0:T(8,128)(2,1)S(1)}, u32[]{:S(2)}, u32[]{:S(2)}) %collective-permute-start.11) | collective-permute-done | bytes 294944 | tf_op jit(solution)/shard_map/ppermute | solution.py:462
  226.9 29.2 %shard_map.205 = f32[8,1536]{1,0:T(8,128)} custom-call(f32[1152,384]{1,0:T(8,128)} %get-tuple-element.102.dlocal, f32[1152,128]{1,0:T(8,128)} %fusion.back, s32[128,1]{1,0:T(8,128)} %copy.79.border_col, s32[4608,1]{1,0:T(8,128)} %copy.75.idx_col, f32[8,4608]{1,0:T(8,128)} %get-tuple-element.100.offs, f32[8,4608]{1,0:T(8,128)} %get-tuple-element.106.doffs_two, ...), custom_call_target="tpu_custom_call" | custom-call | tf_op jit(solution)/shard_map/pallas_call | solution.py:476
  256.9 3.1 %collective-permute-start.12 = (f32[3,384]{1,0:T(4,128)S(1)}, f32[3,384]{1,0:T(4,128)S(1)}, u32[]{:S(2)}, u32[]{:S(2)}) collective-permute-start(f32[3,384]{1,0:T(4,128)S(1)} %get-tuple-element.158), channel_id=1, source_target_pairs={{1,0},{2,1},{3,2},{4,3},{5,4},{6,5},{7,6},{0,7},{9,8},{10,9},{11,1... | collective-permute-start | bytes 13832 | tf_op jit(solution)/shard_map/ppermute | solution.py:462
  260.0 1.3 collective-permute-done.12
  261.4 3.5 %collective-permute-done.13 = f32[3,384]{1,0:T(4,128)S(1)} collective-permute-done((f32[3,384]{1,0:T(4,128)S(1)}, f32[3,384]{1,0:T(4,128)S(1)}, u32[]{:S(2)}, u32[]{:S(2)}) %collective-permute-start.13) | collective-permute-done | bytes 4640 | tf_op jit(solution)/shard_map/ppermute | solution.py:462
  265.6 3.3 %collective-permute-start.14 = (f32[3,128]{1,0:T(4,128)S(1)}, f32[3,128]{1,0:T(4,128)S(1)}, u32[]{:S(2)}, u32[]{:S(2)}) collective-permute-start(f32[3,128]{1,0:T(4,128)S(1)} %get-tuple-element.166), channel_id=1, source_target_pairs={{8,0},{16,8},{24,16},{0,24},{9,1},{17,9},{25,17},{1,25},{10,2},{18... | collective-permute-start | bytes 4616 | tf_op jit(solution)/shard_map/ppermute | solution.py:462
  270.2 3.2 %collective-permute-done.15 = f32[3,128]{1,0:T(4,128)S(1)} collective-permute-done((f32[3,128]{1,0:T(4,128)S(1)}, f32[3,128]{1,0:T(4,128)S(1)}, u32[]{:S(2)}, u32[]{:S(2)}) %collective-permute-start.15) | collective-permute-done | bytes 1568 | tf_op jit(solution)/shard_map/ppermute | solution.py:462
  (154 shorter events, 35.0 us)
Async XLA Ops:
  0.7 10.6 %copy-start.7 = (f32[2,64,64]{2,1,0:T(8,128)S(1)}, f32[2,64,64]{2,1,0:T(8,128)}, u32[]{:S(2)}) copy-start(f32[2,64,64]{2,1,0:T(8,128)} %param.45) | copy-start | bytes 98308
  0.7 10.7 %copy-start.10 = (f32[2,8,64]{2,1,0:T(8,128)S(1)}, f32[2,8,64]{2,1,0:T(8,128)}, u32[]{:S(2)}) copy-start(f32[2,8,64]{2,1,0:T(8,128)} %param.44) | copy-start | bytes 12292
  0.7 11.4 %copy-start.20 = (s32[1,1,256]{2,1,0:T(1,128)S(1)}, s32[1,1,256]{2,1,0:T(1,128)}, u32[]{:S(2)}) copy-start(s32[1,1,256]{2,1,0:T(1,128)} %param.38) | copy-start | bytes 3076
  4.7 19.3 %collective-permute-start.1 = (f32[4,160]{1,0:T(4,128)S(1)}, f32[4,160]{1,0:T(4,128)S(1)}, u32[]{:S(2)}, u32[]{:S(2)}) collective-permute-start(f32[4,160]{1,0:T(4,128)S(1)} %get-tuple-element.174), channel_id=1, source_target_pairs={{8,0},{16,8},{24,16},{0,24},{9,1},{17,9},{25,17},{1,25},{10,2},{18... | collective-permute-start | bytes 7688 | tf_op jit(solution)/shard_map/ppermute | solution.py:462
  8.6 15.5 %collective-permute-start = (f32[4,160]{1,0:T(4,128)S(1)}, f32[4,160]{1,0:T(4,128)S(1)}, u32[]{:S(2)}, u32[]{:S(2)}) collective-permute-start(f32[4,160]{1,0:T(4,128)S(1)} %get-tuple-element.173), channel_id=1, source_target_pairs={{24,0},{0,8},{8,16},{16,24},{25,1},{1,9},{9,17},{17,25},{26,2},{2,... | collective-permute-start | bytes 7688 | tf_op jit(solution)/shard_map/ppermute | solution.py:462
  15.6 12.7 %copy-start.17 = (f32[4]{0:T(128)S(1)}, f32[4]{0:T(128)}, u32[]{:S(2)}) copy-start(f32[4]{0:T(128)} %constant.219.clone.1) | copy-start | bytes 52
  15.6 16.2 %copy-start.16 = (f32[4]{0:T(128)S(1)}, f32[4]{0:T(128)}, u32[]{:S(2)}) copy-start(f32[4]{0:T(128)} %constant.218.clone.1) | copy-start | bytes 52
  24.2 4.1 %collective-permute-start.3 = (f32[4,416]{1,0:T(4,128)S(1)}, f32[4,416]{1,0:T(4,128)S(1)}, u32[]{:S(2)}, u32[]{:S(2)}) collective-permute-start(f32[4,416]{1,0:T(4,128)S(1)} %get-tuple-element.169), channel_id=1, source_target_pairs={{1,0},{2,1},{3,2},{4,3},{5,4},{6,5},{7,6},{0,7},{9,8},{10,9},{11,1... | collective-permute-start | bytes 19976 | tf_op jit(solution)/shard_map/ppermute | solution.py:462
  27.0 4.9 %collective-permute-start.2 = (f32[4,416]{1,0:T(4,128)S(1)}, f32[4,416]{1,0:T(4,128)S(1)}, u32[]{:S(2)}, u32[]{:S(2)}) collective-permute-start(f32[4,416]{1,0:T(4,128)S(1)} %get-tuple-element.168), channel_id=1, source_target_pairs={{7,0},{0,1},{1,2},{2,3},{3,4},{4,5},{5,6},{6,7},{15,8},{8,9},{9,10... | collective-permute-start | bytes 19976 | tf_op jit(solution)/shard_map/ppermute | solution.py:462
  61.4 17.9 %copy-start.8 = (s32[1,4608]{1,0:T(1,128)S(1)}, s32[1,4608]{1,0:T(1,128)}, u32[]{:S(2)}) copy-start(s32[1,4608]{1,0:T(1,128)} %get-tuple-element.99.idx) | copy-start | bytes 55300
  61.4 9.5 %collective-permute-start.4 = (bf16[1152,128]{1,0:T(8,128)(2,1)}, bf16[1152,128]{1,0:T(8,128)(2,1)S(1)}, u32[]{:S(2)}, u32[]{:S(2)}) collective-permute-start(bf16[1152,128]{1,0:T(8,128)(2,1)} %get-tuple-element.98), channel_id=1, source_target_pairs={{24,0},{0,8},{8,16},{16,24},{25,1},{1,9},{9,17},{17,25},{26,2},{2,... | collective-permute-start | bytes 884744 | tf_op jit(solution)/shard_map/ppermute | solution.py:462
  63.2 10.2 %collective-permute-start.5 = (bf16[1152,128]{1,0:T(8,128)(2,1)}, bf16[1152,128]{1,0:T(8,128)(2,1)S(1)}, u32[]{:S(2)}, u32[]{:S(2)}) collective-permute-start(bf16[1152,128]{1,0:T(8,128)(2,1)} %get-tuple-element.98), channel_id=1, source_target_pairs={{8,0},{16,8},{24,16},{0,24},{9,1},{17,9},{25,17},{1,25},{10,2},{18... | collective-permute-start | bytes 884744 | tf_op jit(solution)/shard_map/ppermute | solution.py:462
  73.5 21.6 %copy-start = (bf16[1152,384]{1,0:T(8,128)(2,1)}, bf16[1152,384]{1,0:T(8,128)(2,1)S(1)}, u32[]{:S(2)}) copy-start(bf16[1152,384]{1,0:T(8,128)(2,1)S(1)} %constant_dynamic-update-slice_fusion.center) | copy-start | bytes 2654212
  73.5 21.6 %collective-permute-start.6 = (bf16[1152,384]{1,0:T(8,128)(2,1)S(1)}, bf16[1152,384]{1,0:T(8,128)(2,1)S(1)}, u32[]{:S(2)}, u32[]{:S(2)}) collective-permute-start(bf16[1152,384]{1,0:T(8,128)(2,1)S(1)} %constant_dynamic-update-slice_fusion.center), channel_id=1, source_target_pairs={{7,0},{0,1},{1,2},{2,3},{3,4},{4,5},{5,6},{6,7},{15,8},{8,9},{9,10... | collective-permute-start | bytes 2654216 | tf_op jit(solution)/shard_map/ppermute | solution.py:462
  73.6 21.6 %collective-permute-start.7 = (bf16[1152,384]{1,0:T(8,128)(2,1)S(1)}, bf16[1152,384]{1,0:T(8,128)(2,1)S(1)}, u32[]{:S(2)}, u32[]{:S(2)}) collective-permute-start(bf16[1152,384]{1,0:T(8,128)(2,1)S(1)} %constant_dynamic-update-slice_fusion.center), channel_id=1, source_target_pairs={{1,0},{2,1},{3,2},{4,3},{5,4},{6,5},{7,6},{0,7},{9,8},{10,9},{11,1... | collective-permute-start | bytes 2654216 | tf_op jit(solution)/shard_map/ppermute | solution.py:462
  96.4 91.6 %copy-start.13 = (s32[1,1,128]{2,1,0:T(1,128)S(1)}, s32[1,1,128]{2,1,0:T(1,128)}, u32[]{:S(2)}) copy-start(s32[1,1,128]{2,1,0:T(1,128)} %param.41) | copy-start | bytes 1540
  185.3 22.9 %collective-permute-start.8 = (bf16[1152,384]{1,0:T(8,128)(2,1)}, bf16[1152,384]{1,0:T(8,128)(2,1)S(1)}, u32[]{:S(2)}, u32[]{:S(2)}) collective-permute-start(bf16[1152,384]{1,0:T(8,128)(2,1)} %get-tuple-element.104), channel_id=1, source_target_pairs={{1,0},{2,1},{3,2},{4,3},{5,4},{6,5},{7,6},{0,7},{9,8},{10,9},{11,1... | collective-permute-start | bytes 2654216 | tf_op jit(solution)/shard_map/ppermute | solution.py:462
  188.0 22.4 %collective-permute-start.9 = (bf16[1152,384]{1,0:T(8,128)(2,1)}, bf16[1152,384]{1,0:T(8,128)(2,1)S(1)}, u32[]{:S(2)}, u32[]{:S(2)}) collective-permute-start(bf16[1152,384]{1,0:T(8,128)(2,1)} %get-tuple-element.105), channel_id=1, source_target_pairs={{7,0},{0,1},{1,2},{2,3},{3,4},{4,5},{5,6},{6,7},{15,8},{8,9},{9,10... | collective-permute-start | bytes 2654216 | tf_op jit(solution)/shard_map/ppermute | solution.py:462
  212.2 10.6 %collective-permute-start.10 = (bf16[1152,128]{1,0:T(8,128)(2,1)S(1)}, bf16[1152,128]{1,0:T(8,128)(2,1)S(1)}, u32[]{:S(2)}, u32[]{:S(2)}) collective-permute-start(bf16[1152,128]{1,0:T(8,128)(2,1)S(1)} %get-tuple-element.120), channel_id=1, source_target_pairs={{8,0},{16,8},{24,16},{0,24},{9,1},{17,9},{25,17},{1,25},{10,2},{18... | collective-permute-start | bytes 884744 | tf_op jit(solution)/shard_map/ppermute | solution.py:462
  214.7 11.3 %collective-permute-start.11 = (bf16[1152,128]{1,0:T(8,128)(2,1)S(1)}, bf16[1152,128]{1,0:T(8,128)(2,1)S(1)}, u32[]{:S(2)}, u32[]{:S(2)}) collective-permute-start(bf16[1152,128]{1,0:T(8,128)(2,1)S(1)} %get-tuple-element.121), channel_id=1, source_target_pairs={{24,0},{0,8},{8,16},{16,24},{25,1},{1,9},{9,17},{17,25},{26,2},{2,... | collective-permute-start | bytes 884744 | tf_op jit(solution)/shard_map/ppermute | solution.py:462
  256.9 4.5 %collective-permute-start.12 = (f32[3,384]{1,0:T(4,128)S(1)}, f32[3,384]{1,0:T(4,128)S(1)}, u32[]{:S(2)}, u32[]{:S(2)}) collective-permute-start(f32[3,384]{1,0:T(4,128)S(1)} %get-tuple-element.158), channel_id=1, source_target_pairs={{1,0},{2,1},{3,2},{4,3},{5,4},{6,5},{7,6},{0,7},{9,8},{10,9},{11,1... | collective-permute-start | bytes 13832 | tf_op jit(solution)/shard_map/ppermute | solution.py:462
  260.0 4.9 %collective-permute-start.13 = (f32[3,384]{1,0:T(4,128)S(1)}, f32[3,384]{1,0:T(4,128)S(1)}, u32[]{:S(2)}, u32[]{:S(2)}) collective-permute-start(f32[3,384]{1,0:T(4,128)S(1)} %get-tuple-element.159), channel_id=1, source_target_pairs={{7,0},{0,1},{1,2},{2,3},{3,4},{4,5},{5,6},{6,7},{15,8},{8,9},{9,10... | collective-permute-start | bytes 13832 | tf_op jit(solution)/shard_map/ppermute | solution.py:462
  265.6 4.6 %collective-permute-start.14 = (f32[3,128]{1,0:T(4,128)S(1)}, f32[3,128]{1,0:T(4,128)S(1)}, u32[]{:S(2)}, u32[]{:S(2)}) collective-permute-start(f32[3,128]{1,0:T(4,128)S(1)} %get-tuple-element.166), channel_id=1, source_target_pairs={{8,0},{16,8},{24,16},{0,24},{9,1},{17,9},{25,17},{1,25},{10,2},{18... | collective-permute-start | bytes 4616 | tf_op jit(solution)/shard_map/ppermute | solution.py:462
  268.9 4.5 %collective-permute-start.15 = (f32[3,128]{1,0:T(4,128)S(1)}, f32[3,128]{1,0:T(4,128)S(1)}, u32[]{:S(2)}, u32[]{:S(2)}) collective-permute-start(f32[3,128]{1,0:T(4,128)S(1)} %get-tuple-element.167), channel_id=1, source_target_pairs={{24,0},{0,8},{8,16},{16,24},{25,1},{1,9},{9,17},{17,25},{26,2},{2,... | collective-permute-start | bytes 4616 | tf_op jit(solution)/shard_map/ppermute | solution.py:462
  (15 other events, 78.0 us)

commit v2 on v1

--- a/solution.py
+++ b/solution.py
@@ -34,9 +34,18 @@
     return hi, (x - hi.astype(f32)).astype(bf16)
 
 
+def split_stack(x):
+    hi, lo = hi_lo(x)
+    return jnp.concatenate([hi, hi, lo], axis=0)
+
+
+def split_stack_small(x):
+    hi = x.astype(bf16).astype(f32)
+    return jnp.concatenate([hi, hi, x - hi], axis=0).astype(bf16)
+
+
 def dot_split(stack, x):
-    hi, lo = hi_lo(x)
-    return dot(stack, jnp.concatenate([hi, hi, lo], axis=0))
+    return dot(stack, split_stack(x))
 
 
 def silu(x):
@@ -135,15 +144,17 @@
 
 
 def radial_forward(w_in_t, mid_stack, basis):
-    pre1 = dot_high(w_in_t, basis)
+    pre1 = dot(w_in_t, split_stack_small(basis))
     pre2 = dot_split(mid_stack, silu(pre1))
     return pre1, pre2
 
 
 def radial_backward(out_back, mid_back, w_in, dw, pre1, pre2):
-    dpre2 = dot(out_back, jnp.concatenate([dw, dw], axis=0)) * silu_slope(pre2)
+    both = dot(out_back, dw)
+    half = both.shape[0] // 2
+    dpre2 = (both[:half] + both[half:]) * silu_slope(pre2)
     dpre1 = dot_split(mid_back, dpre2) * silu_slope(pre1)
-    return dot_high(w_in, dpre1)
+    return dot_split(w_in, dpre1)
 
 
 def layer_one_kernel(
@@ -175,15 +186,16 @@
             kind = jnp.where(valid, jnp.maximum(got[3:4], 0.0).astype(jnp.int32), -1)
             hot = one_hot_columns(L, kind)
             f_out[:, at] = dot(emb[...], jnp.concatenate([hot, hot], axis=0))
-            basis, ys = geometry(offset[0:1], offset[1:2], offset[2:3])
-            y_s[:, pl.ds(pl.multiple_of(c * G, G), G)] = jnp.concatenate(ys, axis=0)
-            pre1, pre2 = radial_forward(w_in_t[...], mid_stack[...], basis)
-            pre1_out[:, at] = pre1
-            pre2_out[:, at] = pre2
-            w_out[:, at] = dot_split(out_stack[...], silu(pre2))
             return carry
 
-        lax.fori_loop(0, slots * L // G, gather, 0)
+        lax.fori_loop(0, slots * L // G, gather, 0, unroll=2)
+        all_at = pl.ds(pl.multiple_of(b * (L * slots), L), L * slots)
+        basis, ys = geometry(offs[0:1, all_at], offs[1:2, all_at], offs[2:3, all_at])
+        y_s[...] = jnp.concatenate(ys, axis=0)
+        pre1, pre2 = radial_forward(w_in_t[...], mid_stack[...], basis)
+        pre1_out[:, all_at] = pre1
+        pre2_out[:, all_at] = pre2
+        w_out[:, all_at] = dot_split(out_stack[...], silu(pre2))
 
         def channels(c, carry):
             row = pl.multiple_of(c * CB, CB)
@@ -219,33 +231,67 @@
     border_feats[...] = dot(rounded[...], one_hot_columns(atoms, border[...])).astype(bf16)
 
 
+def radial_two_kernel(offs, w_in_t, mid_stack, h_out, pre1_out, pre2_out, y_out):
+    edges = offs.shape[1] // 3
+
+    def block(b, carry):
+        at = pl.ds(pl.multiple_of(b * edges, L), edges)
+        basis, ys = geometry(offs[0:1, at], offs[1:2, at], offs[2:3, at])
+        y_out[:, at] = jnp.concatenate(ys, axis=0)
+        pre1, pre2 = radial_forward(w_in_t[...], mid_stack[...], basis)
+        pre1_out[:, at] = pre1
+        pre2_out[:, at] = pre2
+        h_out[:, at] = split_stack(silu(pre2))
+        return carry
+
+    lax.fori_loop(0, 3, block, 0)
+
+
+def radial_two_back_kernel(dw, dy, pre1, pre2, offs, w_in, mid_back, out_back, doffs):
+    blocks, _, edges = dw.shape
+
+    def block(b, carry):
+        at = pl.ds(pl.multiple_of(b * edges, L), edges)
+        dbasis = radial_backward(
+            out_back[...], mid_back[...], w_in[...], dw[b], pre1[:, at], pre2[:, at]
+        )
+        dys = tuple(
+            jnp.sum(dy[k * 8 : (k + 1) * 8, at], axis=0, keepdims=True) for k in range(8)
+        )
+        _, pull = jax.vjp(geometry, offs[0:1, at], offs[1:2, at], offs[2:3, at])
+        dx, dyy, dz = pull((dbasis, dys))
+        doffs[:, at] = jnp.concatenate([dx, dyy, dz, jnp.zeros((5, edges), f32)], axis=0)
+        return carry
+
+    lax.fori_loop(0, blocks, block, 0)
+
+
 def layer_two_kernel(
-    rounded, prev, center, nxt, idx, idx_col, offs, occ, w_in, w_in_t, mid_stack, mid_back, out_stack, out_back,
-    mix, mix_t, out, out_t, coefs, lin, hid, hid_t, read,
-    energy, dlocal, dprev, dcenter, dnext, doffs,
-    table, dtable, dres, src, w_s, dw_s, pre1_s, pre2_s, y_s, dy_s, pooled, dpooled,
+    rounded, own_prev, side_prev, side, own_next, side_next, idx, idx_col, h_in, y_in, occ,
+    out_stack, mix, mix_t, out, out_t, coefs, lin, hid, hid_t, read,
+    energy, dlocal, down_prev, dside_prev, dside, down_next, dside_next, dy_out, dw_out,
+    table, dtable, dres, src, w_s, dw_s, pooled, dpooled, dw_sem,
 ):
     atoms = energy.shape[1]
     total = table.shape[1]
     slots = idx.shape[1] // atoms
     edges = slots * L
+    first, second, third = atoms, atoms + 3 * L, atoms + 6 * L
     dtable[...] = jnp.zeros_like(dtable)
     table[:, 0:atoms] = rounded[...]
-    table[:, atoms : atoms + 3 * L] = prev[...]
-    table[:, atoms + 3 * L : atoms + 6 * L] = center[...]
-    table[:, atoms + 6 * L : atoms + 9 * L] = nxt[...]
+    table[:, first : first + L] = own_prev[...]
+    table[:, first + L : second] = side_prev[...]
+    table[:, second : second + L] = jnp.zeros((9 * L, L), bf16)
+    table[:, second + L : third] = side[...]
+    table[:, third : third + L] = own_next[...]
+    table[:, third + L : third + 3 * L] = side_next[...]
 
     def block(b, carry):
         def gather(c, carry):
             at = pl.ds(pl.multiple_of(b * edges + c * G, G), G)
             to = pl.ds(pl.multiple_of(c * G, G), G)
             src[:, to] = dot(table[...], one_hot_columns(total, idx[:, at])).astype(bf16)
-            basis, ys = geometry(offs[0:1, at], offs[1:2, at], offs[2:3, at])
-            y_s[:, to] = jnp.concatenate(ys, axis=0)
-            pre1, pre2 = radial_forward(w_in_t[...], mid_stack[...], basis)
-            pre1_s[:, to] = pre1
-            pre2_s[:, to] = pre2
-            w_s[:, to] = dot_split(out_stack[...], silu(pre2))
+            w_s[:, to] = dot(out_stack[...], h_in[:, at])
             return carry
 
         lax.fori_loop(0, edges // G, gather, 0)
@@ -254,7 +300,8 @@
             at = slice(s * L, (s + 1) * L)
             f = [src[pl.ds(row + k * L, CB), at].astype(f32) for k in range(9)]
             w = [w_s[pl.ds(row + p * L, CB), at] for p in range(7)]
-            y = [y_s[k : k + 1, at] for k in range(8)]
+            far = pl.ds(pl.multiple_of(b * edges + s * L, L), L)
+            y = [y_in[k : k + 1, far] for k in range(8)]
             return f, w, y
 
         def forward(c, carry):
@@ -296,13 +343,15 @@
         dparts, dresidual = pull(occupied)
         for k in range(9):
             dpooled[k * L : (k + 1) * L, :] = dparts[k] / slots
-        dy_s[...] = jnp.zeros_like(dy_s)
+        mine = pl.ds(pl.multiple_of(b * edges, L), edges)
+        dy_out[:, mine] = jnp.zeros((64, edges), f32)
 
         def backward(c, carry):
             row = pl.multiple_of(c * CB, CB)
             g = [dpooled[pl.ds(row + k * L, CB), :] for k in range(9)]
             for s in range(slots):
                 at = slice(s * L, (s + 1) * L)
+                far = pl.ds(pl.multiple_of(b * edges + s * L, L), L)
                 f, w, y = load(row, s)
                 dw = [None] * 7
                 dw[0] = g[0] * f[0]
@@ -327,28 +376,15 @@
                     side = sv if k < 3 else sq
                     direct = w[4] if k < 3 else w[6]
                     dy = base * f[1 + k] + side * g[1 + k]
-                    dy_s[k * 8 : (k + 1) * 8, at] += dy[0:8] + dy[8:16]
+                    dy_out[k * 8 : (k + 1) * 8, far] += dy[0:8] + dy[8:16]
                     df = base * y[k] + direct * g[1 + k]
                     src[pl.ds(row + (1 + k) * L, CB), at] = df.astype(bf16)
             return carry
 
         lax.fori_loop(0, L // CB, backward, 0)
 
-        def edge_back(c, carry):
-            at = pl.ds(pl.multiple_of(b * edges + c * G, G), G)
-            to = pl.ds(pl.multiple_of(c * G, G), G)
-            dbasis = radial_backward(
-                out_back[...], mid_back[...], w_in[...], dw_s[:, to], pre1_s[:, to], pre2_s[:, to]
-            )
-            dys = tuple(
-                jnp.sum(dy_s[k * 8 : (k + 1) * 8, to], axis=0, keepdims=True) for k in range(8)
-            )
-            _, pull = jax.vjp(geometry, offs[0:1, at], offs[1:2, at], offs[2:3, at])
-            dx, dy, dz = pull((dbasis, dys))
-            doffs[:, at] = jnp.concatenate([dx, dy, dz, jnp.zeros((5, G), f32)], axis=0)
-            return carry
-
-        lax.fori_loop(0, edges // G, edge_back, 0)
+        keep = pltpu.make_async_copy(dw_s, dw_out.at[b], dw_sem)
+        keep.start()
 
         def scatter(t, carry):
             to = pl.ds(pl.multiple_of(t * G, G), G)
@@ -359,28 +395,34 @@
             return carry
 
         lax.fori_loop(0, total // G, scatter, 0)
+        keep.wait()
         dres[:, here] = dresidual
         return carry
 
     lax.fori_loop(0, atoms // L, block, 0)
     dlocal[...] = dtable[:, 0:atoms]
     dlocal[0:L, :] += dres[...] + lin[...] * occ[...]
-    dprev[...] = dtable[:, atoms : atoms + 3 * L].astype(bf16)
-    dcenter[...] = dtable[:, atoms + 3 * L : atoms + 6 * L]
-    dnext[...] = dtable[:, atoms + 6 * L : atoms + 9 * L].astype(bf16)
+    down_prev[...] = dtable[:, first : first + L].astype(bf16)
+    dside_prev[...] = dtable[:, first + L : second].astype(bf16)
+    dside[...] = dtable[:, second + L : third]
+    down_next[...] = dtable[:, third : third + L].astype(bf16)
+    dside_next[...] = dtable[:, third + L : third + 3 * L].astype(bf16)
 
 
 def layer_one_back_kernel(
-    dlocal, back, border_col, idx_col, offs, doffs_two, f_in, w_in_edges, pre1_in, pre2_in, pooled,
+    dlocal, back_a, back_b, back_c, back_d, border_col, idx_col, offs, doffs_two, f_in, w_in_edges, pre1_in, pre2_in, pooled,
     w_in, mid_back, out_back, mix, mix_t, outs, outs_t, coefs,
-    dpos, dw_s, y_s, dy_s, dh_s, dpooled,
+    dpos, dw_s, y_s, dy_s, dh_s, dpooled, d_s,
 ):
     atoms = dlocal.shape[1]
     total = dpos.shape[1]
     slots = offs.shape[1] // atoms
     edges = slots * L
     hot = one_hot_rows(border_col[...], 0, atoms)
-    back_hi, back_lo = hi_lo(back[...])
+    back = (back_a[...].astype(f32) + back_b[...].astype(f32)) + (
+        back_c[...].astype(f32) + back_d[...].astype(f32)
+    )
+    back_hi, back_lo = hi_lo(back)
     dh_s[...] = dlocal[...] + dot(back_hi, hot) + dot(back_lo, hot)
     dpos[...] = jnp.zeros_like(dpos)
 
@@ -399,13 +441,9 @@
         for k in range(9):
             dpooled[k * L : (k + 1) * L, :] = dparts[k] / slots
 
-        def harmonics(c, carry):
-            at = pl.ds(pl.multiple_of(b * edges + c * G, G), G)
-            _, ys = geometry(offs[0:1, at], offs[1:2, at], offs[2:3, at])
-            y_s[:, pl.ds(pl.multiple_of(c * G, G), G)] = jnp.concatenate(ys, axis=0)
-            return carry
-
-        lax.fori_loop(0, edges // G, harmonics, 0)
+        mine = pl.ds(pl.multiple_of(b * edges, L), edges)
+        _, ys = geometry(offs[0:1, mine], offs[1:2, mine], offs[2:3, mine])
+        y_s[...] = jnp.concatenate(ys, axis=0)
         dy_s[...] = jnp.zeros_like(dy_s)
 
         def backward(c, carry):
@@ -430,26 +468,29 @@
 
         lax.fori_loop(0, L // CB, backward, 0)
 
-        def edge_back(c, own):
-            at = pl.ds(pl.multiple_of(b * edges + c * G, G), G)
-            to = pl.ds(pl.multiple_of(c * G, G), G)
-            dbasis = radial_backward(
-                out_back[...], mid_back[...], w_in[...], dw_s[:, to], pre1_in[:, at], pre2_in[:, at]
-            )
-            dys = tuple(
-                jnp.sum(dy_s[k * 8 : (k + 1) * 8, to], axis=0, keepdims=True) for k in range(8)
-            )
-            _, pull = jax.vjp(geometry, offs[0:1, at], offs[1:2, at], offs[2:3, at])
-            dx, dy, dz = pull((dbasis, dys))
-            d = jnp.concatenate([dx, dy, dz, jnp.zeros((5, G), f32)], axis=0) + doffs_two[:, at]
-            hi = d.astype(bf16).astype(f32)
-            both = jnp.concatenate([hi, d - hi], axis=0).astype(bf16)
-            column = idx_col[pl.ds(pl.multiple_of(b * edges + c * G, G), G), :]
-            part = dot(both, one_hot_rows(column, 0, total))
-            dpos[...] += part[0:8] + part[8:16]
-            return own + d[:, 0:L] + d[:, L : 2 * L]
-
-        own = lax.fori_loop(0, edges // G, edge_back, jnp.zeros((8, L), f32))
+        dbasis = radial_backward(
+            out_back[...], mid_back[...], w_in[...], dw_s[...], pre1_in[:, mine], pre2_in[:, mine]
+        )
+        dys = tuple(
+            jnp.sum(dy_s[k * 8 : (k + 1) * 8, :], axis=0, keepdims=True) for k in range(8)
+        )
+        _, pull_again = jax.vjp(geometry, offs[0:1, mine], offs[1:2, mine], offs[2:3, mine])
+        dx, dy, dz = pull_again((dbasis, dys))
+        d = jnp.concatenate([dx, dy, dz, jnp.zeros((5, edges), f32)], axis=0) + doffs_two[:, mine]
+        hi = d.astype(bf16).astype(f32)
+        d_s[...] = jnp.concatenate([hi, d - hi], axis=0).astype(bf16)
+        own = d[:, 0:L]
+        for s in range(1, slots):
+            own = own + d[:, s * L : (s + 1) * L]
+
+        def scatter(t, carry):
+            to = pl.ds(pl.multiple_of(t * G, G), G)
+            column = idx_col[pl.ds(pl.multiple_of(b * edges, 8), edges), :]
+            part = dot(d_s[...], one_hot_rows(column, t * G, G))
+            dpos[:, to] += part[0:8] + part[8:16]
+            return carry
+
+        lax.fori_loop(0, total // G, scatter, 0)
         dpos[:, here] -= own
         return carry
 
@@ -472,11 +513,21 @@
     return jnp.concatenate([hi, lo, hi], axis=-1)
 
 
-def call(kernel, outs, scratch, *args):
+def call(kernel, outs, scratch, *args, flops=0, any_outs=()):
+    cost = None
+    if flops:
+        cost = pl.CostEstimate(flops=flops, bytes_accessed=16 * 1024 * 1024, transcendentals=0)
+    specs = [
+        pl.BlockSpec(memory_space=pl.ANY if i in any_outs else pltpu.VMEM)
+        for i in range(len(outs))
+    ]
     return pl.pallas_call(
         kernel,
         out_shape=[jax.ShapeDtypeStruct(s, d) for s, d in outs],
-        scratch_shapes=[pltpu.VMEM(s, d) for s, d in scratch],
+        out_specs=specs,
+        scratch_shapes=[pltpu.VMEM(s, d) for s, d in scratch]
+        + [pltpu.SemaphoreType.DMA(())] * len(any_outs),
+        cost_estimate=cost,
         compiler_params=params(),
     )(*args)
 
@@ -514,7 +565,7 @@
         return block + jnp.zeros((4, 1), f32).at[axis, 0].set(amount)
 
     triple = jnp.concatenate(
-        [shift(up[:, :count], 0, -1.0), edge_packet, shift(down[:, :count], 0, 1.0)], axis=1
+        [edge_packet, shift(up[:, :count], 0, -1.0), shift(down[:, :count], 0, 1.0)], axis=1
     )
     before = from_behind(jnp.concatenate([triple, leave[2]], axis=1), "gy", 1)
     after = from_behind(jnp.concatenate([triple, leave[3]], axis=1), "gy", -1)
@@ -540,21 +591,17 @@
     index = neighbours[0, 0]
     ghost = index - atoms
     which = ghost // count
-    moved = atoms + ((which % 3) * 3 + which // 3) * count + ghost % count
+    across = which // 3
+    across = jnp.where(across == 1, 0, jnp.where(across == 0, 1, 2))
+    moved = atoms + ((which % 3) * 3 + across) * count + ghost % count
     index = jnp.where(index >= atoms, moved, index)
     index = index.reshape(atoms // L, L, slots).transpose(0, 2, 1).reshape(1, edge_total)
 
     emb = jnp.pad(embedding, ((0, L - embedding.shape[0]), (0, 0))).T
     emb = jnp.concatenate(parts_of(emb), axis=1)
-    w_in_t = jnp.swapaxes(radial_in, 1, 2)
-    mid_t = k_stack(jnp.swapaxes(radial_mid, 1, 2))
-    mid = k_stack(radial_mid)
-    one_t, two_t = k_stack(radial_out_one.T), k_stack(radial_out_two.T)
-    one_b = jnp.concatenate(parts_of(radial_out_one), axis=1)
-    two_b = jnp.concatenate(parts_of(radial_out_two), axis=1)
-    mix_t, mix_k = k_stack(jnp.swapaxes(mix, 2, 3)), k_stack(mix)
-    outs_t, outs_k = k_stack(jnp.swapaxes(mix_out_one, 1, 2)), k_stack(mix_out_one)
-
+    mix_t = k_stack(jnp.swapaxes(mix[0], 1, 2))
+    outs_t = k_stack(jnp.swapaxes(mix_out_one, 1, 2))
+    one_coefs = product_one.T
     hidden = radial_in.shape[2]
     rounded, border_feats, idx, offs, f_e, w_e, pre1, pre2, pooled = call(
         layer_one_kernel,
@@ -564,55 +611,87 @@
             ((hidden, edge_total), f32), ((hidden, edge_total), f32), ((feats, atoms), f32),
         ],
         [((8, slots * L), f32)],
-        nodes, index, emb, w_in_t[0], mid_t[0], one_t, mix_k[0], mix_t[0], outs_k, outs_t,
-        product_one.T, border_rows[None],
-    )
+        nodes, index, emb, k_stack(radial_in[0].T), k_stack(radial_mid[0].T),
+        k_stack(radial_out_one.T), mix_t, mix_t, outs_t, outs_t, one_coefs, border_rows[None],
+    )
+    later = lax.optimization_barrier(
+        (border_feats, radial_in, radial_mid, radial_out_one, radial_out_two, mix, mix_out_one,
+         mix_out_two, product_two, read_lin, read_hidden, read_out)
+    )
+    (border_feats, radial_in, radial_mid, radial_out_one, radial_out_two, mix, mix_out_one,
+     mix_out_two, product_two, read_lin, read_hidden, read_out) = later
     left = from_behind(border_feats, "gx", 1)
     right = from_behind(border_feats, "gx", -1)
-    middle = jnp.concatenate([left, border_feats, right], axis=1)
-    prev = from_behind(middle, "gy", 1)
-    nxt = from_behind(middle, "gy", -1)
+    own_prev = from_behind(border_feats, "gy", 1)
+    own_next = from_behind(border_feats, "gy", -1)
+    side = jnp.concatenate([left, right], axis=1)
+    side_prev = from_behind(side, "gy", 1)
+    side_next = from_behind(side, "gy", -1)
     idx_col = idx.reshape(edge_total, 1)
 
-    energy, dlocal, dprev, dcenter, dnext, doffs = call(
+    h_two, pre1_two, pre2_two, y_two = call(
+        radial_two_kernel,
+        [
+            ((3 * hidden, edge_total), bf16), ((hidden, edge_total), f32),
+            ((hidden, edge_total), f32), ((8, edge_total), f32),
+        ],
+        [],
+        offs, k_stack(radial_in[1].T), k_stack(radial_mid[1].T), flops=10**10,
+    )
+
+    two = ((feats, 2 * count), bf16)
+    one = ((feats, count), bf16)
+    energy, dlocal, down_prev, dside_prev, dside, down_next, dside_next, dy_two, dw_two = call(
         layer_two_kernel,
         [
-            ((1, atoms), f32), ((feats, atoms), f32), ((feats, 3 * count), bf16),
-            ((feats, 3 * count), f32), ((feats, 3 * count), bf16), ((8, edge_total), f32),
+            ((1, atoms), f32), ((feats, atoms), f32), one, two, ((feats, 2 * count), f32), one, two,
+            ((64, edge_total), f32), ((atoms // L, 7 * channels, slots * L), bf16),
         ],
         [
             ((feats, total), bf16), ((feats, total), f32), ((channels, atoms), f32),
             ((feats, slots * L), bf16), ((7 * channels, slots * L), f32),
-            ((7 * channels, slots * L), bf16), ((hidden, slots * L), f32),
-            ((hidden, slots * L), f32), ((8, slots * L), f32), ((64, slots * L), f32),
-            ((feats, L), f32), ((feats, L), f32),
+            ((7 * channels, slots * L), bf16), ((feats, L), f32), ((feats, L), f32),
         ],
-        rounded, prev, middle, nxt, idx, idx_col, offs, occupied[None], radial_in[1], w_in_t[1],
-        mid_t[1], mid[1], two_t, two_b, mix_k[1], mix_t[1], k_stack(mix_out_two), k_stack(mix_out_two.T), product_two.T,
-        read_lin[:, None], k_stack(read_hidden), k_stack(read_hidden.T), read_out[:, None],
-    )
-    column = dcenter + from_behind(dprev, "gy", -1).astype(f32)
-    column = column + from_behind(dnext, "gy", 1).astype(f32)
-    back = column[:, count : 2 * count]
-    back = back + from_behind(column[:, :count].astype(bf16), "gx", -1).astype(f32)
-    back = back + from_behind(column[:, 2 * count :].astype(bf16), "gx", 1).astype(f32)
+        rounded, own_prev, side_prev, side, own_next, side_next, idx, idx_col, h_two, y_two,
+        occupied[None], k_stack(radial_out_two.T), k_stack(mix[1]),
+        k_stack(jnp.swapaxes(mix[1], 1, 2)), k_stack(mix_out_two), k_stack(mix_out_two.T),
+        product_two.T, read_lin[:, None], k_stack(read_hidden), k_stack(read_hidden.T),
+        read_out[:, None], flops=10**11, any_outs=(8,),
+    )
+    side_a = from_behind(dside_prev, "gy", -1)
+    side_b = from_behind(dside_next, "gy", 1)
+    side_a, side_b, down_prev, down_next = lax.optimization_barrier(
+        (side_a, side_b, down_prev, down_next)
+    )
+    back_a = from_behind(down_prev, "gy", -1)
+    back_b = from_behind(down_next, "gy", 1)
+    dside = (dside + side_a.astype(f32) + side_b.astype(f32)).astype(bf16)
+    back_c = from_behind(dside[:, :count], "gx", -1)
+    back_d = from_behind(dside[:, count:], "gx", 1)
+    (doffs,) = call(
+        radial_two_back_kernel, [((8, edge_total), f32)], [],
+        dw_two, dy_two, pre1_two, pre2_two, offs, k_stack(radial_in[1]), k_stack(radial_mid[1]),
+        jnp.concatenate(parts_of(radial_out_two), axis=0), flops=10**10,
+    )
 
     (dpos,) = call(
         layer_one_back_kernel,
         [((8, total), f32)],
         [
             ((3 * channels, slots * L), bf16), ((8, slots * L), f32), ((64, slots * L), f32),
-            ((feats, atoms), f32), ((feats, L), f32),
+            ((feats, atoms), f32), ((feats, L), f32), ((16, slots * L), bf16),
         ],
-        dlocal, back, border_rows[:, None], idx_col, offs, doffs, f_e, w_e, pre1, pre2, pooled,
-        radial_in[0], mid[0], one_b, mix_k[0], mix_t[0], outs_k, outs_t, product_one.T,
+        dlocal, back_a, back_b, back_c, back_d, border_rows[:, None], idx_col, offs, doffs, f_e, w_e,
+        pre1, pre2, pooled, k_stack(radial_in[0]), k_stack(radial_mid[0]),
+        jnp.concatenate(parts_of(radial_out_one), axis=0), k_stack(mix[0]), mix_t,
+        k_stack(mix_out_one), outs_t, one_coefs,
     )
     dpos = dpos[:3]
     column = dpos[:, atoms + 3 * count : atoms + 6 * count]
     column = column + from_behind(dpos[:, atoms : atoms + 3 * count], "gy", -1)
     column = column + from_behind(dpos[:, atoms + 6 * count :], "gy", 1)
-    back = column[:, count : 2 * count]
-    back = back + from_behind(column[:, :count], "gx", -1)
+    back = column[:, :count]
+    back = back + from_behind(column[:, count : 2 * count], "gx", -1)
     back = back + from_behind(column[:, 2 * count :], "gx", 1)
     hot = (border_rows[:, None] == jnp.arange(atoms)[None, :]).astype(f32)
     forces = -(dpos[:, :atoms] + jnp.dot(back, hot, precision=highest))

time: 275 us -> 228 us (0.83)
  waiting for transfers between devices: 67.1 us -> 30.5 us
  Pallas kernels: 146 us -> 132 us
  other arithmetic: 14.9 us -> 18.1 us
    ppermute x16 -> x20, waiting for transfers between devices: 67.1 us -> 30.5 us  [from_behind(): return lax.ppermute(block, axis, route)]
    pallas_call x3 -> x5, Pallas kernels: 146 us -> 132 us  [call(): pl.pallas_call(kernel, out_shape=[jax.ShapeDtypeStruct(s, d) for s, d in...]
    concatenate x10 -> x19, other arithmetic: 4.32 us -> 10.3 us  [k_stack(): return jnp.concatenate([hi, lo, hi], axis=-1)]
    squeeze x5 -> x0, local copies, waits for them, and re-layouts: 3.54 us -> none  [the longest x1 1.07 us: on_device(): mix_t[1]]
    concatenate x1 -> x5, local copies, waits for them, and re-layouts: 0.72 us -> 3.68 us  [k_stack(): return jnp.concatenate([hi, lo, hi], axis=-1)]
    unnamed x60 -> x69, local copies, waits for them, and re-layouts: 7.26 us -> 4.78 us
    ppermute x16 -> x20, starting transfers between devices: 25.3 us -> 27.3 us  [from_behind(): return lax.ppermute(block, axis, route)]
  transfers between devices with their start and end apart: 16 -> 20, of which waited for: 13 -> 9; matrix products, arithmetic and copies ran while one was open for 8% -> 12% of each run, Pallas kernels for 0% -> 6%
where the time goes in v2:
time: 228 us
  Pallas kernels  132 us (58%)
  waiting for transfers between devices  30.5 us (13%)
  starting transfers between devices  27.3 us (12%)
  other arithmetic  18.1 us (8%)
  local copies, waits for them, and re-layouts  18 us (8%)
    pallas_call x5, Pallas kernels, call(): pl.pallas_call(kernel, out_shape=[jax.ShapeDtypeStruct(s, d) for s, d in...  132 us
    ppermute x20, waiting for transfers between devices, from_behind(): return lax.ppermute(block, axis, route)  30.5 us
    ppermute x20, starting transfers between devices, from_behind(): return lax.ppermute(block, axis, route)  27.3 us
    concatenate x19, other arithmetic, k_stack(): return jnp.concatenate([hi, lo, hi], axis=-1)  10.3 us
    unnamed x69, local copies, waits for them, and re-layouts  4.78 us
  transfers between devices with their start and end apart: 20, of which 9 were waited for; matrix products, arithmetic and copies ran while one was open for 12% of the time, Pallas kernels for 6%

profile of v2, /device:TPU:0, one launch (start us, length us, event | category | flops | bytes accessed | tf_op | source)
XLA Modules:
  0.0 227.7 jit_solution(10856418241924721421)
XLA Ops:
  4.6 3.9 %collective-permute-start.1 = (f32[4,160]{1,0:T(4,128)S(1)}, f32[4,160]{1,0:T(4,128)S(1)}, u32[]{:S(2)}, u32[]{:S(2)}) collective-permute-start(f32[4,160]{1,0:T(4,128)S(1)} %get-tuple-element.222), channel_id=1, source_target_pairs={{8,0},{16,8},{24,16},{0,24},{9,1},{17,9},{25,17},{1,25},{10,2},{18... | collective-permute-start | bytes 7688 | tf_op jit(solution)/shard_map/ppermute | solution.py:503
  17.5 2.8 %collective-permute-start.3 = (f32[4,416]{1,0:T(4,128)S(1)}, f32[4,416]{1,0:T(4,128)S(1)}, u32[]{:S(2)}, u32[]{:S(2)}) collective-permute-start(f32[4,416]{1,0:T(4,128)S(1)} %get-tuple-element.217), channel_id=1, source_target_pairs={{1,0},{2,1},{3,2},{4,3},{5,4},{6,5},{7,6},{0,7},{9,8},{10,9},{11,1... | collective-permute-start | bytes 19976 | tf_op jit(solution)/shard_map/ppermute | solution.py:503
  21.7 3.4 %collective-permute-done.2 = f32[4,416]{1,0:T(4,128)S(1)} collective-permute-done((f32[4,416]{1,0:T(4,128)S(1)}, f32[4,416]{1,0:T(4,128)S(1)}, u32[]{:S(2)}, u32[]{:S(2)}) %collective-permute-start.2) | collective-permute-done | bytes 6688 | tf_op jit(solution)/shard_map/ppermute | solution.py:503
  26.3 21.0 %shard_map.203 = (bf16[1152,384]{1,0:T(8,128)(2,1)}, bf16[1152,128]{1,0:T(8,128)(2,1)}, s32[1,4608]{1,0:T(1,128)}, f32[8,4608]{1,0:T(8,128)}, f32[128,4608]{1,0:...) custom-call(f32[8,1536]{1,0:T(8,128)} %maximum_maximum_fusion.nodes, ...), custom_call_target="tpu_custom_call" | custom-call | tf_op jit(solution)/shard_map/pallas_call | solution.py:524
  47.7 1.7 collective-permute-start.5
  49.5 1.2 collective-permute-start.6
  50.7 3.5 %collective-permute-start.8 = (bf16[1152,128]{1,0:T(8,128)(2,1)}, bf16[1152,128]{1,0:T(8,128)(2,1)}, u32[]{:S(2)}, u32[]{:S(2)}) collective-permute-start(bf16[1152,128]{1,0:T(8,128)(2,1)} %get-tuple-element.122), channel_id=1, source_target_pairs={{1,0},{2,1},{3,2},{4,3},{5,4},{6,5},{7,6},{0,7},{9,8},{10,9},{11,1... | collective-permute-start | bytes 884744 | tf_op jit(solution)/shard_map/ppermute | solution.py:503
  61.8 4.5 %shard_map.204 = (bf16[192,4608]{1,0:T(8,128)(2,1)}, f32[64,4608]{1,0:T(8,128)}, f32[64,4608]{1,0:T(8,128)}, f32[8,4608]{1,0:T(8,128)}) custom-call(f32[8,4608]{1,0:T(8,128)} %get-tuple-element.124.offs, bf16[64,24]{1,0:T(8,128)(2,1)} %copy.80.w_in_t, bf16[64,192]{1,0:T(8,128)(2,1)} %copy.81.mid_stack), custom_call_target="tpu_custom_call" | custom-call | flops 10000000000 | bytes 16777216 | tf_op jit(solution)/shard_map/pallas_call | solution.py:524
  67.2 3.5 %collective-permute-start.9 = (bf16[1152,256]{1,0:T(8,128)(2,1)S(1)}, bf16[1152,256]{1,0:T(8,128)(2,1)}, u32[]{:S(2)}, u32[]{:S(2)}) collective-permute-start(bf16[1152,256]{1,0:T(8,128)(2,1)S(1)} %constant_dynamic-update-slice_fusion.side), channel_id=1, source_target_pairs={{1,0},{2,1},{3,2},{4,3},{5,4},{6,5},{7,6},{0,7},{9,8},{10,9},{11,1... | collective-permute-start | bytes 1769480 | tf_op jit(solution)/shard_map/ppermute | solution.py:503
  72.4 2.1 copy.86.idx_col
  78.0 3.8 %collective-permute-done.7.side_prev = bf16[1152,256]{1,0:T(8,128)(2,1)S(1)} collective-permute-done((bf16[1152,256]{1,0:T(8,128)(2,1)S(1)}, bf16[1152,256]{1,0:T(8,128)(2,1)S(1)}, u32[]{:S(2)}, u32[]{:S(2)}) %collective-permute-start.7) | collective-permute-done | bytes 589856 | tf_op jit(solution)/shard_map/ppermute | solution.py:503
  82.7 72.3 %shard_map.205 = (f32[1,384]{1,0:T(1,128)}, f32[1152,384]{1,0:T(8,128)}, bf16[1152,128]{1,0:T(8,128)(2,1)}, bf16[1152,256]{1,0:T(8,128)(2,1)}, f32[1152,256]{1,0...) custom-call(bf16[1152,384]{1,0:T(8,128)(2,1)} %get-tuple-element.120, ...), custom_call_target="tpu_custom_call" | custom-call | flops 99999997952 | bytes 16777216 | tf_op jit(solution)/shard_map/pallas_call | solution.py:524
  157.8 11.1 %collective-permute-done.10 = bf16[1152,256]{1,0:T(8,128)(2,1)S(1)} collective-permute-done((bf16[1152,256]{1,0:T(8,128)(2,1)}, bf16[1152,256]{1,0:T(8,128)(2,1)S(1)}, u32[]{:S(2)}, u32[]{:S(2)}) %collective-permute-start.10) | collective-permute-done | bytes 589856 | tf_op jit(solution)/shard_map/ppermute | solution.py:503
  169.2 1.8 collective-permute-start.14
  171.3 3.1 %collective-permute-start.12 = (bf16[1152,128]{1,0:T(8,128)(2,1)S(1)}, bf16[1152,128]{1,0:T(8,128)(2,1)S(1)}, u32[]{:S(2)}, u32[]{:S(2)}) collective-permute-start(bf16[1152,128]{1,0:T(8,128)(2,1)S(1)} %copy-done.29), channel_id=1, source_target_pairs={{1,0},{2,1},{3,2},{4,3},{5,4},{6,5},{7,6},{0,7},{9,8},{10,9},{11,1... | collective-permute-start | bytes 884744 | tf_op jit(solution)/shard_map/ppermute | solution.py:503
  174.5 8.7 %shard_map.206.doffs_two = f32[8,4608]{1,0:T(8,128)} custom-call(bf16[3,896,1536]{2,1,0:T(8,128)(2,1)} %get-tuple-element.147.dw, f32[64,4608]{1,0:T(8,128)} %get-tuple-element.148.dy, f32[64,4608]{1,0:T(8,128)} %get-tuple-element.149.pre1, f32[64,4608]{1,0:T(8,128)} %get-tuple-element.150.pre2, f32[8,4608]{1,0:T(8,128)} %get-tuple-element.124.offs, ...), custom_call_target="tpu_custom_call" | custom-call | flops 10000000000 | bytes 16777216 | tf_op jit(solution)/shard_map/pallas_call | solution.py:524
  183.1 1.6 collective-permute-done.15.back_d
  185.6 25.0 %shard_map.207 = f32[8,1536]{1,0:T(8,128)} custom-call(f32[1152,384]{1,0:T(8,128)} %get-tuple-element.137.dlocal, bf16[1152,128]{1,0:T(8,128)(2,1)} %copy-done.7, bf16[1152,128]{1,0:T(8,128)(2,1)} %copy-done.8, bf16[1152,128]{1,0:T(8,128)(2,1)} %copy-done.5, bf16[1152,128]{1,0:T(8,128)(2,1)} %copy-done.6, s32[128,1]{1,0:T(8,128)} %copy.91.border_col, ...), custom_call_target="tpu_custom_call" | custom-call | tf_op jit(solution)/shard_map/pallas_call | solution.py:524
  211.3 2.1 collective-permute-start.16
  213.4 1.3 collective-permute-done.16
  214.8 3.5 %collective-permute-done.17 = f32[3,384]{1,0:T(4,128)S(1)} collective-permute-done((f32[3,384]{1,0:T(4,128)S(1)}, f32[3,384]{1,0:T(4,128)S(1)}, u32[]{:S(2)}, u32[]{:S(2)}) %collective-permute-start.17) | collective-permute-done | bytes 4640 | tf_op jit(solution)/shard_map/ppermute | solution.py:503
  219.0 2.6 %collective-permute-start.18 = (f32[3,128]{1,0:T(4,128)S(1)}, f32[3,128]{1,0:T(4,128)S(1)}, u32[]{:S(2)}, u32[]{:S(2)}) collective-permute-start(f32[3,128]{1,0:T(4,128)S(1)} %get-tuple-element.214), channel_id=1, source_target_pairs={{8,0},{16,8},{24,16},{0,24},{9,1},{17,9},{25,17},{1,25},{10,2},{18... | collective-permute-start | bytes 4616 | tf_op jit(solution)/shard_map/ppermute | solution.py:503
  221.6 1.3 collective-permute-done.18
  223.0 3.2 %collective-permute-done.19 = f32[3,128]{1,0:T(4,128)S(1)} collective-permute-done((f32[3,128]{1,0:T(4,128)S(1)}, f32[3,128]{1,0:T(4,128)S(1)}, u32[]{:S(2)}, u32[]{:S(2)}) %collective-permute-start.19) | collective-permute-done | bytes 1568 | tf_op jit(solution)/shard_map/ppermute | solution.py:503
  (193 shorter events, 37.3 us)
Async XLA Ops:
  4.6 12.7 %collective-permute-start.1 = (f32[4,160]{1,0:T(4,128)S(1)}, f32[4,160]{1,0:T(4,128)S(1)}, u32[]{:S(2)}, u32[]{:S(2)}) collective-permute-start(f32[4,160]{1,0:T(4,128)S(1)} %get-tuple-element.222), channel_id=1, source_target_pairs={{8,0},{16,8},{24,16},{0,24},{9,1},{17,9},{25,17},{1,25},{10,2},{18... | collective-permute-start | bytes 7688 | tf_op jit(solution)/shard_map/ppermute | solution.py:503
  8.5 8.8 %collective-permute-start = (f32[4,160]{1,0:T(4,128)S(1)}, f32[4,160]{1,0:T(4,128)S(1)}, u32[]{:S(2)}, u32[]{:S(2)}) collective-permute-start(f32[4,160]{1,0:T(4,128)S(1)} %get-tuple-element.221), channel_id=1, source_target_pairs={{24,0},{0,8},{8,16},{16,24},{25,1},{1,9},{9,17},{17,25},{26,2},{2,... | collective-permute-start | bytes 7688 | tf_op jit(solution)/shard_map/ppermute | solution.py:503
  14.4 32.9 %copy-start.13 = (f32[128,16]{0,1:T(8,128)S(1)}, f32[128,16]{0,1:T(8,128)}, u32[]{:S(2)}) copy-start(f32[128,16]{0,1:T(8,128)} %param.54) | copy-start | bytes 24580
  14.4 32.9 %copy-start.9 = (f32[128,128]{1,0:T(8,128)S(1)}, f32[128,128]{1,0:T(8,128)}, u32[]{:S(2)}) copy-start(f32[128,128]{1,0:T(8,128)} %param.50) | copy-start | bytes 196612
  15.1 32.4 %copy-start = (f32[2,3,128,128]{3,2,1,0:T(8,128)S(1)}, f32[2,3,128,128]{3,2,1,0:T(8,128)}, u32[]{:S(2)}) copy-start(f32[2,3,128,128]{3,2,1,0:T(8,128)} %param.48) | copy-start | bytes 1179652
  17.5 4.1 %collective-permute-start.3 = (f32[4,416]{1,0:T(4,128)S(1)}, f32[4,416]{1,0:T(4,128)S(1)}, u32[]{:S(2)}, u32[]{:S(2)}) collective-permute-start(f32[4,416]{1,0:T(4,128)S(1)} %get-tuple-element.217), channel_id=1, source_target_pairs={{1,0},{2,1},{3,2},{4,3},{5,4},{6,5},{7,6},{0,7},{9,8},{10,9},{11,1... | collective-permute-start | bytes 19976 | tf_op jit(solution)/shard_map/ppermute | solution.py:503
  20.3 4.9 %collective-permute-start.2 = (f32[4,416]{1,0:T(4,128)S(1)}, f32[4,416]{1,0:T(4,128)S(1)}, u32[]{:S(2)}, u32[]{:S(2)}) collective-permute-start(f32[4,416]{1,0:T(4,128)S(1)} %get-tuple-element.216), channel_id=1, source_target_pairs={{7,0},{0,1},{1,2},{2,3},{3,4},{4,5},{5,6},{6,7},{15,8},{8,9},{9,10... | collective-permute-start | bytes 19976 | tf_op jit(solution)/shard_map/ppermute | solution.py:503
  47.7 19.3 %collective-permute-start.5 = (bf16[1152,128]{1,0:T(8,128)(2,1)}, bf16[1152,128]{1,0:T(8,128)(2,1)S(1)}, u32[]{:S(2)}, u32[]{:S(2)}) collective-permute-start(bf16[1152,128]{1,0:T(8,128)(2,1)} %get-tuple-element.122), channel_id=1, source_target_pairs={{24,0},{0,8},{8,16},{16,24},{25,1},{1,9},{9,17},{17,25},{26,2},{2,... | collective-permute-start | bytes 884744 | tf_op jit(solution)/shard_map/ppermute | solution.py:503
  49.5 17.6 %collective-permute-start.6 = (bf16[1152,128]{1,0:T(8,128)(2,1)}, bf16[1152,128]{1,0:T(8,128)(2,1)S(1)}, u32[]{:S(2)}, u32[]{:S(2)}) collective-permute-start(bf16[1152,128]{1,0:T(8,128)(2,1)} %get-tuple-element.122), channel_id=1, source_target_pairs={{8,0},{16,8},{24,16},{0,24},{9,1},{17,9},{25,17},{1,25},{10,2},{18... | collective-permute-start | bytes 884744 | tf_op jit(solution)/shard_map/ppermute | solution.py:503
  50.7 27.3 %collective-permute-start.4 = (bf16[1152,128]{1,0:T(8,128)(2,1)}, bf16[1152,128]{1,0:T(8,128)(2,1)}, u32[]{:S(2)}, u32[]{:S(2)}) collective-permute-start(bf16[1152,128]{1,0:T(8,128)(2,1)} %get-tuple-element.122), channel_id=1, source_target_pairs={{7,0},{0,1},{1,2},{2,3},{3,4},{4,5},{5,6},{6,7},{15,8},{8,9},{9,10... | collective-permute-start | bytes 884744 | tf_op jit(solution)/shard_map/ppermute | solution.py:503
  50.7 27.3 %collective-permute-start.8 = (bf16[1152,128]{1,0:T(8,128)(2,1)}, bf16[1152,128]{1,0:T(8,128)(2,1)}, u32[]{:S(2)}, u32[]{:S(2)}) collective-permute-start(bf16[1152,128]{1,0:T(8,128)(2,1)} %get-tuple-element.122), channel_id=1, source_target_pairs={{1,0},{2,1},{3,2},{4,3},{5,4},{6,5},{7,6},{0,7},{9,8},{10,9},{11,1... | collective-permute-start | bytes 884744 | tf_op jit(solution)/shard_map/ppermute | solution.py:503
  67.2 14.6 %collective-permute-start.7 = (bf16[1152,256]{1,0:T(8,128)(2,1)S(1)}, bf16[1152,256]{1,0:T(8,128)(2,1)S(1)}, u32[]{:S(2)}, u32[]{:S(2)}) collective-permute-start(bf16[1152,256]{1,0:T(8,128)(2,1)S(1)} %constant_dynamic-update-slice_fusion.side), channel_id=1, source_target_pairs={{7,0},{0,1},{1,2},{2,3},{3,4},{4,5},{5,6},{6,7},{15,8},{8,9},{9,10... | collective-permute-start | bytes 1769480 | tf_op jit(solution)/shard_map/ppermute | solution.py:503
  67.2 14.6 %collective-permute-start.9 = (bf16[1152,256]{1,0:T(8,128)(2,1)S(1)}, bf16[1152,256]{1,0:T(8,128)(2,1)}, u32[]{:S(2)}, u32[]{:S(2)}) collective-permute-start(bf16[1152,256]{1,0:T(8,128)(2,1)S(1)} %constant_dynamic-update-slice_fusion.side), channel_id=1, source_target_pairs={{1,0},{2,1},{3,2},{4,3},{5,4},{6,5},{7,6},{0,7},{9,8},{10,9},{11,1... | collective-permute-start | bytes 1769480 | tf_op jit(solution)/shard_map/ppermute | solution.py:503
  155.0 13.9 %collective-permute-start.10 = (bf16[1152,256]{1,0:T(8,128)(2,1)}, bf16[1152,256]{1,0:T(8,128)(2,1)S(1)}, u32[]{:S(2)}, u32[]{:S(2)}) collective-permute-start(bf16[1152,256]{1,0:T(8,128)(2,1)} %get-tuple-element.138), channel_id=1, source_target_pairs={{1,0},{2,1},{3,2},{4,3},{5,4},{6,5},{7,6},{0,7},{9,8},{10,9},{11,1... | collective-permute-start | bytes 1769480 | tf_op jit(solution)/shard_map/ppermute | solution.py:503
  155.1 13.9 %collective-permute-start.11 = (bf16[1152,256]{1,0:T(8,128)(2,1)}, bf16[1152,256]{1,0:T(8,128)(2,1)S(1)}, u32[]{:S(2)}, u32[]{:S(2)}) collective-permute-start(bf16[1152,256]{1,0:T(8,128)(2,1)} %get-tuple-element.139), channel_id=1, source_target_pairs={{7,0},{0,1},{1,2},{2,3},{3,4},{4,5},{5,6},{6,7},{15,8},{8,9},{9,10... | collective-permute-start | bytes 1769480 | tf_op jit(solution)/shard_map/ppermute | solution.py:503
  169.2 13.9 %collective-permute-start.14 = (bf16[1152,128]{1,0:T(8,128)(2,1)S(1)}, bf16[1152,128]{1,0:T(8,128)(2,1)S(1)}, u32[]{:S(2)}, u32[]{:S(2)}) collective-permute-start(bf16[1152,128]{1,0:T(8,128)(2,1)S(1)} %get-tuple-element.165), channel_id=1, source_target_pairs={{8,0},{16,8},{24,16},{0,24},{9,1},{17,9},{25,17},{1,25},{10,2},{18... | collective-permute-start | bytes 884744 | tf_op jit(solution)/shard_map/ppermute | solution.py:503
  171.0 13.7 %collective-permute-start.15 = (bf16[1152,128]{1,0:T(8,128)(2,1)S(1)}, bf16[1152,128]{1,0:T(8,128)(2,1)S(1)}, u32[]{:S(2)}, u32[]{:S(2)}) collective-permute-start(bf16[1152,128]{1,0:T(8,128)(2,1)S(1)} %get-tuple-element.164), channel_id=1, source_target_pairs={{24,0},{0,8},{8,16},{16,24},{25,1},{1,9},{9,17},{17,25},{26,2},{2,... | collective-permute-start | bytes 884744 | tf_op jit(solution)/shard_map/ppermute | solution.py:503
  171.3 13.4 %collective-permute-start.12 = (bf16[1152,128]{1,0:T(8,128)(2,1)S(1)}, bf16[1152,128]{1,0:T(8,128)(2,1)S(1)}, u32[]{:S(2)}, u32[]{:S(2)}) collective-permute-start(bf16[1152,128]{1,0:T(8,128)(2,1)S(1)} %copy-done.29), channel_id=1, source_target_pairs={{1,0},{2,1},{3,2},{4,3},{5,4},{6,5},{7,6},{0,7},{9,8},{10,9},{11,1... | collective-permute-start | bytes 884744 | tf_op jit(solution)/shard_map/ppermute | solution.py:503
  174.5 10.2 %collective-permute-start.13 = (bf16[1152,128]{1,0:T(8,128)(2,1)S(1)}, bf16[1152,128]{1,0:T(8,128)(2,1)S(1)}, u32[]{:S(2)}, u32[]{:S(2)}) collective-permute-start(bf16[1152,128]{1,0:T(8,128)(2,1)S(1)} %copy-done.28), channel_id=1, source_target_pairs={{7,0},{0,1},{1,2},{2,3},{3,4},{4,5},{5,6},{6,7},{15,8},{8,9},{9,10... | collective-permute-start | bytes 884744 | tf_op jit(solution)/shard_map/ppermute | solution.py:503
  185.6 40.5 %copy-start.18 = (s32[1,1,128]{2,1,0:T(1,128)S(1)}, s32[1,1,128]{2,1,0:T(1,128)}, u32[]{:S(2)}) copy-start(s32[1,1,128]{2,1,0:T(1,128)} %param.41) | copy-start | bytes 1540
  211.3 3.5 %collective-permute-start.16 = (f32[3,384]{1,0:T(4,128)S(1)}, f32[3,384]{1,0:T(4,128)S(1)}, u32[]{:S(2)}, u32[]{:S(2)}) collective-permute-start(f32[3,384]{1,0:T(4,128)S(1)} %get-tuple-element.198), channel_id=1, source_target_pairs={{1,0},{2,1},{3,2},{4,3},{5,4},{6,5},{7,6},{0,7},{9,8},{10,9},{11,1... | collective-permute-start | bytes 13832 | tf_op jit(solution)/shard_map/ppermute | solution.py:503
  213.4 4.9 %collective-permute-start.17 = (f32[3,384]{1,0:T(4,128)S(1)}, f32[3,384]{1,0:T(4,128)S(1)}, u32[]{:S(2)}, u32[]{:S(2)}) collective-permute-start(f32[3,384]{1,0:T(4,128)S(1)} %get-tuple-element.199), channel_id=1, source_target_pairs={{7,0},{0,1},{1,2},{2,3},{3,4},{4,5},{5,6},{6,7},{15,8},{8,9},{9,10... | collective-permute-start | bytes 13832 | tf_op jit(solution)/shard_map/ppermute | solution.py:503
  219.0 3.9 %collective-permute-start.18 = (f32[3,128]{1,0:T(4,128)S(1)}, f32[3,128]{1,0:T(4,128)S(1)}, u32[]{:S(2)}, u32[]{:S(2)}) collective-permute-start(f32[3,128]{1,0:T(4,128)S(1)} %get-tuple-element.214), channel_id=1, source_target_pairs={{8,0},{16,8},{24,16},{0,24},{9,1},{17,9},{25,17},{1,25},{10,2},{18... | collective-permute-start | bytes 4616 | tf_op jit(solution)/shard_map/ppermute | solution.py:503
  221.6 4.5 %collective-permute-start.19 = (f32[3,128]{1,0:T(4,128)S(1)}, f32[3,128]{1,0:T(4,128)S(1)}, u32[]{:S(2)}, u32[]{:S(2)}) collective-permute-start(f32[3,128]{1,0:T(4,128)S(1)} %get-tuple-element.215), channel_id=1, source_target_pairs={{24,0},{0,8},{8,16},{16,24},{25,1},{1,9},{9,17},{17,25},{26,2},{2,... | collective-permute-start | bytes 4616 | tf_op jit(solution)/shard_map/ppermute | solution.py:503
  (27 other events, 132.5 us)

commit v3 on v2

v3 whole, which is shorter than its diff:
```python
import functools
import math

import jax
import jax.numpy as jnp
from jax import lax
from jax.experimental import pallas as pl
from jax.experimental.pallas import tpu as pltpu
from jax.sharding import PartitionSpec as P

f32 = jnp.float32
bf16 = jnp.bfloat16
CUT = 5.0
L = 128
G = 256
CB = 16
VMEM_LIMIT = 56 * 1024 * 1024


MESH = pl.DeviceIdType.MESH
AROUND = [(a - 1, b - 1) for a in range(3) for b in range(3) if (a, b) != (1, 1)]
ORDER = sorted(range(8), key=lambda q: -abs(AROUND[q][1]))


def cell(grid, da, db):
    x, y = lax.axis_index("gx"), lax.axis_index("gy")
    return (lax.rem(x + da + grid[0], grid[0]), lax.rem(y + db + grid[1], grid[1]))


def greet(grid):
    barrier = pltpu.get_barrier_semaphore()
    for da, db in AROUND:
        pl.semaphore_signal(barrier, inc=1, device_id=cell(grid, da, db), device_id_type=MESH)
    pl.semaphore_wait(barrier, 8)


def send_around(grid, sign, source, target, sends, recvs):
    copies = []
    for q in ORDER:
        da, db = AROUND[q]
        copy = pltpu.make_async_remote_copy(
            src_ref=source(q),
            dst_ref=target.at[q],
            send_sem=sends.at[q],
            recv_sem=recvs.at[q],
            device_id=cell(grid, sign * da, sign * db),
            device_id_type=MESH,
        )
        copy.start()
        copies.append(copy)
    return copies


def three_parts(x):
    hi = x.astype(bf16).astype(f32)
    mid = (x - hi).astype(bf16).astype(f32)
    return jnp.concatenate([hi, mid, x - hi - mid, jnp.zeros_like(x)], axis=0).astype(bf16)


def exact_pick(x, hot):
    got = dot(three_parts(x), hot)
    return got[0:8] + got[8:16] + got[16:24]


def dot(a, b):
    return jnp.dot(a, b, preferred_element_type=f32)


def hi_lo(x):
    hi = x.astype(bf16)
    return hi, (x - hi.astype(f32)).astype(bf16)


def split_stack(x):
    hi, lo = hi_lo(x)
    return jnp.concatenate([hi, hi, lo], axis=0)


def split_stack_small(x):
    hi = x.astype(bf16).astype(f32)
    return jnp.concatenate([hi, hi, x - hi], axis=0).astype(bf16)


def rows_stack(w):
    if w.shape[0] % 16:
        hi = w.astype(bf16).astype(f32)
        return jnp.concatenate([hi, w - hi, hi], axis=0).astype(bf16)
    hi, lo = hi_lo(w)
    return jnp.concatenate([hi, lo, hi], axis=0)


def lanes_stack(w):
    hi, lo = hi_lo(w)
    return jnp.concatenate([hi, lo, hi], axis=1)


def dot_rows(stack, x_stack):
    return lax.dot_general(
        stack, x_stack, (((0,), (0,)), ((), ())), preferred_element_type=f32
    )


def dot_back(w, x):
    w_hi, w_lo = hi_lo(w)
    x_hi, x_lo = hi_lo(x)
    return dot(w_hi, x_hi) + dot(w_lo, x_hi) + dot(w_hi, x_lo)


def column_of(row):
    size = row.shape[1]
    down = lax.broadcasted_iota(jnp.int32, (size, size), 0)
    along = lax.broadcasted_iota(jnp.int32, (size, size), 1)
    return jnp.sum(jnp.where(down == along, row, 0.0), axis=1, keepdims=True)


def row_of(column):
    size = column.shape[0]
    down = lax.broadcasted_iota(jnp.int32, (size, size), 0)
    along = lax.broadcasted_iota(jnp.int32, (size, size), 1)
    return jnp.sum(jnp.where(down == along, column, 0.0), axis=0, keepdims=True)


def silu(x):
    return x * jax.nn.sigmoid(x)


def silu_slope(x):
    sig = jax.nn.sigmoid(x)
    return sig * (1.0 + x * (1.0 - sig))


def geometry(ox, oy, oz):
    squared = ox * ox + oy * oy + oz * oz + 1.0
    distance = jnp.sqrt(squared)
    inverse = 1.0 / distance
    ux, uy, uz = ox * inverse, oy * inverse, oz * inverse
    t = distance / CUT
    sixth = t * t * t * t * t * t
    envelope = 1.0 - 28.0 * sixth + 48.0 * sixth * t - 21.0 * sixth * t * t
    orders = (lax.broadcasted_iota(jnp.int32, (8, ox.shape[1]), 0) + 1).astype(f32)
    wave = jnp.sin(orders * (math.pi / CUT) * jnp.broadcast_to(distance, orders.shape))
    scale = math.sqrt(2.0 / CUT) * envelope * inverse
    basis = wave * jnp.broadcast_to(scale, orders.shape)
    r3, r5, r15 = math.sqrt(3.0), math.sqrt(5.0), math.sqrt(15.0)
    harmonics = (
        r3 * ux,
        r3 * uy,
        r3 * uz,
        r15 * ux * uy,
        r15 * uy * uz,
        0.5 * r5 * (2.0 * uz * uz - ux * ux - uy * uy),
        r15 * ux * uz,
        0.5 * r15 * (ux * ux - uy * uy),
    )
    return basis, harmonics


def one_hot_columns(rows, index_row):
    place = lax.broadcasted_iota(jnp.int32, (rows, index_row.shape[1]), 0)
    return jnp.where(place == index_row, 1.0, 0.0).astype(bf16)


def one_hot_rows(index_column, base, columns):
    place = lax.broadcasted_iota(jnp.int32, (index_column.shape[0], columns), 1) + base
    return jnp.where(place == index_column, 1.0, 0.0).astype(bf16)


@jax.custom_vjp
def mixed(w, x):
    return dot_rows(w[0], split_stack(x))


def mixed_fwd(w, x):
    return mixed(w, x), w


def mixed_bwd(w, g):
    if w[1].shape[1] % L:
        return None, dot_back(w[1], g)
    return None, dot(w[1], split_stack(g))


mixed.defvjp(mixed_fwd, mixed_bwd)


def both_ways(w):
    return rows_stack(w), lanes_stack(w)


def mix_orders(mats, parts):
    scalar = mixed(mats[0], parts[0])
    vector = mixed(mats[1], jnp.concatenate(parts[1:4], axis=1))
    tensor = mixed(mats[2], jnp.concatenate(parts[4:9], axis=1))
    return scalar, [vector[:, i * L : (i + 1) * L] for i in range(3)], [
        tensor[:, i * L : (i + 1) * L] for i in range(5)
    ]


def product_scalar(coefs, s, v, q):
    total = s + coefs[0] * s * s
    total = total + coefs[1] * (v[0] * v[0] + v[1] * v[1] + v[2] * v[2])
    return total + coefs[2] * (
        q[0] * q[0] + q[1] * q[1] + q[2] * q[2] + q[3] * q[3] + q[4] * q[4]
    )


def node_one(parts, mats, outs, coefs):
    s, v, q = mix_orders(mats, parts)
    b0 = product_scalar(coefs, s, v, q)
    gate1 = 1.0 + coefs[3] * s
    gate2 = 1.0 + coefs[4] * s
    s, v, q = mix_orders(outs, [b0] + [x * gate1 for x in v] + [x * gate2 for x in q])
    return [s] + v + q


def node_two(parts, residual, mats, out, coefs, hid, read):
    s, v, q = mix_orders(mats, parts)
    scalars = mixed(out, product_scalar(coefs, s, v, q)) + residual
    hidden = silu(mixed(hid, scalars))
    return jnp.sum(read * hidden, axis=0, keepdims=True)


def radial_forward(w_in, w_mid, basis):
    pre1 = dot_rows(rows_stack(w_in), split_stack_small(basis))
    pre2 = dot_rows(rows_stack(w_mid), split_stack(silu(pre1)))
    return pre1, pre2


def radial_backward(w_out, w_mid, w_in, dw, pre1, pre2):
    both = dot(jnp.concatenate(hi_lo(w_out), axis=0), dw)
    half = both.shape[0] // 2
    dpre2 = (both[:half] + both[half:]) * silu_slope(pre2)
    dpre1 = dot_back(w_mid, dpre2) * silu_slope(pre1)
    return dot_back(w_in, dpre1)


def layer_one_kernel(
    nodes, idx, emb, w_in, w_mid, w_out, mix, out_mix, coefs, border,
    rounded, border_feats, idx_out, offs, f_out, w_edges, pre1_out, pre2_out, pooled, y_s, emb_s,
):
    atoms = rounded.shape[1]
    total = nodes.shape[1]
    slots = idx.shape[1] // atoms
    stack = three_parts(nodes[...])
    elements = emb_s.shape[0]
    emb_s[...] = jnp.zeros_like(emb_s)
    emb_s[0 : emb.shape[0], :] = emb[...]
    emb_stack = jnp.concatenate(hi_lo(emb_s[...]), axis=0)
    out_stack = rows_stack(w_out[...])
    mats = [both_ways(mix[0, k]) for k in range(3)]
    outs = [both_ways(out_mix[k]) for k in range(3)]
    cs = [column_of(coefs[k : k + 1, :]) for k in range(5)]

    def block(b, carry):
        own = nodes[:, pl.ds(pl.multiple_of(b * L, L), L)]
        own2 = jnp.concatenate([own, own], axis=1)

        def gather(c, carry):
            at = pl.ds(pl.multiple_of(b * (L * slots) + c * G, G), G)
            index = idx[:, at]
            got = dot(stack, one_hot_columns(total, index))
            got = got[0:8] + got[8:16] + got[16:24]
            valid = (index >= 0) & (got[4:5] * own2[4:5] > 0.5)
            idx_out[:, at] = jnp.where(valid, index, -1)
            offset = got - own2
            offs[:, at] = offset
            kind = jnp.where(valid, jnp.maximum(got[3:4], 0.0).astype(jnp.int32), -1)
            hot = one_hot_columns(elements, kind)
            f_out[:, at] = dot_rows(emb_stack, jnp.concatenate([hot, hot], axis=0))
            return carry

        lax.fori_loop(0, slots * L // G, gather, 0, unroll=2)
        all_at = pl.ds(pl.multiple_of(b * (L * slots), L), L * slots)
        basis, ys = geometry(offs[0:1, all_at], offs[1:2, all_at], offs[2:3, all_at])
        y_s[...] = jnp.concatenate(ys, axis=0)
        pre1, pre2 = radial_forward(w_in[0], w_mid[0], basis)
        pre1_out[:, all_at] = pre1
        pre2_out[:, all_at] = pre2
        w_edges[:, all_at] = dot_rows(out_stack, split_stack(silu(pre2)))

        def channels(c, carry):
            row = pl.multiple_of(c * CB, CB)
            acc = [jnp.zeros((CB, L), f32)] * 9
            for s in range(slots):
                at = pl.ds(pl.multiple_of(b * (L * slots) + s * L, L), L)
                f = f_out[pl.ds(row, CB), at]
                w = [w_edges[pl.ds(row + p * L, CB), at] * f for p in range(3)]
                acc[0] = acc[0] + w[0]
                for k in range(8):
                    y = y_s[k : k + 1, s * L : (s + 1) * L]
                    acc[1 + k] = acc[1 + k] + (w[1] if k < 3 else w[2]) * y
            for k in range(9):
                pooled[pl.ds(row + k * L, CB), pl.ds(pl.multiple_of(b * L, L), L)] = acc[k] / slots
            return carry

        lax.fori_loop(0, L // CB, channels, 0)
        here = pl.ds(pl.multiple_of(b * L, L), L)
        parts = [pooled[k * L : (k + 1) * L, here] for k in range(9)]
        new = node_one(parts, mats, outs, cs)
        kind = jnp.maximum(own[3:4], 0.0).astype(jnp.int32)
        hot = one_hot_columns(elements, kind)
        new[0] = new[0] + dot_rows(emb_stack, jnp.concatenate([hot, hot], axis=0))
        for k in range(9):
            rounded[k * L : (k + 1) * L, here] = new[k].astype(bf16)
        return carry

    lax.fori_loop(0, atoms // L, block, 0)
    border_feats[...] = dot(rounded[...], one_hot_columns(atoms, border[...])).astype(bf16)


def arrivals_kernel(
    grid, positions, kinds, keys, listed, counts, border, neighbours,
    nodes, idx, border_col, packet, arrived, sends, recvs,
):
    own_count = positions.shape[1]
    slot_count = listed.shape[1] // 4
    greet(grid)
    own = jnp.concatenate(
        [positions[...], kinds[...].astype(f32), jnp.zeros((4, own_count), f32)], axis=0
    )
    lane = lax.broadcasted_iota(jnp.int32, (8, L), 1)
    row = lax.broadcasted_iota(jnp.int32, (8, L), 0)
    used = jnp.zeros((8, L), jnp.int32)
    for d in range(4):
        used = jnp.where(lane // slot_count == d, counts[:, d : d + 1], used)
    leaving = exact_pick(own, one_hot_columns(own_count, listed[...]))
    leaving = jnp.where((row == 3) & (lane % slot_count >= used), -1.0, leaving)
    packet[:, 0:L] = exact_pick(own, one_hot_columns(own_count, border[...]))
    packet[:, L : 2 * L] = leaving
    copies = send_around(grid, -1, lambda q: packet, arrived, sends, recvs)
    own_row = lax.broadcasted_iota(jnp.int32, (8, own_count), 0)
    staying = jnp.where(keys[...] == 0, 1.0, 0.0)
    nodes[:, 0:own_count] = jnp.where(own_row == 4, staying, own)
    border_col[...] = column_of(border[...].astype(f32)).astype(jnp.int32)
    atoms, slots = neighbours.shape
    for b in range(atoms // L):
        block = neighbours[b * L : (b + 1) * L, :]
        block = jnp.where(block >= atoms + 5 * L, block - L, block).astype(f32)
        for s in range(slots):
            at = (b * slots + s) * L
            idx[:, at : at + L] = row_of(block[:, s : s + 1]).astype(jnp.int32)
    for copy in copies:
        copy.wait()
    incoming = jnp.zeros((8, L), f32)
    for d, (da, db) in enumerate([(-1, 0), (1, 0), (0, -1), (0, 1)]):
        shift = jnp.where(row == 0, float(da), 0.0) + jnp.where(row == 1, float(db), 0.0)
        piece = arrived[AROUND.index((da, db)), :, L : 2 * L] + shift
        incoming = jnp.where(lane // slot_count == d, piece, incoming)
    there = jnp.where(incoming[3:4] >= 0.0, 1.0, 0.0)
    nodes[:, own_count : own_count + L] = jnp.where(row == 4, there, incoming)
    first = own_count + L
    for q, (da, db) in enumerate(AROUND):
        shift = jnp.where(row == 0, float(da), 0.0) + jnp.where(row == 1, float(db), 0.0)
        shift = shift + jnp.where(row == 4, 1.0, 0.0)
        nodes[:, first + q * L : first + (q + 1) * L] = arrived[q, :, 0:L] + shift
    nodes[:, first + 8 * L : first + 9 * L] = jnp.zeros((8, L), f32)


def features_kernel(
    grid, feats, offs, idx, w_in, w_mid,
    h_out, pre1_out, pre2_out, y_out, ghosts, idx_col, sends, recvs,
):
    greet(grid)
    copies = send_around(grid, -1, lambda q: feats, ghosts, sends, recvs)
    edges = offs.shape[1] // 3

    def block(b, carry):
        at = pl.ds(pl.multiple_of(b * edges, L), edges)
        basis, ys = geometry(offs[0:1, at], offs[1:2, at], offs[2:3, at])
        y_out[:, at] = jnp.concatenate(ys, axis=0)
        pre1, pre2 = radial_forward(w_in[1], w_mid[1], basis)
        pre1_out[:, at] = pre1
        pre2_out[:, at] = pre2
        h_out[:, at] = split_stack(silu(pre2))
        return carry

    lax.fori_loop(0, 3, block, 0)

    def turn(t, carry):
        at = pl.ds(pl.multiple_of(t * L, L), L)
        idx_col[at, :] = column_of(idx[:, at].astype(f32)).astype(jnp.int32)
        return carry

    lax.fori_loop(0, offs.shape[1] // L, turn, 0)
    for copy in copies:
        copy.wait()


def features_back_kernel(
    grid, dghosts, dw, dy, pre1, pre2, offs, w_in, w_mid, w_out, doffs, back, sends, recvs
):
    greet(grid)
    copies = send_around(grid, 1, lambda q: dghosts.at[q], back, sends, recvs)
    blocks, _, edges = dw.shape

    def block(b, carry):
        at = pl.ds(pl.multiple_of(b * edges, L), edges)
        dbasis = radial_backward(
            w_out[...], w_mid[1], w_in[1], dw[b], pre1[:, at], pre2[:, at]
        )
        dys = tuple(
            jnp.sum(dy[k * 8 : (k + 1) * 8, at], axis=0, keepdims=True) for k in range(8)
        )
        _, pull = jax.vjp(geometry, offs[0:1, at], offs[1:2, at], offs[2:3, at])
        dx, dyy, dz = pull((dbasis, dys))
        doffs[:, at] = jnp.concatenate([dx, dyy, dz, jnp.zeros((5, edges), f32)], axis=0)
        return carry

    lax.fori_loop(0, blocks, block, 0)
    for copy in copies:
        copy.wait()


def forces_kernel(grid, dpos, border_col, forces, back, sends, recvs):
    atoms = forces.shape[1]
    greet(grid)
    copies = send_around(
        grid, 1, lambda q: dpos.at[:, atoms + q * L : atoms + (q + 1) * L], back, sends, recvs
    )
    hot = one_hot_rows(border_col[...], 0, atoms)
    for copy in copies:
        copy.wait()
    total = back[0]
    for q in range(1, 8):
        total = total + back[q]
    forces[...] = -(dpos[:, 0:atoms] + exact_pick(total, hot))[0:3]


def layer_two_kernel(
    rounded, ghosts, idx, idx_col, h_in, y_in, nodes,
    w_out, mix, out_mix, coefs, lin_in, hid_in, read_in,
    energy, dlocal, dghosts, dy_out, dw_out,
    table, dtable, dres, src, w_s, dw_s, pooled, dpooled, dw_sem,
):
    atoms = energy.shape[1]
    total = table.shape[1]
    slots = idx.shape[1] // atoms
    edges = slots * L
    occ = nodes[4:5, 0:atoms]
    out_stack = rows_stack(w_out[...])
    mats = [both_ways(mix[1, k]) for k in range(3)]
    out = both_ways(out_mix[...])
    hid = (rows_stack(hid_in[...]), hid_in[...])
    cs = [column_of(coefs[k : k + 1, :]) for k in range(3)]
    lin = column_of(lin_in[...])
    read = column_of(read_in[...])
    dtable[...] = jnp.zeros_like(dtable)
    table[:, 0:atoms] = rounded[...]
    for q in range(8):
        table[:, atoms + q * L : atoms + (q + 1) * L] = ghosts[q]
    table[:, atoms + 8 * L :] = jnp.zeros((table.shape[0], total - atoms - 8 * L), bf16)

    def block(b, carry):
        def gather(c, carry):
            at = pl.ds(pl.multiple_of(b * edges + c * G, G), G)
            to = pl.ds(pl.multiple_of(c * G, G), G)
            src[:, to] = dot(table[...], one_hot_columns(total, idx[:, at])).astype(bf16)
            w_s[:, to] = dot_rows(out_stack, h_in[:, at])
            return carry

        lax.fori_loop(0, edges // G, gather, 0)

        def load(row, s):
            at = slice(s * L, (s + 1) * L)
            f = [src[pl.ds(row + k * L, CB), at].astype(f32) for k in range(9)]
            w = [w_s[pl.ds(row + p * L, CB), at] for p in range(7)]
            far = pl.ds(pl.multiple_of(b * edges + s * L, L), L)
            y = [y_in[k : k + 1, far] for k in range(8)]
            return f, w, y

        def forward(c, carry):
            row = pl.multiple_of(c * CB, CB)
            acc = [jnp.zeros((CB, L), f32)] * 9
            for s in range(slots):
                f, w, y = load(row, s)
                along1 = f[1] * y[0] + f[2] * y[1] + f[3] * y[2]
                along2 = f[4] * y[3] + f[5] * y[4] + f[6] * y[5] + f[7] * y[6] + f[8] * y[7]
                acc[0] = acc[0] + w[0] * f[0] + w[1] * along1 + w[2] * along2
                s1, s2 = w[3] * f[0], w[5] * f[0]
                for k in range(3):
                    acc[1 + k] = acc[1 + k] + s1 * y[k] + w[4] * f[1 + k]
                for k in range(3, 8):
                    acc[1 + k] = acc[1 + k] + s2 * y[k] + w[6] * f[1 + k]
            for k in range(9):
                pooled[pl.ds(row + k * L, CB), :] = acc[k] / slots
            return carry

        lax.fori_loop(0, L // CB, forward, 0)
        here = pl.ds(pl.multiple_of(b * L, L), L)
        occupied = nodes[4:5, here]

        def node(parts, residual):
            return node_two(parts, residual, mats, out, cs, hid, read)

        residual = table[0:L, here].astype(f32)
        value, pull = jax.vjp(
            node, [pooled[k * L : (k + 1) * L, :] for k in range(9)], residual
        )
        linear = jnp.sum(lin * residual, axis=0, keepdims=True)
        energy[:, here] = (value + linear) * occupied
        dparts, dresidual = pull(occupied)
        for k in range(9):
            dpooled[k * L : (k + 1) * L, :] = dparts[k] / slots
        mine = pl.ds(pl.multiple_of(b * edges, L), edges)
        dy_out[:, mine] = jnp.zeros((64, edges), f32)

        def backward(c, carry):
            row = pl.multiple_of(c * CB, CB)
            g = [dpooled[pl.ds(row + k * L, CB), :] for k in range(9)]
            for s in range(slots):
                at = slice(s * L, (s + 1) * L)
                far = pl.ds(pl.multiple_of(b * edges + s * L, L), L)
                f, w, y = load(row, s)
                dw = [None] * 7
                dw[0] = g[0] * f[0]
                dw[1] = g[0] * (f[1] * y[0] + f[2] * y[1] + f[3] * y[2])
                dw[2] = g[0] * (
                    f[4] * y[3] + f[5] * y[4] + f[6] * y[5] + f[7] * y[6] + f[8] * y[7]
                )
                g1 = g[1] * y[0] + g[2] * y[1] + g[3] * y[2]
                g2 = g[4] * y[3] + g[5] * y[4] + g[6] * y[5] + g[7] * y[6] + g[8] * y[7]
                dw[3] = f[0] * g1
                dw[4] = g[1] * f[1] + g[2] * f[2] + g[3] * f[3]
                dw[5] = f[0] * g2
                dw[6] = g[4] * f[4] + g[5] * f[5] + g[6] * f[6] + g[7] * f[7] + g[8] * f[8]
                for p in range(7):
                    dw_s[pl.ds(row + p * L, CB), at] = dw[p].astype(bf16)
                v0, q0 = w[1] * g[0], w[2] * g[0]
                sv, sq = w[3] * f[0], w[5] * f[0]
                df = w[0] * g[0] + w[3] * g1 + w[5] * g2
                src[pl.ds(row, CB), at] = df.astype(bf16)
                for k in range(8):
                    base = v0 if k < 3 else q0
                    side = sv if k < 3 else sq
                    direct = w[4] if k < 3 else w[6]
                    dy = base * f[1 + k] + side * g[1 + k]
                    dy_out[k * 8 : (k + 1) * 8, far] += dy[0:8] + dy[8:16]
                    df = base * y[k] + direct * g[1 + k]
                    src[pl.ds(row + (1 + k) * L, CB), at] = df.astype(bf16)
            return carry

        lax.fori_loop(0, L // CB, backward, 0)

        keep = pltpu.make_async_copy(dw_s, dw_out.at[b], dw_sem)
        keep.start()

        def scatter(t, carry):
            to = pl.ds(pl.multiple_of(t * G, G), G)
            column = idx_col[pl.ds(pl.multiple_of(b * edges, 8), edges), :]
            part = dot(src[...], one_hot_rows(column, t * G, G))

            dtable[:, to] += part
            return carry

        lax.fori_loop(0, total // G, scatter, 0)
        keep.wait()
        dres[:, here] = dresidual
        return carry

    lax.fori_loop(0, atoms // L, block, 0)
    dlocal[...] = dtable[:, 0:atoms]
    dlocal[0:L, :] += dres[...] + lin * occ
    for q in range(8):
        dghosts[q] = dtable[:, atoms + q * L : atoms + (q + 1) * L].astype(bf16)


def layer_one_back_kernel(
    dlocal, back_in, border_col, idx_col, offs, doffs_two, f_in, w_in_edges, pre1_in, pre2_in, pooled,
    w_in, w_mid, w_out, mix, out_mix, coefs,
    dpos, dw_s, y_s, dy_s, dh_s, dpooled, d_s,
):
    atoms = dlocal.shape[1]
    total = dpos.shape[1]
    slots = offs.shape[1] // atoms
    edges = slots * L
    mats = [both_ways(mix[0, k]) for k in range(3)]
    outs = [both_ways(out_mix[k]) for k in range(3)]
    cs = [column_of(coefs[k : k + 1, :]) for k in range(5)]
    hot = one_hot_rows(border_col[...], 0, atoms)
    back = back_in[0].astype(f32)
    for q in range(1, 8):
        back = back + back_in[q].astype(f32)
    back_hi, back_lo = hi_lo(back)
    dh_s[...] = dlocal[...] + dot(back_hi, hot) + dot(back_lo, hot)
    dpos[...] = jnp.zeros_like(dpos)

    def block(b, carry):
        here = pl.ds(pl.multiple_of(b * L, L), L)
        _, pull = jax.vjp(
            lambda parts: node_one(parts, mats, outs, cs),
            [pooled[k * L : (k + 1) * L, here] for k in range(9)],
        )
        (dparts,) = pull([dh_s[k * L : (k + 1) * L, here] for k in range(9)])
        for k in range(9):
            dpooled[k * L : (k + 1) * L, :] = dparts[k] / slots

        mine = pl.ds(pl.multiple_of(b * edges, L), edges)
        _, ys = geometry(offs[0:1, mine], offs[1:2, mine], offs[2:3, mine])
        y_s[...] = jnp.concatenate(ys, axis=0)
        dy_s[...] = jnp.zeros_like(dy_s)

        def backward(c, carry):
            row = pl.multiple_of(c * CB, CB)
            g = [dpooled[pl.ds(row + k * L, CB), :] for k in range(9)]
            for s in range(slots):
                at = slice(s * L, (s + 1) * L)
                far = pl.ds(pl.multiple_of(b * edges + s * L, L), L)
                f = f_in[pl.ds(row, CB), far]
                y = [y_s[k : k + 1, at] for k in range(8)]
                dw_s[pl.ds(row, CB), at] = (g[0] * f).astype(bf16)
                g1 = g[1] * y[0] + g[2] * y[1] + g[3] * y[2]
                g2 = g[4] * y[3] + g[5] * y[4] + g[6] * y[5] + g[7] * y[6] + g[8] * y[7]
                dw_s[pl.ds(row + L, CB), at] = (f * g1).astype(bf16)
                dw_s[pl.ds(row + 2 * L, CB), at] = (f * g2).astype(bf16)
                w1 = w_in_edges[pl.ds(row + L, CB), far] * f
                w2 = w_in_edges[pl.ds(row + 2 * L, CB), far] * f
                for k in range(8):
                    dy = (w1 if k < 3 else w2) * g[1 + k]
                    dy_s[k * 8 : (k + 1) * 8, at] += dy[0:8] + dy[8:16]
            return carry

        lax.fori_loop(0, L // CB, backward, 0)

        dbasis = radial_backward(
            w_out[...], w_mid[0], w_in[0], dw_s[...], pre1_in[:, mine], pre2_in[:, mine]
        )
        dys = tuple(
            jnp.sum(dy_s[k * 8 : (k + 1) * 8, :], axis=0, keepdims=True) for k in range(8)
        )
        _, pull_again = jax.vjp(geometry, offs[0:1, mine], offs[1:2, mine], offs[2:3, mine])
        dx, dy, dz = pull_again((dbasis, dys))
        d = jnp.concatenate([dx, dy, dz, jnp.zeros((5, edges), f32)], axis=0) + doffs_two[:, mine]
        hi = d.astype(bf16).astype(f32)
        d_s[...] = jnp.concatenate([hi, d - hi], axis=0).astype(bf16)
        own = d[:, 0:L]
        for s in range(1, slots):
            own = own + d[:, s * L : (s + 1) * L]

        def scatter(t, carry):
            to = pl.ds(pl.multiple_of(t * G, G), G)
            column = idx_col[pl.ds(pl.multiple_of(b * edges, 8), edges), :]
            part = dot(d_s[...], one_hot_rows(column, t * G, G))
            dpos[:, to] += part[0:8] + part[8:16]
            return carry

        lax.fori_loop(0, total // G, scatter, 0)
        dpos[:, here] -= own
        return carry

    lax.fori_loop(0, atoms // L, block, 0)


def call(kernel, outs, scratch, *args, any_outs=(), remote=None):
    specs = [
        pl.BlockSpec(memory_space=pl.ANY if i in any_outs else pltpu.VMEM)
        for i in range(len(outs))
    ]
    semaphores = [pltpu.SemaphoreType.DMA(())] * len(any_outs)
    options = {}
    if remote is not None:
        semaphores = [pltpu.SemaphoreType.DMA((8,))] * 2
        options = dict(collective_id=remote, has_side_effects=True)
    return pl.pallas_call(
        kernel,
        out_shape=[jax.ShapeDtypeStruct(s, d) for s, d in outs],
        out_specs=specs,
        scratch_shapes=[pltpu.VMEM(s, d) for s, d in scratch] + semaphores,
        compiler_params=pltpu.CompilerParams(vmem_limit_bytes=VMEM_LIMIT, **options),
    )(*args)


def on_device(
    positions, species, dest_key, send_list, send_count, border, neighbours, embedding, radial_in,
    radial_mid, radial_out_one, radial_out_two, mix, mix_out_one, mix_out_two, product_one,
    product_two, read_lin, read_hidden, read_out,
):
    grid = (lax.axis_size("gx"), lax.axis_size("gy"))
    listed = send_list[0, 0]
    border_rows = border[0, 0]
    atoms, slots = neighbours.shape[2:]
    count = border_rows.shape[0]
    edge_total = atoms * slots
    total = atoms + 9 * count
    channels = embedding.shape[1]
    feats = 9 * channels

    edges = slots * L
    nodes, idx, border_col = call(
        functools.partial(arrivals_kernel, grid),
        [((8, total), f32), ((1, edge_total), jnp.int32), ((count, 1), jnp.int32)],
        [((8, 2 * L), f32), ((8, 8, 2 * L), f32)],
        positions[0, 0], species[0], dest_key[0], listed.reshape(1, -1), send_count[0],
        border_rows[None], neighbours[0, 0], remote=0,
    )
    hidden = radial_in.shape[2]
    rounded, border_feats, idx, offs, f_e, w_e, pre1, pre2, pooled = call(
        layer_one_kernel,
        [
            ((feats, atoms), bf16), ((feats, count), bf16), ((1, edge_total), jnp.int32),
            ((8, edge_total), f32), ((channels, edge_total), f32), ((3 * channels, edge_total), f32),
            ((hidden, edge_total), f32), ((hidden, edge_total), f32), ((feats, atoms), f32),
        ],
        [((8, edges), f32), ((-(-embedding.shape[0] // 16) * 16, channels), f32)],
        nodes, idx, embedding, radial_in, radial_mid, radial_out_one, mix, mix_out_one,
        product_one, border_rows[None],
    )
    h_two, pre1_two, pre2_two, y_two, ghosts, idx_col = call(
        functools.partial(features_kernel, grid),
        [
            ((3 * hidden, edge_total), bf16), ((hidden, edge_total), f32),
            ((hidden, edge_total), f32), ((8, edge_total), f32), ((8, feats, count), bf16),
            ((edge_total, 1), jnp.int32),
        ],
        [],
        border_feats, offs, idx, radial_in, radial_mid, remote=1,
    )
    energy, dlocal, dghosts, dy_two, dw_two = call(
        layer_two_kernel,
        [
            ((1, atoms), f32), ((feats, atoms), f32), ((8, feats, count), bf16),
            ((64, edge_total), f32), ((atoms // L, 7 * channels, edges), bf16),
        ],
        [
            ((feats, total), bf16), ((feats, total), f32), ((channels, atoms), f32),
            ((feats, edges), bf16), ((7 * channels, edges), f32),
            ((7 * channels, edges), bf16), ((feats, L), f32), ((feats, L), f32),
        ],
        rounded, ghosts, idx, idx_col, h_two, y_two, nodes, radial_out_two, mix, mix_out_two,
        product_two, read_lin[None], read_hidden, read_out[None], any_outs=(4,),
    )
    doffs, back = call(
        functools.partial(features_back_kernel, grid),
        [((8, edge_total), f32), ((8, feats, count), bf16)], [],
        dghosts, dw_two, dy_two, pre1_two, pre2_two, offs, radial_in, radial_mid,
        radial_out_two, remote=2,
    )
    (dpos,) = call(
        layer_one_back_kernel,
        [((8, total), f32)],
        [
            ((3 * channels, edges), bf16), ((8, edges), f32), ((64, edges), f32),
            ((feats, atoms), f32), ((feats, L), f32), ((16, edges), bf16),
        ],
        dlocal, back, border_col, idx_col, offs, doffs, f_e, w_e, pre1, pre2, pooled,
        radial_in, radial_mid, radial_out_one, mix, mix_out_one, product_one,
    )
    (forces,) = call(
        functools.partial(forces_kernel, grid),
        [((3, atoms), f32)], [((8, 8, L), f32)], dpos, border_col, remote=3,
    )
    return (energy[None], forces[None, None])


def solution(mesh):
    whole = P()
    in_specs = (
        P("gx", "gy", None, None),
        P("gx", "gy", None),
        P("gx", "gy", None),
        P("gx", "gy", None, None),
        P("gx", "gy", None),
        P("gx", "gy", None),
        P("gx", "gy", None, None),
    ) + (whole,) * 13
    out_specs = (P("gx", "gy", None), P("gx", "gy", None, None))
    return jax.shard_map(
        on_device, mesh=mesh, in_specs=in_specs, out_specs=out_specs, check_vma=False
    )
```

time: 228 us -> 242 us (1.061)
  Pallas kernels: 132 us -> 234 us
  waiting for transfers between devices: 30.5 us -> 0 us
  starting transfers between devices: 27.3 us -> 0 us
  other arithmetic: 18.1 us -> 0 us
  local copies, waits for them, and re-layouts: 18 us -> 6.79 us
    pallas_call x5 -> x7, Pallas kernels: 132 us -> 234 us  [call(): pl.pallas_call(kernel, out_shape=[jax.ShapeDtypeStruct(s, d) for s, d in...]
    ppermute x20 -> x0, waiting for transfers between devices: 30.5 us -> none  [from_behind(): return lax.ppermute(block, axis, route)]
    ppermute x20 -> x0, starting transfers between devices: 27.3 us -> none  [from_behind(): return lax.ppermute(block, axis, route)]
    concatenate x32 -> x0, other arithmetic: 13.9 us -> none  [the longest x19 10.3 us: k_stack(): return jnp.concatenate([hi, lo, hi], axis=-1)]
    concatenate x8 -> x0, local copies, waits for them, and re-layouts: 3.93 us -> none  [the longest x5 3.68 us: k_stack(): return jnp.concatenate([hi, lo, hi], axis=-1)]
    reshape x2 -> x0, local copies, waits for them, and re-layouts: 2.73 us -> none  [the longest x1 2.11 us: on_device(): idx_col = idx.reshape(edge_total, 1)]
    unnamed x69 -> x4, local copies, waits for them, and re-layouts: 4.78 us -> 5.52 us
  transfers between devices with their start and end apart: 20 -> 0, of which waited for: 9 -> 0; matrix products, arithmetic and copies ran while one was open for 12% -> 0% of each run, Pallas kernels for 6% -> 0%
where the time goes in v3:
time: 242 us; the launch traced here: 241 us
  Pallas kernels  234 us (97%)
  local copies, waits for them, and re-layouts  6.79 us (3%)
    pallas_call x7, Pallas kernels, call(): pl.pallas_call(kernel, out_shape=[jax.ShapeDtypeStruct(s, d) for s, d in...  234 us
    unnamed x4, local copies, waits for them, and re-layouts  5.52 us

profile of v3, /device:TPU:0, one launch (start us, length us, event | category | flops | bytes accessed | tf_op | source)
XLA Modules:
  0.0 241.3 jit_solution(17214066913297117826)
XLA Ops:
  0.6 1.3 reshape_squeeze.3.listed
  1.9 1.3 copy.27
  3.2 1.4 copy.23.hid_in
  4.6 1.5 copy.22
  6.1 11.0 %shard_map.203 = (f32[8,1536]{1,0:T(8,128)}, s32[1,4608]{1,0:T(1,128)}, s32[128,1]{1,0:T(8,128)}) custom-call(f32[3,256]{1,0:T(4,128)} %bitcast.14, s32[1,256]{1,0:T(1,128)} %bitcast.17, s32[1,256]{1,0:T(1,128)} %bitcast.18, s32[1,128]{1,0:T(1,128)} %reshape_squeeze.3.listed, s32[1,4]{1,0:T(1,128)} %bitcast.19, s32[1,128]{1,0:T(1,128)} %bitcast.15, ...), custom_call_target="tpu_custom_call" | custom-call | tf_op jit(solution)/shard_map/pallas_call | solution.py:663
  17.1 21.1 %shard_map.204 = (bf16[1152,384]{1,0:T(8,128)(2,1)}, bf16[1152,128]{1,0:T(8,128)(2,1)}, s32[1,4608]{1,0:T(1,128)}, f32[8,4608]{1,0:T(8,128)}, f32[128,4608]{1,0:...) custom-call(f32[8,1536]{1,0:T(8,128)} %get-tuple-element.27.nodes, ...), custom_call_target="tpu_custom_call" | custom-call | tf_op jit(solution)/shard_map/pallas_call | solution.py:663
  38.2 46.4 %shard_map.205 = (bf16[192,4608]{1,0:T(8,128)(2,1)}, f32[64,4608]{1,0:T(8,128)}, f32[64,4608]{1,0:T(8,128)}, f32[8,4608]{1,0:T(8,128)}, bf16[8,1152,128]{2,1,0:T(8,128)(2,1)}, /*index=5*/s32[4608,1]{1,0:T(8,128)}) custom-call(bf16[1152,128]{1,0:T(8,128)(2,1)} %get-tuple-element.30.feats, f32[8,4608]{1,0:T(8,128)} %get-tuple-element.31.offs, ...), custom_call_target="tpu_custom_call" | custom-call | tf_op jit(solution)/shard_map/pallas_call | solution.py:663
  84.6 72.3 %shard_map.206 = (f32[1,384]{1,0:T(1,128)}, f32[1152,384]{1,0:T(8,128)}, bf16[8,1152,128]{2,1,0:T(8,128)(2,1)}, f32[64,4608]{1,0:T(8,128)}, bf16[3,896,1536]{2,1,0:T(8,128)(2,1)}) custom-call(bf16[1152,384]{1,0:T(8,128)(2,1)} %get-tuple-element.29.rounded, bf16[8,1152,128]{2,1,0:T(8,128)(2,1)} %get-tuple-element.33.ghosts, s32[1,4608]{1,0:T(1,128)} %get-tuple-element.32.idx, ...), custom_call_target="tpu_custom_call" | custom-call | tf_op jit(solution)/shard_map/pallas_call | solution.py:663
  156.9 48.6 %shard_map.207 = (f32[8,4608]{1,0:T(8,128)}, bf16[8,1152,128]{2,1,0:T(8,128)(2,1)}) custom-call(bf16[8,1152,128]{2,1,0:T(8,128)(2,1)} %get-tuple-element.39.dghosts, bf16[3,896,1536]{2,1,0:T(8,128)(2,1)} %get-tuple-element.40.dw, f32[64,4608]{1,0:T(8,128)} %get-tuple-element.41.dy, f32[64,4608]{1,0:T(8,128)} %get-tuple-element.42.pre1, ...), custom_call_target="tpu_custom_call" | custom-call | tf_op jit(solution)/shard_map/pallas_call | solution.py:663
  205.5 26.1 %shard_map.208.dpos = f32[8,1536]{1,0:T(8,128)} custom-call(f32[1152,384]{1,0:T(8,128)} %get-tuple-element.38.dlocal, bf16[8,1152,128]{2,1,0:T(8,128)(2,1)} %get-tuple-element.44.back_in, s32[128,1]{1,0:T(8,128)} %get-tuple-element.45.border_col, s32[4608,1]{1,0:T(8,128)} %get-tuple-element.34.idx_col, f32[8,4608]{1,0:T(8,128)} %get-tuple-element.31.offs, ...), custom_call_target="tpu_custom_call" | custom-call | tf_op jit(solution)/shard_map/pallas_call | solution.py:663
  231.6 8.5 %shard_map.209 = f32[3,384]{1,0:T(4,128)} custom-call(f32[8,1536]{1,0:T(8,128)} %shard_map.208.dpos, s32[128,1]{1,0:T(8,128)} %get-tuple-element.45.border_col), custom_call_target="tpu_custom_call" | custom-call | tf_op jit(solution)/shard_map/pallas_call | solution.py:663
  240.1 1.3 copy.24

commit v4 on v3

--- a/solution.py
+++ b/solution.py
@@ -19,6 +19,7 @@
 
 MESH = pl.DeviceIdType.MESH
 AROUND = [(a - 1, b - 1) for a in range(3) for b in range(3) if (a, b) != (1, 1)]
+CORNERS = [(-1, -1), (-1, 1), (1, -1), (1, 1)]
 ORDER = sorted(range(8), key=lambda q: -abs(AROUND[q][1]))
 
 
@@ -32,6 +33,35 @@
     for da, db in AROUND:
         pl.semaphore_signal(barrier, inc=1, device_id=cell(grid, da, db), device_id_type=MESH)
     pl.semaphore_wait(barrier, 8)
+
+
+def greet_sides(grid):
+    barrier = pltpu.get_barrier_semaphore()
+    for da, db in ((1, 0), (-1, 0), (0, 1), (0, -1)):
+        pl.semaphore_signal(barrier, inc=1, device_id=cell(grid, da, db), device_id_type=MESH)
+    pl.semaphore_wait(barrier, 4)
+
+
+def at_cell(da, db):
+    return AROUND.index((da, db))
+
+
+def half_of(array, h):
+    rows = array.shape[0] // 2
+    return array.at[pl.ds(h * rows, rows), :]
+
+
+def send_half(grid, place, h, source, target, to, sends, recvs):
+    copy = pltpu.make_async_remote_copy(
+        src_ref=source,
+        dst_ref=target,
+        send_sem=sends.at[place, h],
+        recv_sem=recvs.at[place, h],
+        device_id=cell(grid, *to),
+        device_id_type=MESH,
+    )
+    copy.start()
+    return copy
 
 
 def send_around(grid, sign, source, target, sends, recvs):
@@ -111,13 +141,6 @@
     down = lax.broadcasted_iota(jnp.int32, (size, size), 0)
     along = lax.broadcasted_iota(jnp.int32, (size, size), 1)
     return jnp.sum(jnp.where(down == along, row, 0.0), axis=1, keepdims=True)
-
-
-def row_of(column):
-    size = column.shape[0]
-    down = lax.broadcasted_iota(jnp.int32, (size, size), 0)
-    along = lax.broadcasted_iota(jnp.int32, (size, size), 1)
-    return jnp.sum(jnp.where(down == along, column, 0.0), axis=0, keepdims=True)
 
 
 def silu(x):
@@ -175,12 +198,26 @@
 
 
 def mixed_bwd(w, g):
-    if w[1].shape[1] % L:
-        return None, dot_back(w[1], g)
     return None, dot(w[1], split_stack(g))
 
 
 mixed.defvjp(mixed_fwd, mixed_bwd)
+
+
+@jax.custom_vjp
+def mixed_across(w, x):
+    return dot(w[0], split_stack(x))
+
+
+def mixed_across_fwd(w, x):
+    return mixed_across(w, x), w
+
+
+def mixed_across_bwd(w, g):
+    return None, dot_rows(w[1], split_stack(g))
+
+
+mixed_across.defvjp(mixed_across_fwd, mixed_across_bwd)
 
 
 def both_ways(w):
@@ -216,7 +253,7 @@
 def node_two(parts, residual, mats, out, coefs, hid, read):
     s, v, q = mix_orders(mats, parts)
     scalars = mixed(out, product_scalar(coefs, s, v, q)) + residual
-    hidden = silu(mixed(hid, scalars))
+    hidden = silu(mixed_across(hid, scalars))
     return jnp.sum(read * hidden, axis=0, keepdims=True)
 
 
@@ -312,11 +349,13 @@
     grid, positions, kinds, keys, listed, counts, border, neighbours,
     nodes, idx, border_col, packet, arrived, sends, recvs,
 ):
-    own_count = positions.shape[1]
+    own_count = positions.shape[2]
     slot_count = listed.shape[1] // 4
     greet(grid)
     own = jnp.concatenate(
-        [positions[...], kinds[...].astype(f32), jnp.zeros((4, own_count), f32)], axis=0
+        [positions[0], positions[1], positions[2], kinds[...].astype(f32)]
+        + [jnp.zeros((4, own_count), f32)],
+        axis=0,
     )
     lane = lax.broadcasted_iota(jnp.int32, (8, L), 1)
     row = lax.broadcasted_iota(jnp.int32, (8, L), 0)
@@ -332,13 +371,12 @@
     staying = jnp.where(keys[...] == 0, 1.0, 0.0)
     nodes[:, 0:own_count] = jnp.where(own_row == 4, staying, own)
     border_col[...] = column_of(border[...].astype(f32)).astype(jnp.int32)
-    atoms, slots = neighbours.shape
+    slots, _, atoms = neighbours.shape
     for b in range(atoms // L):
-        block = neighbours[b * L : (b + 1) * L, :]
-        block = jnp.where(block >= atoms + 5 * L, block - L, block).astype(f32)
         for s in range(slots):
             at = (b * slots + s) * L
-            idx[:, at : at + L] = row_of(block[:, s : s + 1]).astype(jnp.int32)
+            listing = neighbours[s, :, b * L : (b + 1) * L]
+            idx[:, at : at + L] = jnp.where(listing >= atoms + 5 * L, listing - L, listing)
     for copy in copies:
         copy.wait()
     incoming = jnp.zeros((8, L), f32)
@@ -360,8 +398,23 @@
     grid, feats, offs, idx, w_in, w_mid,
     h_out, pre1_out, pre2_out, y_out, ghosts, idx_col, sends, recvs,
 ):
-    greet(grid)
-    copies = send_around(grid, -1, lambda q: feats, ghosts, sends, recvs)
+    greet_sides(grid)
+
+    def send(h, da, db, source, to):
+        place = at_cell(da, db)
+        target = half_of(ghosts.at[place], h)
+        return send_half(grid, place, h, source, target, to, sends, recvs)
+
+    def send_across(h):
+        mine = half_of(feats, h)
+        return [send(h, -1, 0, mine, (1, 0)), send(h, 1, 0, mine, (-1, 0))]
+
+    across = [send_across(0)]
+    others = []
+    for h in range(2):
+        mine = half_of(feats, h)
+        others.append(send(h, 0, -1, mine, (0, 1)))
+        others.append(send(h, 0, 1, mine, (0, -1)))
     edges = offs.shape[1] // 3
 
     def block(b, carry):
@@ -375,6 +428,7 @@
         return carry
 
     lax.fori_loop(0, 3, block, 0)
+    across.append(send_across(1))
 
     def turn(t, carry):
         at = pl.ds(pl.multiple_of(t * L, L), L)
@@ -382,21 +436,61 @@
         return carry
 
     lax.fori_loop(0, offs.shape[1] // L, turn, 0)
-    for copy in copies:
+    for h in range(2):
+        for da, copy in zip((-1, 1), across[h]):
+            copy.wait()
+            landed = half_of(ghosts.at[at_cell(da, 0)], h)
+            others.append(send(h, da, -1, landed, (0, 1)))
+            others.append(send(h, da, 1, landed, (0, -1)))
+    for copy in others:
         copy.wait()
 
 
 def features_back_kernel(
-    grid, dghosts, dw, dy, pre1, pre2, offs, w_in, w_mid, w_out, doffs, back, sends, recvs
+    grid, dghosts, dw, dy, pre1, pre2, offs, w_in, w_mid, w_out, doffs, back,
+    dw_s, corner, total, sends, recvs, dw_sem,
 ):
-    greet(grid)
-    copies = send_around(grid, 1, lambda q: dghosts.at[q], back, sends, recvs)
+    greet_sides(grid)
     blocks, _, edges = dw.shape
 
-    def block(b, carry):
-        at = pl.ds(pl.multiple_of(b * edges, L), edges)
+    def send_corners(h):
+        copies = []
+        for i, (da, db) in enumerate(CORNERS):
+            place = at_cell(da, db)
+            copies.append(
+                send_half(
+                    grid, place, h, half_of(dghosts.at[place], h), half_of(corner.at[i], h),
+                    (0, db), sends, recvs,
+                )
+            )
+        return copies
+
+    def send_sums(h):
+        copies = []
+        rows = dghosts.shape[1] // 2
+        at = slice(h * rows, (h + 1) * rows)
+        for i, da in enumerate((-1, 1)):
+            place = at_cell(da, 0)
+            total[i, at, :] = (
+                dghosts[place, at, :].astype(f32)
+                + corner[2 * i, at, :].astype(f32)
+                + corner[2 * i + 1, at, :].astype(f32)
+            ).astype(bf16)
+            copies.append(
+                send_half(
+                    grid, place, h, half_of(total.at[i], h), half_of(back.at[i], h),
+                    (da, 0), sends, recvs,
+                )
+            )
+        return copies
+
+    def block(b):
+        fetch = pltpu.make_async_copy(dw.at[b], dw_s, dw_sem)
+        fetch.start()
+        fetch.wait()
+        at = slice(b * edges, (b + 1) * edges)
         dbasis = radial_backward(
-            w_out[...], w_mid[1], w_in[1], dw[b], pre1[:, at], pre2[:, at]
+            w_out[...], w_mid[1], w_in[1], dw_s[...], pre1[:, at], pre2[:, at]
         )
         dys = tuple(
             jnp.sum(dy[k * 8 : (k + 1) * 8, at], axis=0, keepdims=True) for k in range(8)
@@ -404,10 +498,29 @@
         _, pull = jax.vjp(geometry, offs[0:1, at], offs[1:2, at], offs[2:3, at])
         dx, dyy, dz = pull((dbasis, dys))
         doffs[:, at] = jnp.concatenate([dx, dyy, dz, jnp.zeros((5, edges), f32)], axis=0)
-        return carry
-
-    lax.fori_loop(0, blocks, block, 0)
-    for copy in copies:
+
+    early = send_corners(0)
+    block(0)
+    late = send_corners(1)
+    for b in range(1, blocks - 1):
+        block(b)
+    for copy in early:
+        copy.wait()
+    rest = send_sums(0)
+    for i, db in enumerate((-1, 1)):
+        place = at_cell(0, db)
+        for h in range(2):
+            rest.append(
+                send_half(
+                    grid, place, h, half_of(dghosts.at[place], h), half_of(back.at[2 + i], h),
+                    (0, db), sends, recvs,
+                )
+            )
+    block(blocks - 1)
+    for copy in late:
+        copy.wait()
+    rest += send_sums(1)
+    for copy in rest:
         copy.wait()
 
 
@@ -440,11 +553,10 @@
     out_stack = rows_stack(w_out[...])
     mats = [both_ways(mix[1, k]) for k in range(3)]
     out = both_ways(out_mix[...])
-    hid = (rows_stack(hid_in[...]), hid_in[...])
+    hid = (lanes_stack(hid_in[...]), rows_stack(hid_in[...]))
     cs = [column_of(coefs[k : k + 1, :]) for k in range(3)]
     lin = column_of(lin_in[...])
     read = column_of(read_in[...])
-    dtable[...] = jnp.zeros_like(dtable)
     table[:, 0:atoms] = rounded[...]
     for q in range(8):
         table[:, atoms + q * L : atoms + (q + 1) * L] = ghosts[q]
@@ -453,18 +565,17 @@
     def block(b, carry):
         def gather(c, carry):
             at = pl.ds(pl.multiple_of(b * edges + c * G, G), G)
-            to = pl.ds(pl.multiple_of(c * G, G), G)
-            src[:, to] = dot(table[...], one_hot_columns(total, idx[:, at])).astype(bf16)
-            w_s[:, to] = dot_rows(out_stack, h_in[:, at])
+            src[:, at] = dot(table[...], one_hot_columns(total, idx[:, at])).astype(bf16)
             return carry
 
-        lax.fori_loop(0, edges // G, gather, 0)
+        lax.fori_loop(0, edges // G, gather, 0, unroll=2)
+        w_s[...] = dot_rows(out_stack, h_in[:, pl.ds(pl.multiple_of(b * edges, L), edges)])
 
         def load(row, s):
             at = slice(s * L, (s + 1) * L)
-            f = [src[pl.ds(row + k * L, CB), at].astype(f32) for k in range(9)]
+            far = pl.ds(pl.multiple_of(b * edges + s * L, L), L)
+            f = [src[pl.ds(row + k * L, CB), far].astype(f32) for k in range(9)]
             w = [w_s[pl.ds(row + p * L, CB), at] for p in range(7)]
-            far = pl.ds(pl.multiple_of(b * edges + s * L, L), L)
             y = [y_in[k : k + 1, far] for k in range(8)]
             return f, w, y
 
@@ -524,11 +635,11 @@
                 dw[5] = f[0] * g2
                 dw[6] = g[4] * f[4] + g[5] * f[5] + g[6] * f[6] + g[7] * f[7] + g[8] * f[8]
                 for p in range(7):
-                    dw_s[pl.ds(row + p * L, CB), at] = dw[p].astype(bf16)
+                    dw_s[b, pl.ds(row + p * L, CB), at] = dw[p].astype(bf16)
                 v0, q0 = w[1] * g[0], w[2] * g[0]
                 sv, sq = w[3] * f[0], w[5] * f[0]
                 df = w[0] * g[0] + w[3] * g1 + w[5] * g2
-                src[pl.ds(row, CB), at] = df.astype(bf16)
+                src[pl.ds(row, CB), far] = df.astype(bf16)
                 for k in range(8):
                     base = v0 if k < 3 else q0
                     side = sv if k < 3 else sq
@@ -536,28 +647,25 @@
                     dy = base * f[1 + k] + side * g[1 + k]
                     dy_out[k * 8 : (k + 1) * 8, far] += dy[0:8] + dy[8:16]
                     df = base * y[k] + direct * g[1 + k]
-                    src[pl.ds(row + (1 + k) * L, CB), at] = df.astype(bf16)
+                    src[pl.ds(row + (1 + k) * L, CB), far] = df.astype(bf16)
             return carry
 
         lax.fori_loop(0, L // CB, backward, 0)
 
-        keep = pltpu.make_async_copy(dw_s, dw_out.at[b], dw_sem)
-        keep.start()
-
-        def scatter(t, carry):
-            to = pl.ds(pl.multiple_of(t * G, G), G)
-            column = idx_col[pl.ds(pl.multiple_of(b * edges, 8), edges), :]
-            part = dot(src[...], one_hot_rows(column, t * G, G))
-
-            dtable[:, to] += part
-            return carry
-
-        lax.fori_loop(0, total // G, scatter, 0)
-        keep.wait()
+        pltpu.make_async_copy(dw_s.at[b], dw_out.at[b], dw_sem.at[b]).start()
         dres[:, here] = dresidual
         return carry
 
     lax.fori_loop(0, atoms // L, block, 0)
+
+    def scatter(t, carry):
+        to = pl.ds(pl.multiple_of(t * G, G), G)
+        dtable[:, to] = dot(src[...], one_hot_rows(idx_col[...], t * G, G))
+        return carry
+
+    lax.fori_loop(0, total // G, scatter, 0)
+    for b in range(atoms // L):
+        pltpu.make_async_copy(dw_s.at[b], dw_out.at[b], dw_sem.at[b]).wait()
     dlocal[...] = dtable[:, 0:atoms]
     dlocal[0:L, :] += dres[...] + lin * occ
     for q in range(8):
@@ -578,7 +686,7 @@
     cs = [column_of(coefs[k : k + 1, :]) for k in range(5)]
     hot = one_hot_rows(border_col[...], 0, atoms)
     back = back_in[0].astype(f32)
-    for q in range(1, 8):
+    for q in range(1, 4):
         back = back + back_in[q].astype(f32)
     back_hi, back_lo = hi_lo(back)
     dh_s[...] = dlocal[...] + dot(back_hi, hot) + dot(back_lo, hot)
@@ -650,20 +758,21 @@
     lax.fori_loop(0, atoms // L, block, 0)
 
 
-def call(kernel, outs, scratch, *args, any_outs=(), remote=None):
-    specs = [
-        pl.BlockSpec(memory_space=pl.ANY if i in any_outs else pltpu.VMEM)
-        for i in range(len(outs))
-    ]
-    semaphores = [pltpu.SemaphoreType.DMA(())] * len(any_outs)
+def call(kernel, outs, scratch, *args, any_ins=(), any_outs=(), semaphores=(), remote=None):
+    def places(count, anywhere):
+        return [
+            pl.BlockSpec(memory_space=pl.ANY if i in anywhere else pltpu.VMEM) for i in range(count)
+        ]
+
+    semaphores = [pltpu.SemaphoreType.DMA(shape) for shape in semaphores]
     options = {}
     if remote is not None:
-        semaphores = [pltpu.SemaphoreType.DMA((8,))] * 2
         options = dict(collective_id=remote, has_side_effects=True)
     return pl.pallas_call(
         kernel,
         out_shape=[jax.ShapeDtypeStruct(s, d) for s, d in outs],
-        out_specs=specs,
+        in_specs=places(len(args), any_ins),
+        out_specs=places(len(outs), any_outs),
         scratch_shapes=[pltpu.VMEM(s, d) for s, d in scratch] + semaphores,
         compiler_params=pltpu.CompilerParams(vmem_limit_bytes=VMEM_LIMIT, **options),
     )(*args)
@@ -689,8 +798,8 @@
         functools.partial(arrivals_kernel, grid),
         [((8, total), f32), ((1, edge_total), jnp.int32), ((count, 1), jnp.int32)],
         [((8, 2 * L), f32), ((8, 8, 2 * L), f32)],
-        positions[0, 0], species[0], dest_key[0], listed.reshape(1, -1), send_count[0],
-        border_rows[None], neighbours[0, 0], remote=0,
+        positions[0].transpose(1, 0, 2), species[0], dest_key[0], listed.reshape(1, -1), send_count[0],
+        border_rows[None], neighbours[0].transpose(2, 0, 1), semaphores=((8,), (8,)), remote=0,
     )
     hidden = radial_in.shape[2]
     rounded, border_feats, idx, offs, f_e, w_e, pre1, pre2, pooled = call(
@@ -712,7 +821,8 @@
             ((edge_total, 1), jnp.int32),
         ],
         [],
-        border_feats, offs, idx, radial_in, radial_mid, remote=1,
+        border_feats, offs, idx, radial_in, radial_mid, any_outs=(4,),
+        semaphores=((8, 2), (8, 2)), remote=1,
     )
     energy, dlocal, dghosts, dy_two, dw_two = call(
         layer_two_kernel,
@@ -722,17 +832,19 @@
         ],
         [
             ((feats, total), bf16), ((feats, total), f32), ((channels, atoms), f32),
-            ((feats, edges), bf16), ((7 * channels, edges), f32),
-            ((7 * channels, edges), bf16), ((feats, L), f32), ((feats, L), f32),
+            ((feats, edge_total), bf16), ((7 * channels, edges), f32),
+            ((atoms // L, 7 * channels, edges), bf16), ((feats, L), f32), ((feats, L), f32),
         ],
         rounded, ghosts, idx, idx_col, h_two, y_two, nodes, radial_out_two, mix, mix_out_two,
-        product_two, read_lin[None], read_hidden, read_out[None], any_outs=(4,),
+        product_two, read_lin[None], read_hidden.T, read_out[None], any_outs=(4,),
+        semaphores=((atoms // L,),),
     )
     doffs, back = call(
         functools.partial(features_back_kernel, grid),
-        [((8, edge_total), f32), ((8, feats, count), bf16)], [],
+        [((8, edge_total), f32), ((4, feats, count), bf16)],
+        [((7 * channels, edges), bf16), ((4, feats, count), bf16), ((2, feats, count), bf16)],
         dghosts, dw_two, dy_two, pre1_two, pre2_two, offs, radial_in, radial_mid,
-        radial_out_two, remote=2,
+        radial_out_two, any_ins=(1,), semaphores=((8, 2), (8, 2), ()), remote=2,
     )
     (dpos,) = call(
         layer_one_back_kernel,
@@ -746,7 +858,8 @@
     )
     (forces,) = call(
         functools.partial(forces_kernel, grid),
-        [((3, atoms), f32)], [((8, 8, L), f32)], dpos, border_col, remote=3,
+        [((3, atoms), f32)], [((8, 8, L), f32)], dpos, border_col,
+        semaphores=((8,), (8,)), remote=3,
     )
     return (energy[None], forces[None, None])
 

time: 242 us -> 195 us (0.81)
  Pallas kernels: 234 us -> 191 us
  local copies, waits for them, and re-layouts: 6.79 us -> 2.56 us
    pallas_call x7, Pallas kernels: 234 us -> 191 us  [call(): pl.pallas_call(kernel, out_shape=[jax.ShapeDtypeStruct(s, d) for s, d in...]
    unnamed x4 -> x1, local copies, waits for them, and re-layouts: 5.52 us -> 1.29 us
where the time goes in v4:
time: 195 us; the launch traced here: 194 us
  Pallas kernels  191 us (98%)
  local copies, waits for them, and re-layouts  2.56 us (1%)
    pallas_call x7, Pallas kernels, call(): pl.pallas_call(kernel, out_shape=[jax.ShapeDtypeStruct(s, d) for s, d in...  191 us

profile of v4, /device:TPU:0, one launch (start us, length us, event | category | flops | bytes accessed | tf_op | source)
XLA Modules:
  0.0 194.1 jit_solution(10128167474095509550)
XLA Ops:
  0.6 1.3 reshape_squeeze.3.listed
  1.9 10.7 %shard_map.203 = (f32[8,1536]{1,0:T(8,128)}, s32[1,4608]{1,0:T(1,128)}, s32[128,1]{1,0:T(8,128)}) custom-call(f32[3,1,256]{2,1,0:T(1,128)} %bitcast.16, s32[1,256]{1,0:T(1,128)} %bitcast.19, s32[1,256]{1,0:T(1,128)} %bitcast.20, s32[1,128]{1,0:T(1,128)} %reshape_squeeze.3.listed, s32[1,4]{1,0:T(1,128)} %bitcast.23, s32[1,128]{1,0:T(1,128)} %bitcast.17, ...), custom_call_target="tpu_custom_call" | custom-call | tf_op jit(solution)/shard_map/pallas_call | solution.py:771
  12.7 21.1 %shard_map.204 = (bf16[1152,384]{1,0:T(8,128)(2,1)}, bf16[1152,128]{1,0:T(8,128)(2,1)}, s32[1,4608]{1,0:T(1,128)}, f32[8,4608]{1,0:T(8,128)}, f32[128,4608]{1,0:...) custom-call(f32[8,1536]{1,0:T(8,128)} %get-tuple-element.27.nodes, ...), custom_call_target="tpu_custom_call" | custom-call | tf_op jit(solution)/shard_map/pallas_call | solution.py:771
  33.7 28.3 %shard_map.205 = (bf16[192,4608]{1,0:T(8,128)(2,1)}, f32[64,4608]{1,0:T(8,128)}, f32[64,4608]{1,0:T(8,128)}, f32[8,4608]{1,0:T(8,128)}, bf16[8,1152,128]{2,1,0:T(8,128)(2,1)}, /*index=5*/s32[4608,1]{1,0:T(8,128)}) custom-call(bf16[1152,128]{1,0:T(8,128)(2,1)} %get-tuple-element.30.feats, f32[8,4608]{1,0:T(8,128)} %get-tuple-element.31.offs, ...), custom_call_target="tpu_custom_call" | custom-call | tf_op jit(solution)/shard_map/pallas_call | solution.py:771
  62.1 68.7 %shard_map.206 = (f32[1,384]{1,0:T(1,128)}, f32[1152,384]{1,0:T(8,128)}, bf16[8,1152,128]{2,1,0:T(8,128)(2,1)}, f32[64,4608]{1,0:T(8,128)}, bf16[3,896,1536]{2,1,0:T(8,128)(2,1)}) custom-call(bf16[1152,384]{1,0:T(8,128)(2,1)} %get-tuple-element.29.rounded, bf16[8,1152,128]{2,1,0:T(8,128)(2,1)} %get-tuple-element.33.ghosts, s32[1,4608]{1,0:T(1,128)} %get-tuple-element.32.idx, ...), custom_call_target="tpu_custom_call" | custom-call | tf_op jit(solution)/shard_map/pallas_call | solution.py:771
  130.8 28.1 %shard_map.207 = (f32[8,4608]{1,0:T(8,128)}, bf16[4,1152,128]{2,1,0:T(8,128)(2,1)}) custom-call(bf16[8,1152,128]{2,1,0:T(8,128)(2,1)} %get-tuple-element.39.dghosts, bf16[3,896,1536]{2,1,0:T(8,128)(2,1)} %get-tuple-element.40.dw, f32[64,4608]{1,0:T(8,128)} %get-tuple-element.41.dy, f32[64,4608]{1,0:T(8,128)} %get-tuple-element.42.pre1, ...), custom_call_target="tpu_custom_call" | custom-call | tf_op jit(solution)/shard_map/pallas_call | solution.py:771
  158.9 25.5 %shard_map.208.dpos = f32[8,1536]{1,0:T(8,128)} custom-call(f32[1152,384]{1,0:T(8,128)} %get-tuple-element.38.dlocal, bf16[4,1152,128]{2,1,0:T(8,128)(2,1)} %get-tuple-element.44.back_in, s32[128,1]{1,0:T(8,128)} %get-tuple-element.45.border_col, s32[4608,1]{1,0:T(8,128)} %get-tuple-element.34.idx_col, f32[8,4608]{1,0:T(8,128)} %get-tuple-element.31.offs, ...), custom_call_target="tpu_custom_call" | custom-call | tf_op jit(solution)/shard_map/pallas_call | solution.py:771
  184.3 8.5 %shard_map.209 = f32[3,384]{1,0:T(4,128)} custom-call(f32[8,1536]{1,0:T(8,128)} %shard_map.208.dpos, s32[128,1]{1,0:T(8,128)} %get-tuple-element.45.border_col), custom_call_target="tpu_custom_call" | custom-call | tf_op jit(solution)/shard_map/pallas_call | solution.py:771
  192.8 1.3 copy.22
